TPU v7x, 256 devices: a whole 4x4x8 slice. The times are simulated.
256 devices in a mesh: tile: 64 (over z, y, core), probe: 4 (over x).
Axes of the slice: x: 4, y: 4, z: 8, core: 2. Of those that a mesh axis runs over, the one named last changes fastest.
Arguments:
- probes: float32 [256, 32, 128], P('tile', 'probe'), may hold values from -6 to 6
- viscosity: float32 [256, 16, 128], P('tile'), may hold values from 0.005 to 0.05
- friction: float32 [256, 128], P('tile'), may hold values from 0.5 to 4
- base_velocity: float32 [256, 2, 128], P('tile'), may hold values from -4 to 4
- obs_tile: int32 [32768, 1], P('tile'), may hold values from 0 to 63; in each aligned block of 512 rows (0 to 511, 512 to 1023, ...) at most 16 rows name the same one
- obs_cell: int32 [32768], P('tile'), may hold values from 0 to 511
- sight_lines: float32 [2, 32768], P(None, 'tile'), may hold values from -1 to 1
- obs_precision: float32 [32768, 512], P('tile'), may hold values from -1 to 32, as said below
- basis: float32 [256, 256, 128], P('probe', 'tile'), may hold values from -0.03125 to 0.03125
Outputs:
- filtered: float32 [256, 32, 128], P('tile', 'probe')
- coefficients: float32 [32, 256], P('probe')
Inputs may be any that keep to these rules, and one draw needn't show every extreme that they name: `obs_tile`: within the rows of one owner (aligned blocks of 512 rows) no tile is named by more than 16 rows, and in some block one tile is named by exactly 16 rows. `obs_precision`: each swath's block is symmetric and positive definite.
All inputs are finite; a program needn't handle non-finite values.
Results may differ from a plain program's by a relative error of at most 0.0003.
Values sent between devices are 32-bit elements; how exact they have to be, the bound alone decides.
No kernel may reach another device: no remote copies, remote signals or barrier semaphores. Data moves between devices by JAX's collectives and lax.ppermute only.
A program may use at most 128 MiB of HBM per device.

v0:
```python
import jax
import jax.numpy as jnp
from jax import lax
from jax.sharding import PartitionSpec as P

SWEEPS = 5


aspect_sq = 1024.0
highest = lax.Precision.HIGHEST


def extended_2(value, sides, width):
    for axis, dim in sides:
        count, length = (lax.axis_size(axis), value.shape[dim])
        up = [(i, (i + 1) % count) for i in range(count - 1)]
        down = [(j, i) for i, j in up]
        last = lax.slice_in_dim(value, length - width, length, axis=dim)
        first = lax.slice_in_dim(value, 0, width, axis=dim)
        before = lax.ppermute(last, axis, up)
        after = lax.ppermute(first, axis, down)
        value = jnp.concatenate([before, value, after], axis=dim)
    return value


def operator_parts(stacked, layers):
    viscous = stacked[:, :layers, :]
    y_padded = jnp.pad(viscous, ((0, 0), (0, 0), (1, 1)))
    centre = viscous[1:-1]
    cells_x = centre.shape[0]
    cells_y = centre.shape[2]
    face_east = 0.5 * (centre + viscous[2:])
    face_west = 0.5 * (centre + viscous[:-2])
    face_north = 0.5 * (centre + y_padded[1:-1, :, 2:])
    face_south = 0.5 * (centre + y_padded[1:-1, :, :-2])
    diagonal_terms = []
    for shift_x in (1, -1):
        for shift_y in (1, -1):
            corner = y_padded[
                1 + shift_x : 1 + shift_x + cells_x, :, 1 + shift_y : 1 + shift_y + cells_y
            ]
            diagonal_terms.append(0.375 * shift_x * shift_y * (centre + corner))
    vertical = 0.5 * (centre[:, :-1] + centre[:, 1:])
    empty_row = jnp.zeros_like(centre[:, :1])
    face_up = jnp.concatenate([vertical, empty_row], axis=1)
    face_down = jnp.concatenate([empty_row, vertical], axis=1)
    friction_base = stacked[1:-1, layers]
    basal_term = jnp.concatenate([friction_base[:, None, :], jnp.zeros_like(centre[:, 1:])], axis=1)
    column = aspect_sq * (face_up + face_down) + basal_term
    diag_u = 4.0 * (face_east + face_west) + (face_north + face_south) + column
    diag_v = face_east + face_west + 4.0 * (face_north + face_south) + column
    pivots_main = jnp.stack([diag_u, diag_v], axis=1)
    lower_diag = -aspect_sq * face_down
    upper_diag = -aspect_sq * face_up
    inverses = []
    ratios = []
    for layer_index in range(layers):
        pivot_now = pivots_main[:, :, layer_index]
        if layer_index > 0:
            pivot_now = pivot_now - lower_diag[:, None, layer_index] * ratios[-1]
        inverse = 1.0 / pivot_now
        inverses.append(inverse)
        ratios.append(upper_diag[:, None, layer_index] * inverse)
    horizontal = (face_east[:, None], face_west[:, None], face_north[:, None], face_south[:, None])
    corners = tuple((entry[:, None] for entry in diagonal_terms))
    return (horizontal, corners, lower_diag, inverses, ratios)


def neighbours(extended, stencil_parts):
    horizontal, corners, lower_diag, inverses, ratios = stencil_parts
    face_east, face_west, face_north, face_south = horizontal
    cells_x = extended.shape[0] - 2
    cells_y = extended.shape[4]
    y_padded = jnp.pad(extended, ((0, 0), (0, 0), (0, 0), (0, 0), (1, 1)))

    def shifted(shift_x, shift_y, component):
        return y_padded[
            1 + shift_x : 1 + shift_x + cells_x,
            :,
            component,
            :,
            1 + shift_y : 1 + shift_y + cells_y,
        ]

    along_u = 4.0 * (face_east * shifted(1, 0, 0) + face_west * shifted(-1, 0, 0)) + (
        face_north * shifted(0, 1, 0) + face_south * shifted(0, -1, 0)
    )
    along_v = (
        face_east * shifted(1, 0, 1)
        + face_west * shifted(-1, 0, 1)
        + 4.0 * (face_north * shifted(0, 1, 1) + face_south * shifted(0, -1, 1))
    )
    offsets = ((1, 1), (1, -1), (-1, 1), (-1, -1))
    cross_u = corners[0] * shifted(offsets[0][0], offsets[0][1], 1)
    cross_v = corners[0] * shifted(offsets[0][0], offsets[0][1], 0)
    for which in range(1, 4):
        cross_u = cross_u + corners[which] * shifted(offsets[which][0], offsets[which][1], 1)
        cross_v = cross_v + corners[which] * shifted(offsets[which][0], offsets[which][1], 0)
    return jnp.stack([along_u + cross_u, along_v + cross_v], axis=2)


def column_solve(right_side, load_layer, loading, stencil_parts):
    horizontal, corners, lower_diag, inverses, ratios = stencil_parts
    layers = len(inverses)
    forward = []
    for layer_index in range(layers):
        if right_side is None:
            current = loading if layer_index == load_layer else jnp.zeros_like(loading)
        else:
            current = right_side[:, :, :, layer_index]
            if layer_index == load_layer:
                current = current + loading
        if layer_index > 0:
            current = current - lower_diag[:, None, None, layer_index] * forward[-1]
        forward.append(current * inverses[layer_index][:, None])
    solved = [forward[-1]]
    for layer_index in range(layers - 2, -1, -1):
        solved.insert(0, forward[layer_index] - ratios[layer_index][:, None] * solved[0])
    return jnp.stack(solved, axis=3)


def per_device(
    probes,
    viscosity,
    friction,
    base_velocity,
    obs_tile,
    obs_cell,
    sight_lines,
    obs_precision,
    basis,
):
    tile_count = lax.axis_size("tile")
    cells_x = probes.shape[0]
    probe_count = probes.shape[1]
    cells_y = probes.shape[2]
    layers = viscosity.shape[1]
    stacked = jnp.concatenate([viscosity, friction[:, None, :], base_velocity], axis=1)
    coef_wide = extended_2(stacked, (("tile", 0),), 2)
    parts_near = operator_parts(coef_wide[1:-1], layers)
    basal_gain = -(friction[:, None, None, :] * base_velocity[:, None, :, :])

    def relax(loading, load_layer):
        velocity = column_solve(None, load_layer, loading, parts_near)
        for sweep_index in range(SWEEPS - 1):
            extended = extended_2(velocity, (("tile", 0),), 1)
            velocity = column_solve(
                neighbours(extended, parts_near), load_layer, loading, parts_near
            )
        return velocity

    velocity_state = relax(basal_gain * probes[:, :, None, :], 0)
    surface = velocity_state[:, :, :, layers - 1, :]
    surface_cells = jnp.transpose(surface, (0, 3, 1, 2)).reshape(cells_x * cells_y, probe_count, 2)
    target = obs_tile[:, 0]
    row_count = target.shape[0]
    capacity = 2 * row_count // tile_count
    onehot = (target[:, None] == jnp.arange(tile_count, dtype=jnp.int32)[None, :]).astype(jnp.int32)
    earlier = jnp.cumsum(onehot, axis=0) - onehot
    slot_index = target * capacity + jnp.sum(earlier * onehot, axis=1)
    request = jnp.zeros((tile_count * capacity,), jnp.int32).at[slot_index].set(obs_cell)
    asked = lax.all_to_all(
        request.reshape(tile_count, capacity), "tile", split_axis=0, concat_axis=0, tiled=True
    ).reshape(-1)
    picked = surface_cells[asked]
    sight_rows = jnp.transpose(sight_lines)
    shipped = lax.all_to_all(
        picked.reshape(tile_count, capacity * probe_count * 2),
        "tile",
        split_axis=0,
        concat_axis=0,
        tiled=True,
    )
    arrived = shipped.reshape(tile_count * capacity, probe_count, 2)[slot_index]
    predicted = sight_rows[:, 0:1] * arrived[:, :, 0] + sight_rows[:, 1:2] * arrived[:, :, 1]
    weighted = jnp.dot(obs_precision, predicted, precision=highest)
    row_loads = weighted[:, :, None] * sight_rows[:, None, :]
    outgoing = (
        jnp.zeros((tile_count * capacity, probe_count, 2), jnp.float32)
        .at[slot_index]
        .set(row_loads)
    )
    returned = lax.all_to_all(
        outgoing.reshape(tile_count, capacity * probe_count * 2),
        "tile",
        split_axis=0,
        concat_axis=0,
        tiled=True,
    )
    returned = returned.reshape(tile_count * capacity, probe_count, 2)
    top_sum = jax.ops.segment_sum(returned, asked, num_segments=cells_x * cells_y)
    top_load = jnp.transpose(top_sum.reshape(cells_x, cells_y, probe_count, 2), (0, 2, 3, 1))
    adjoint = relax(top_load, layers - 1)
    hessian = jnp.sum(basal_gain * adjoint[:, :, :, 0, :], axis=2)
    panels = lax.all_gather(basis, "probe", axis=0, tiled=True)
    gram_part = jnp.einsum("bxy,cxy->bc", panels, panels, precision=highest)
    moment_part = jnp.einsum("bxy,xky->bk", panels, hessian, precision=highest)
    gram, moments = lax.psum((gram_part, moment_part), "tile")
    factor = jnp.linalg.cholesky(gram)
    coeffs = jax.scipy.linalg.cho_solve((factor, True), moments)
    filtered = hessian - jnp.einsum("bxy,bk->xky", panels, coeffs, precision=highest)
    return (filtered, jnp.transpose(coeffs))


def solution(mesh):
    in_specs = (
        P("tile", "probe", None),
        P("tile", None, None),
        P("tile", None),
        P("tile", None, None),
        P("tile", None),
        P("tile"),
        P(None, "tile"),
        P("tile", None),
        P("probe", "tile", None),
    )
    out_specs = (P("tile", "probe", None), P("probe", None))
    return jax.shard_map(
        per_device, mesh=mesh, in_specs=in_specs, out_specs=out_specs, check_vma=False
    )
```

profile of v0, /device:TPU:128, one launch (start us, length us, event | category | flops | bytes accessed | tf_op | source)
XLA Modules:
  0.0 621.0 jit_solution(13382703658135517389)
XLA Ops:
  8.1 3.9 collective-permute-start
  12.0 1.9 collective-permute-start.1
  17.7 2.6 scatter_custom_fusion
  20.9 11.6 %all-to-all-start = ((s32[64,1,16]{2,1,0:T(1,128)}), s32[64,1,16]{2,1,0:T(1,128)S(1)}, u32[]{:S(2)}, u32[]{:S(2)}) async-start(s32[64,1,16]{2,1,0:T(1,128)} %bitcast.52), calls=%async_computation | async-start | bytes 65536 | tf_op jit(solution)/shard_map/all_to_all | solution.py:162
  33.5 13.1 %all_gather.3 = f32[256,4,128]{2,0,1:T(8,128)S(1)} all-gather(f32[64,4,128]{2,0,1:T(8,128)S(1)} %copy.926), channel_id=1, replica_groups=mesh['tile'=64,'probe'=4] {'probe'}, dimensions={0}, use_global_device_ids=true | all-gather | bytes 655360 | tf_op jit(solution)/shard_map/all_gather | solution.py:195
  55.5 2.4 collective-permute-start.2
  57.9 1.9 collective-permute-start.3
  60.4 7.1 %collective-permute-done.3 = f32[1,8,2,16,128]{4,3,2,1,0:T(8,128)S(1)} collective-permute-done((f32[1,8,2,16,128]{4,3,2,1,0:T(8,128)S(1)}, f32[1,8,2,16,128]{4,3,2,1,0:T(8,128)S(1)}, u32[]{:S(2)}, u32[]{:S(2)}) %collective-permute-start.3) | collective-permute-done | bytes 131104 | tf_op jit(solution)/shard_map/ppermute | solution.py:20
  70.8 1.9 collective-permute-start.4
  72.8 2.6 collective-permute-start.5
  76.0 6.5 %collective-permute-done.5 = f32[1,8,2,16,128]{4,3,2,1,0:T(8,128)S(1)} collective-permute-done((f32[1,8,2,16,128]{4,3,2,1,0:T(8,128)S(1)}, f32[1,8,2,16,128]{4,3,2,1,0:T(8,128)S(1)}, u32[]{:S(2)}, u32[]{:S(2)}) %collective-permute-start.5) | collective-permute-done | bytes 131104 | tf_op jit(solution)/shard_map/ppermute | solution.py:20
  85.8 1.9 collective-permute-start.6
  87.7 2.4 collective-permute-start.7
  90.2 7.2 %collective-permute-done.7 = f32[1,8,2,16,128]{4,3,2,1,0:T(8,128)S(1)} collective-permute-done((f32[1,8,2,16,128]{4,3,2,1,0:T(8,128)S(1)}, f32[1,8,2,16,128]{4,3,2,1,0:T(8,128)S(1)}, u32[]{:S(2)}, u32[]{:S(2)}) %collective-permute-start.7) | collective-permute-done | bytes 131104 | tf_op jit(solution)/shard_map/ppermute | solution.py:20
  102.6 2.4 collective-permute-start.9
  105.7 115.0 %all-reduce.15.cloned.1.call-done = f32[256,256]{0,1:T(8,128)} async-done(((f32[256,256]{0,1:T(8,128)}), f32[256,256]{0,1:T(8,128)}) %all-reduce.15.cloned.1.call-update) | async-done | bytes 262160 | tf_op jit(solution)/shard_map/psum | solution.py:198
  224.6 4.0 gather_fusion
  228.6 8.0 %copy.787 = f32[1024,8,2]{2,1,0:T(8,128)} copy(f32[1024,8,2]{1,2,0:T(2,128)S(1)} %gather_fusion) | data formatting | bytes 131072 | tf_op jit(solution)/shard_map/gather | solution.py:165
  236.7 5.2 all_to_all.24
  241.9 10.8 %all-to-all-start.1 = ((f32[64,1,256]{2,1,0:T(1,128)}), f32[64,1,256]{2,1,0:T(1,128)S(1)}, u32[]{:S(2)}, u32[]{:S(2)}) async-start(f32[64,1,256]{2,1,0:T(1,128)} %all_to_all.24), calls=%async_computation.1 | async-start | bytes 131072 | tf_op jit(solution)/shard_map/all_to_all | solution.py:167
  252.7 11.7 %cholesky.50 = f32[128,128]{1,0:T(8,128)S(1)} custom-call(f32[128,128]{1,0:T(8,128)S(1)} %cholesky.118), custom_call_target="Cholesky" | custom-call | tf_op jit(solution)/shard_map/jit(cholesky)/cholesky | solution.py:199
  265.1 10.4 %custom-call.18 = f32[1,128,128]{1,2,0:T(8,128)} custom-call(f32[1,128,128]{2,1,0:T(8,128)S(1)} %get-tuple-element.382), custom_call_target="InvertDiagBlocksLowerTriangular" | custom-call | tf_op jit(solution)/shard_map/jit(cholesky)/cholesky | solution.py:199
  276.4 5.6 reshape.1215
  282.0 8.3 %copy.789 = f32[1024,8,2]{1,2,0:T(2,128)S(1)} copy(f32[1024,8,2]{2,1,0:T(8,128)} %reshape.1215) | data formatting | bytes 131072 | tf_op jit(solution)/shard_map/reshape | solution.py:174
  290.3 2.2 gather_fusion.1
  296.0 13.6 %scatter_fusion = f32[1024,8,2]{1,2,0:T(2,128)S(1)} fusion(f32[1024,8,2]{1,2,0:T(2,128)S(1)} %broadcast_in_dim.9, s32[512]{0:T(512)S(1)} %bitcast.1046, f32[512,8,2]{1,2,0:T(2,128)S(1)} %broadcast_multiply_fusion), kind=kCustom, calls=%fused_computation.3 | custom fusion | bytes 100352 | tf_op jit(solution)/shard_map/scatter | solution.py:181
  309.6 8.0 %copy.793 = f32[1024,8,2]{2,1,0:T(8,128)} copy(f32[1024,8,2]{1,2,0:T(2,128)S(1)} %scatter_fusion) | data formatting | bytes 131072 | tf_op jit(solution)/shard_map/scatter | solution.py:181
  317.6 5.5 all_to_all.25
  323.1 10.3 %all-to-all-start.2 = ((f32[64,1,256]{2,1,0:T(1,128)}), f32[64,1,256]{2,1,0:T(1,128)S(1)}, u32[]{:S(2)}, u32[]{:S(2)}) async-start(f32[64,1,256]{2,1,0:T(1,128)} %all_to_all.25), calls=%async_computation.2 | async-start | bytes 131072 | tf_op jit(solution)/shard_map/all_to_all | solution.py:183
  333.7 4.9 all-to-all-done.2
  338.8 5.6 reshape.1273
  344.3 8.3 %copy.795 = f32[1024,8,2]{1,2,0:T(2,128)S(1)} copy(f32[1024,8,2]{2,1,0:T(8,128)} %reshape.1273) | data formatting | bytes 131072 | tf_op jit(solution)/shard_map/reshape | solution.py:190
  352.9 33.0 %scatter_fusion.1 = f32[512,8,2]{1,2,0:T(2,128)S(1)} fusion(f32[512,8,2]{1,2,0:T(2,128)S(1)} %broadcast_in_dim.8, s32[1024]{0:T(1024)S(1)} %copy-done.51, f32[1024,8,2]{1,2,0:T(2,128)S(1)} %copy.795), kind=kCustom, calls=%fused_computation.4 | custom fusion | flops 16384 | bytes 200704 | tf_op jit(solution)/shard_map/scatter-add | solution.py:191
  388.4 6.9 %collective-permute-start.10 = (f32[1,8,2,16,128]{4,3,2,1,0:T(8,128)S(1)}, f32[1,8,2,16,128]{4,3,2,1,0:T(8,128)S(1)}, u32[]{:S(2)}, u32[]{:S(2)}) collective-permute-start(f32[1,8,2,16,128]{4,3,2,1,0:T(8,128)S(1)} %get-tuple-element.300), channel_id=1, source_target_pairs={{4,0},{8,4},{12,8},{16,12},{20,16},{24,20},{28,24},{32,28},{36,32}... | collective-permute-start | bytes 393224 | tf_op jit(solution)/shard_map/ppermute | solution.py:21
  395.3 2.1 collective-permute-start.11
  397.7 12.3 %cholesky.105 = f32[128,128]{1,0:T(8,128)} custom-call(f32[128,128]{1,0:T(8,128)S(1)} %convolution_subtract_fusion), custom_call_target="Cholesky" | custom-call | tf_op jit(solution)/shard_map/jit(cholesky)/cholesky | solution.py:199
  413.4 7.0 %collective-permute-start.12 = (f32[1,8,2,16,128]{4,3,2,1,0:T(8,128)S(1)}, f32[1,8,2,16,128]{4,3,2,1,0:T(8,128)S(1)}, u32[]{:S(2)}, u32[]{:S(2)}) collective-permute-start(f32[1,8,2,16,128]{4,3,2,1,0:T(8,128)S(1)} %get-tuple-element.282), channel_id=1, source_target_pairs={{4,0},{8,4},{12,8},{16,12},{20,16},{24,20},{28,24},{32,28},{36,32}... | collective-permute-start | bytes 393224 | tf_op jit(solution)/shard_map/ppermute | solution.py:21
  420.3 1.9 collective-permute-start.13
  424.3 5.7 collective-permute-done.13
  433.1 1.9 collective-permute-start.14
  435.0 2.6 collective-permute-start.15
  437.7 6.9 %collective-permute-done.15 = f32[1,8,2,16,128]{4,3,2,1,0:T(8,128)S(1)} collective-permute-done((f32[1,8,2,16,128]{4,3,2,1,0:T(8,128)S(1)}, f32[1,8,2,16,128]{4,3,2,1,0:T(8,128)S(1)}, u32[]{:S(2)}, u32[]{:S(2)}) %collective-permute-start.15) | collective-permute-done | bytes 131104 | tf_op jit(solution)/shard_map/ppermute | solution.py:20
  449.7 2.4 collective-permute-start.17
  452.2 5.2 while.1
  452.8 2.0 bitcast_dynamic-update-slice_fusion.2
  455.3 2.0 bitcast_dynamic-update-slice_fusion.2
  457.4 20.5 %custom-call.19 = f32[2,128,128]{1,2,0:T(8,128)S(1)} custom-call(f32[2,128,128]{2,1,0:T(8,128)} %get-tuple-element.9), custom_call_target="InvertDiagBlocksLowerTriangular" | custom-call | tf_op jit(solution)/shard_map/jit(_cho_solve)/triangular_solve | solution.py:200
  480.5 130.7 %psum.15 = f32[256,8]{0,1:T(8,128)S(1)} all-reduce(f32[256,8]{0,1:T(8,128)S(1)} %convolution_bitcast_fusion.3), channel_id=1, replica_groups=mesh['tile'=64,'probe'=4] {'tile'}, use_global_device_ids=true, to_apply=%region_12.13 | all-reduce | flops 2048 | bytes 16384 | tf_op jit(solution)/shard_map/psum | solution.py:198
  (370 shorter events, 58.1 us)
Async XLA Ops:
  7.2 285.8 %copy-start = (f32[512,512]{1,0:T(8,128)S(1)}, f32[512,512]{1,0:T(8,128)}, u32[]{:S(2)}) copy-start(f32[512,512]{1,0:T(8,128)} %param.16) | copy-start | bytes 3145732
  8.1 44.5 %collective-permute-start = (f32[2,19,128]{2,1,0:T(8,128)S(1)}, f32[2,19,128]{2,1,0:T(8,128)S(1)}, u32[]{:S(2)}, u32[]{:S(2)}) collective-permute-start(f32[2,19,128]{2,1,0:T(8,128)S(1)} %get-tuple-element.401), channel_id=1, source_target_pairs={{4,0},{8,4},{12,8},{16,12},{20,16},{24,20},{28,24},{32,28},{36,32}... | collective-permute-start | bytes 58376 | tf_op jit(solution)/shard_map/ppermute | solution.py:21
  12.0 40.6 %collective-permute-start.1 = (f32[2,19,128]{2,1,0:T(8,128)S(1)}, f32[2,19,128]{2,1,0:T(8,128)S(1)}, u32[]{:S(2)}, u32[]{:S(2)}) collective-permute-start(f32[2,19,128]{2,1,0:T(8,128)S(1)} %get-tuple-element.402), channel_id=1, source_target_pairs={{0,4},{4,8},{8,12},{12,16},{16,20},{20,24},{24,28},{28,32},{32,36}... | collective-permute-start | bytes 58376 | tf_op jit(solution)/shard_map/ppermute | solution.py:20
  14.6 33.4 %copy-start.7 = (f32[4,16,128]{2,1,0:T(8,128)S(1)}, f32[4,16,128]{2,1,0:T(8,128)}, u32[]{:S(2)}) copy-start(f32[4,16,128]{2,1,0:T(8,128)} %param.10) | copy-start | bytes 98308
  14.6 33.4 %copy-start.43 = (f32[4,2,128]{2,1,0:T(2,128)S(1)}, f32[4,2,128]{2,1,0:T(2,128)}, u32[]{:S(2)}) copy-start(f32[4,2,128]{2,1,0:T(2,128)} %param.12) | copy-start | bytes 12292
  14.7 33.4 %copy-start.46 = (f32[4,128]{1,0:T(4,128)S(1)}, f32[4,128]{1,0:T(4,128)}, u32[]{:S(2)}) copy-start(f32[4,128]{1,0:T(4,128)} %param.11) | copy-start | bytes 6148
  14.7 34.0 %copy-start.52 = (f32[2,512]{1,0:T(2,128)S(1)}, f32[2,512]{1,0:T(2,128)}, u32[]{:S(2)}) copy-start(f32[2,512]{1,0:T(2,128)} %param.15) | copy-start | bytes 12292
  20.9 29.7 %all-to-all-start = ((s32[64,1,16]{2,1,0:T(1,128)}), s32[64,1,16]{2,1,0:T(1,128)S(1)}, u32[]{:S(2)}, u32[]{:S(2)}) async-start(s32[64,1,16]{2,1,0:T(1,128)} %bitcast.52), calls=%async_computation | async-start | bytes 65536 | tf_op jit(solution)/shard_map/all_to_all | solution.py:162
  32.5 188.1 %all-reduce.15.cloned.1.call-start = ((), (), s32[]{:S(2)}) async-start(), calls=%async_computation.3 | async-start | bytes 524288 | tf_op jit(solution)/shard_map/psum | solution.py:198
  53.0 171.0 %copy-start.16 = (f32[4,1,128]{2,1,0:T(1,128)}, f32[4,1,128]{2,1,0:T(1,128)S(1)}, u32[]{:S(2)}) copy-start(f32[4,1,128]{2,1,0:T(1,128)S(1)} %get-tuple-element.419) | copy-start | bytes 6148
  53.0 171.0 %copy-start.19 = (f32[4,1,128]{2,1,0:T(1,128)}, f32[4,1,128]{2,1,0:T(1,128)S(1)}, u32[]{:S(2)}) copy-start(f32[4,1,128]{2,1,0:T(1,128)S(1)} %get-tuple-element.420) | copy-start | bytes 6148
  53.0 171.0 %copy-start.22 = (f32[4,1,128]{2,1,0:T(1,128)}, f32[4,1,128]{2,1,0:T(1,128)S(1)}, u32[]{:S(2)}) copy-start(f32[4,1,128]{2,1,0:T(1,128)S(1)} %get-tuple-element.421) | copy-start | bytes 6148
  53.0 171.0 %copy-start.25 = (f32[4,1,128]{2,1,0:T(1,128)}, f32[4,1,128]{2,1,0:T(1,128)S(1)}, u32[]{:S(2)}) copy-start(f32[4,1,128]{2,1,0:T(1,128)S(1)} %get-tuple-element.422) | copy-start | bytes 6148
  53.0 171.0 %copy-start.28 = (f32[4,1,128]{2,1,0:T(1,128)}, f32[4,1,128]{2,1,0:T(1,128)S(1)}, u32[]{:S(2)}) copy-start(f32[4,1,128]{2,1,0:T(1,128)S(1)} %get-tuple-element.424) | copy-start | bytes 6148
  53.0 171.0 %copy-start.31 = (f32[4,1,128]{2,1,0:T(1,128)}, f32[4,1,128]{2,1,0:T(1,128)S(1)}, u32[]{:S(2)}) copy-start(f32[4,1,128]{2,1,0:T(1,128)S(1)} %get-tuple-element.426) | copy-start | bytes 6148
  53.0 171.0 %copy-start.34 = (f32[4,1,128]{2,1,0:T(1,128)}, f32[4,1,128]{2,1,0:T(1,128)S(1)}, u32[]{:S(2)}) copy-start(f32[4,1,128]{2,1,0:T(1,128)S(1)} %get-tuple-element.428) | copy-start | bytes 6148
  53.0 171.0 %copy-start.37 = (f32[4,1,128]{2,1,0:T(1,128)}, f32[4,1,128]{2,1,0:T(1,128)S(1)}, u32[]{:S(2)}) copy-start(f32[4,1,128]{2,1,0:T(1,128)S(1)} %get-tuple-element.430) | copy-start | bytes 6148
  53.1 171.0 %copy-start.40 = (f32[4,1,128]{2,1,0:T(1,128)}, f32[4,1,128]{2,1,0:T(1,128)S(1)}, u32[]{:S(2)}) copy-start(f32[4,1,128]{2,1,0:T(1,128)S(1)} %get-tuple-element.432) | copy-start | bytes 6148
  53.9 45.1 %copy-start.10 = (f32[4,2,128]{2,1,0:T(2,128)}, f32[4,2,128]{2,1,0:T(2,128)S(1)}, u32[]{:S(2)}) copy-start(f32[4,2,128]{2,1,0:T(2,128)S(1)} %copy.614) | copy-start | bytes 12292
  53.9 45.1 %copy-start.13 = (f32[4,2,128]{2,1,0:T(2,128)}, f32[4,2,128]{2,1,0:T(2,128)S(1)}, u32[]{:S(2)}) copy-start(f32[4,2,128]{2,1,0:T(2,128)S(1)} %copy.617) | copy-start | bytes 12292
  55.5 4.9 collective-permute-start.2
  57.9 9.6 %collective-permute-start.3 = (f32[1,8,2,16,128]{4,3,2,1,0:T(8,128)S(1)}, f32[1,8,2,16,128]{4,3,2,1,0:T(8,128)S(1)}, u32[]{:S(2)}, u32[]{:S(2)}) collective-permute-start(f32[1,8,2,16,128]{4,3,2,1,0:T(8,128)S(1)} %get-tuple-element.373), channel_id=1, source_target_pairs={{0,4},{4,8},{8,12},{12,16},{16,20},{20,24},{24,28},{28,32},{32,36}... | collective-permute-start | bytes 393224 | tf_op jit(solution)/shard_map/ppermute | solution.py:20
  70.8 5.1 collective-permute-start.4
  72.8 9.7 %collective-permute-start.5 = (f32[1,8,2,16,128]{4,3,2,1,0:T(8,128)S(1)}, f32[1,8,2,16,128]{4,3,2,1,0:T(8,128)S(1)}, u32[]{:S(2)}, u32[]{:S(2)}) collective-permute-start(f32[1,8,2,16,128]{4,3,2,1,0:T(8,128)S(1)} %get-tuple-element.355), channel_id=1, source_target_pairs={{0,4},{4,8},{8,12},{12,16},{16,20},{20,24},{24,28},{28,32},{32,36}... | collective-permute-start | bytes 393224 | tf_op jit(solution)/shard_map/ppermute | solution.py:20
  85.8 4.4 collective-permute-start.6
  87.7 9.7 %collective-permute-start.7 = (f32[1,8,2,16,128]{4,3,2,1,0:T(8,128)S(1)}, f32[1,8,2,16,128]{4,3,2,1,0:T(8,128)S(1)}, u32[]{:S(2)}, u32[]{:S(2)}) collective-permute-start(f32[1,8,2,16,128]{4,3,2,1,0:T(8,128)S(1)} %get-tuple-element.337), channel_id=1, source_target_pairs={{0,4},{4,8},{8,12},{12,16},{16,20},{20,24},{24,28},{28,32},{32,36}... | collective-permute-start | bytes 393224 | tf_op jit(solution)/shard_map/ppermute | solution.py:20
  100.7 121.8 %collective-permute-start.8 = (f32[1,8,2,16,128]{4,3,2,1,0:T(8,128)S(1)}, f32[1,8,2,16,128]{4,3,2,1,0:T(8,128)S(1)}, u32[]{:S(2)}, u32[]{:S(2)}) collective-permute-start(f32[1,8,2,16,128]{4,3,2,1,0:T(8,128)S(1)} %get-tuple-element.320), channel_id=1, source_target_pairs={{4,0},{8,4},{12,8},{16,12},{20,16},{24,20},{28,24},{32,28},{36,32}... | collective-permute-start | bytes 393224 | tf_op jit(solution)/shard_map/ppermute | solution.py:21
  102.6 119.8 %collective-permute-start.9 = (f32[1,8,2,16,128]{4,3,2,1,0:T(8,128)S(1)}, f32[1,8,2,16,128]{4,3,2,1,0:T(8,128)S(1)}, u32[]{:S(2)}, u32[]{:S(2)}) collective-permute-start(f32[1,8,2,16,128]{4,3,2,1,0:T(8,128)S(1)} %get-tuple-element.319), channel_id=1, source_target_pairs={{0,4},{4,8},{8,12},{12,16},{16,20},{20,24},{24,28},{28,32},{32,36}... | collective-permute-start | bytes 393224 | tf_op jit(solution)/shard_map/ppermute | solution.py:20
  241.9 34.4 %all-to-all-start.1 = ((f32[64,1,256]{2,1,0:T(1,128)}), f32[64,1,256]{2,1,0:T(1,128)S(1)}, u32[]{:S(2)}, u32[]{:S(2)}) async-start(f32[64,1,256]{2,1,0:T(1,128)} %all_to_all.24), calls=%async_computation.1 | async-start | bytes 131072 | tf_op jit(solution)/shard_map/all_to_all | solution.py:167
  323.1 15.5 %all-to-all-start.2 = ((f32[64,1,256]{2,1,0:T(1,128)}), f32[64,1,256]{2,1,0:T(1,128)S(1)}, u32[]{:S(2)}, u32[]{:S(2)}) async-start(f32[64,1,256]{2,1,0:T(1,128)} %all_to_all.25), calls=%async_computation.2 | async-start | bytes 131072 | tf_op jit(solution)/shard_map/all_to_all | solution.py:183
  352.8 33.3 %copy-start.17 = (f32[4,1,128]{2,1,0:T(1,128)S(1)}, f32[4,1,128]{2,1,0:T(1,128)}, u32[]{:S(2)}) copy-start(f32[4,1,128]{2,1,0:T(1,128)} %copy-done.16) | copy-start | bytes 6148
  352.9 33.3 %copy-start.20 = (f32[4,1,128]{2,1,0:T(1,128)S(1)}, f32[4,1,128]{2,1,0:T(1,128)}, u32[]{:S(2)}) copy-start(f32[4,1,128]{2,1,0:T(1,128)} %copy-done.19) | copy-start | bytes 6148
  352.9 33.3 %copy-start.23 = (f32[4,1,128]{2,1,0:T(1,128)S(1)}, f32[4,1,128]{2,1,0:T(1,128)}, u32[]{:S(2)}) copy-start(f32[4,1,128]{2,1,0:T(1,128)} %copy-done.22) | copy-start | bytes 6148
  352.9 33.3 %copy-start.26 = (f32[4,1,128]{2,1,0:T(1,128)S(1)}, f32[4,1,128]{2,1,0:T(1,128)}, u32[]{:S(2)}) copy-start(f32[4,1,128]{2,1,0:T(1,128)} %copy-done.25) | copy-start | bytes 6148
  352.9 33.3 %copy-start.29 = (f32[4,1,128]{2,1,0:T(1,128)S(1)}, f32[4,1,128]{2,1,0:T(1,128)}, u32[]{:S(2)}) copy-start(f32[4,1,128]{2,1,0:T(1,128)} %copy-done.28) | copy-start | bytes 6148
  352.9 33.3 %copy-start.32 = (f32[4,1,128]{2,1,0:T(1,128)S(1)}, f32[4,1,128]{2,1,0:T(1,128)}, u32[]{:S(2)}) copy-start(f32[4,1,128]{2,1,0:T(1,128)} %copy-done.31) | copy-start | bytes 6148
  352.9 33.3 %copy-start.35 = (f32[4,1,128]{2,1,0:T(1,128)S(1)}, f32[4,1,128]{2,1,0:T(1,128)}, u32[]{:S(2)}) copy-start(f32[4,1,128]{2,1,0:T(1,128)} %copy-done.34) | copy-start | bytes 6148
  352.9 33.3 %copy-start.38 = (f32[4,1,128]{2,1,0:T(1,128)S(1)}, f32[4,1,128]{2,1,0:T(1,128)}, u32[]{:S(2)}) copy-start(f32[4,1,128]{2,1,0:T(1,128)} %copy-done.37) | copy-start | bytes 6148
  352.9 33.3 %copy-start.41 = (f32[4,1,128]{2,1,0:T(1,128)S(1)}, f32[4,1,128]{2,1,0:T(1,128)}, u32[]{:S(2)}) copy-start(f32[4,1,128]{2,1,0:T(1,128)} %copy-done.40) | copy-start | bytes 6148
  388.4 21.6 %collective-permute-start.10 = (f32[1,8,2,16,128]{4,3,2,1,0:T(8,128)S(1)}, f32[1,8,2,16,128]{4,3,2,1,0:T(8,128)S(1)}, u32[]{:S(2)}, u32[]{:S(2)}) collective-permute-start(f32[1,8,2,16,128]{4,3,2,1,0:T(8,128)S(1)} %get-tuple-element.300), channel_id=1, source_target_pairs={{4,0},{8,4},{12,8},{16,12},{20,16},{24,20},{28,24},{32,28},{36,32}... | collective-permute-start | bytes 393224 | tf_op jit(solution)/shard_map/ppermute | solution.py:21
  395.3 14.7 %collective-permute-start.11 = (f32[1,8,2,16,128]{4,3,2,1,0:T(8,128)S(1)}, f32[1,8,2,16,128]{4,3,2,1,0:T(8,128)S(1)}, u32[]{:S(2)}, u32[]{:S(2)}) collective-permute-start(f32[1,8,2,16,128]{4,3,2,1,0:T(8,128)S(1)} %get-tuple-element.299), channel_id=1, source_target_pairs={{0,4},{4,8},{8,12},{12,16},{16,20},{20,24},{24,28},{28,32},{32,36}... | collective-permute-start | bytes 393224 | tf_op jit(solution)/shard_map/ppermute | solution.py:20
  413.4 10.9 %collective-permute-start.12 = (f32[1,8,2,16,128]{4,3,2,1,0:T(8,128)S(1)}, f32[1,8,2,16,128]{4,3,2,1,0:T(8,128)S(1)}, u32[]{:S(2)}, u32[]{:S(2)}) collective-permute-start(f32[1,8,2,16,128]{4,3,2,1,0:T(8,128)S(1)} %get-tuple-element.282), channel_id=1, source_target_pairs={{4,0},{8,4},{12,8},{16,12},{20,16},{24,20},{28,24},{32,28},{36,32}... | collective-permute-start | bytes 393224 | tf_op jit(solution)/shard_map/ppermute | solution.py:21
  420.3 9.6 %collective-permute-start.13 = (f32[1,8,2,16,128]{4,3,2,1,0:T(8,128)S(1)}, f32[1,8,2,16,128]{4,3,2,1,0:T(8,128)S(1)}, u32[]{:S(2)}, u32[]{:S(2)}) collective-permute-start(f32[1,8,2,16,128]{4,3,2,1,0:T(8,128)S(1)} %get-tuple-element.281), channel_id=1, source_target_pairs={{0,4},{4,8},{8,12},{12,16},{16,20},{20,24},{24,28},{28,32},{32,36}... | collective-permute-start | bytes 393224 | tf_op jit(solution)/shard_map/ppermute | solution.py:20
  433.1 4.6 collective-permute-start.14
  435.0 9.6 %collective-permute-start.15 = (f32[1,8,2,16,128]{4,3,2,1,0:T(8,128)S(1)}, f32[1,8,2,16,128]{4,3,2,1,0:T(8,128)S(1)}, u32[]{:S(2)}, u32[]{:S(2)}) collective-permute-start(f32[1,8,2,16,128]{4,3,2,1,0:T(8,128)S(1)} %get-tuple-element.263), channel_id=1, source_target_pairs={{0,4},{4,8},{8,12},{12,16},{16,20},{20,24},{24,28},{28,32},{32,36}... | collective-permute-start | bytes 393224 | tf_op jit(solution)/shard_map/ppermute | solution.py:20
  447.7 30.1 %collective-permute-start.16 = (f32[1,8,2,16,128]{4,3,2,1,0:T(8,128)S(1)}, f32[1,8,2,16,128]{4,3,2,1,0:T(8,128)S(1)}, u32[]{:S(2)}, u32[]{:S(2)}) collective-permute-start(f32[1,8,2,16,128]{4,3,2,1,0:T(8,128)S(1)} %get-tuple-element.246), channel_id=1, source_target_pairs={{4,0},{8,4},{12,8},{16,12},{20,16},{24,20},{28,24},{32,28},{36,32}... | collective-permute-start | bytes 393224 | tf_op jit(solution)/shard_map/ppermute | solution.py:21
  449.7 28.2 %collective-permute-start.17 = (f32[1,8,2,16,128]{4,3,2,1,0:T(8,128)S(1)}, f32[1,8,2,16,128]{4,3,2,1,0:T(8,128)S(1)}, u32[]{:S(2)}, u32[]{:S(2)}) collective-permute-start(f32[1,8,2,16,128]{4,3,2,1,0:T(8,128)S(1)} %get-tuple-element.245), channel_id=1, source_target_pairs={{0,4},{4,8},{8,12},{12,16},{16,20},{20,24},{24,28},{28,32},{32,36}... | collective-permute-start | bytes 393224 | tf_op jit(solution)/shard_map/ppermute | solution.py:20
  479.0 134.9 %copy-start.1 = (f32[512,512]{1,0:T(8,128)S(1)}, f32[512,512]{1,0:T(8,128)}, u32[]{:S(2)}) copy-start(f32[512,512]{1,0:T(8,128)} %param.16) | copy-start | bytes 3145732
  (30 other events, 309.8 us)
Sparse Core Ops, SparseCore 0:
  48.1 172.5 all-reduce.14
where the time goes:
time: 629 us; the launch traced here: 621 us
  waiting for transfers between devices  153 us (24%)
  blocking collectives  144 us (23%)
  other arithmetic  117 us (19%)
  local copies, waits for them, and re-layouts  99.7 us (16%)
  starting transfers between devices  82.8 us (13%)
  between operations  18 us (3%)
    psum x1, blocking collectives, per_device(): gram, moments = lax.psum((gram_part, moment_part), 'tile')  131 us
    psum x1, waiting for transfers between devices, per_device(): gram, moments = lax.psum((gram_part, moment_part), 'tile')  115 us
    another operation x6, other arithmetic, per_device(): factor = jnp.linalg.cholesky(gram)  35.8 us
    ppermute x9, waiting for transfers between devices, extended_2(): before = lax.ppermute(last, axis, up)  33.4 us
    scatter-add x1, other arithmetic, per_device(): jax.ops.segment_sum(returned, asked, num_segments=cells_x * cells_y)  33 us
    ppermute x9, starting transfers between devices, extended_2(): after = lax.ppermute(first, axis, down)  29.8 us
    scatter x2, local copies, waits for them, and re-layouts, per_device(): outgoing = jnp.zeros((tile_count * capacity, probe_count, 2), jnp.float32...  21.6 us
    another operation x3, other arithmetic, per_device(): coeffs = jax.scipy.linalg.cho_solve((factor, True), moments)  21 us
  transfers between devices with their start and end apart: 22, of which 8 were waited for; matrix products, arithmetic and copies ran while one was open for 15% of the time, Pallas kernels for 0%

commit v1 on v0

v1 whole, which is shorter than its diff:
```python
import functools

import jax
import jax.numpy as jnp
from jax import lax
from jax.experimental import pallas as pl
from jax.experimental.pallas import tpu as pltpu
from jax.sharding import PartitionSpec as P

SWEEPS = 5
CX = 4
NY = 128
NZ = 16
KD = 8
CAP = 16
TILES = 64
ROWS = CX * 3
ASPECT = 1024.0
N_COEF = 13
F_E, F_W, A_N, A_S, C_PP, C_MP, C_PM, C_MM, LOW, INV_U, INV_V, Q_U, Q_V = range(N_COEF)
BLOCK = 64
f32 = jnp.float32
bf16 = jnp.bfloat16
PARAMS = pltpu.CompilerParams(vmem_limit_bytes=32 * 2**20)
VM = pl.BlockSpec(memory_space=pltpu.VMEM)
SM = pl.BlockSpec(memory_space=pltpu.SMEM)

NN = (((1,), (0,)), ((), ()))
NT = (((1,), (1,)), ((), ()))


def call(kernel, out_shape, args, scratch=(), scalars=0, flops=0, moved=0, aliases=None):
    single = not isinstance(out_shape, (list, tuple))
    shapes = [out_shape] if single else list(out_shape)
    out = pl.pallas_call(
        kernel,
        out_shape=shapes,
        in_specs=[SM] * scalars + [VM] * (len(args) - scalars),
        out_specs=[VM] * len(shapes),
        scratch_shapes=list(scratch),
        compiler_params=PARAMS,
        input_output_aliases=aliases or {},
        cost_estimate=pl.CostEstimate(flops=flops, bytes_accessed=moved, transcendentals=0),
    )(*args)
    return out[0] if single else out


def sds(shape, dtype=f32):
    return jax.ShapeDtypeStruct(shape, dtype)


def dot(a, b, dims):
    return lax.dot_general(a, b, dims, preferred_element_type=f32)


def split2(x):
    high = x.astype(bf16)
    return high, (x - high.astype(f32)).astype(bf16)


def split3(x):
    high = x.astype(bf16)
    rest = x - high.astype(f32)
    middle = rest.astype(bf16)
    return high, middle, (rest - middle.astype(f32)).astype(bf16)


def dot3(a, b, dims):
    a_high, a_low = a
    b_high, b_low = b
    return dot(a_high, b_high, dims) + (dot(a_high, b_low, dims) + dot(a_low, b_high, dims))


def iota(shape, axis):
    return lax.broadcasted_iota(jnp.int32, shape, axis)


def meta_kernel(tile_ref, cell_ref, sight_ref, payload_ref, rank_ref):
    rows = tile_ref.shape[1]
    one_hot = (iota((TILES, rows), 0) == tile_ref[...]).astype(f32)
    before = (iota((rows, rows), 0) < iota((rows, rows), 1)).astype(f32).astype(bf16)
    one_hot_b = one_hot.astype(bf16)
    earlier = dot(one_hot_b, before, NN)
    rank = jnp.sum(one_hot * earlier, axis=0, keepdims=True).astype(jnp.int32)
    rank_ref[...] = rank
    chosen = (iota((CAP, rows), 0) == rank).astype(f32)
    values = jnp.concatenate(
        [
            chosen * cell_ref[...].astype(f32),
            chosen * sight_ref[0:1, :],
            chosen * sight_ref[1:2, :],
            jnp.zeros((128 - 3 * CAP, rows), f32),
        ],
        axis=0,
    )
    parts = [dot(one_hot_b, part, NT) for part in split3(values)]
    payload_ref[...] = parts[0] + (parts[1] + parts[2])


def build_coefs(visc, fric, coef, upper):
    lane = iota((NZ, NY), 1)
    layer = iota((NZ, NY), 0)

    def row(i, carry):
        centre = visc[i]
        east = visc[i + 1]
        west = visc[i - 1]

        def from_south(x):
            return pltpu.roll(x, 1, 1)

        def from_north(x):
            return pltpu.roll(x, NY - 1, 1)

        south_centre = jnp.where(lane == 0, 0.0, from_south(centre))
        north_centre = jnp.where(lane == NY - 1, 0.0, from_north(centre))
        face_e = 0.5 * (centre + east)
        face_w = 0.5 * (centre + west)
        face_n = 0.5 * (centre + north_centre)
        face_s = 0.5 * (centre + south_centre)
        coef[F_E, i - 1] = face_e
        coef[F_W, i - 1] = face_w
        coef[A_N, i - 1] = jnp.where(lane == 0, 0.0, face_s)
        coef[A_S, i - 1] = jnp.where(lane == NY - 1, 0.0, face_n)
        coef[C_PP, i - 1] = jnp.where(lane == 0, 0.0, 0.375 * (south_centre + east))
        coef[C_MP, i - 1] = jnp.where(lane == 0, 0.0, -0.375 * (south_centre + west))
        coef[C_PM, i - 1] = jnp.where(lane == NY - 1, 0.0, -0.375 * (north_centre + east))
        coef[C_MM, i - 1] = jnp.where(lane == NY - 1, 0.0, 0.375 * (north_centre + west))
        above = pltpu.roll(centre, NZ - 1, 0)
        up = jnp.where(layer == NZ - 1, 0.0, ASPECT * 0.5 * (centre + above))
        down = jnp.where(layer == 0, 0.0, pltpu.roll(up, 1, 0))
        coef[LOW, i - 1] = down
        upper[i - 1] = up
        column = (up + down) + jnp.where(layer == 0, fric[i - 1], 0.0)
        coef[INV_U, i - 1] = 4.0 * (face_e + face_w) + (face_n + face_s) + column
        coef[INV_V, i - 1] = face_e + face_w + 4.0 * (face_n + face_s) + column
        return carry

    lax.fori_loop(1, ROWS + 1, row, 0)
    inside = visc[pl.ds(1, ROWS), 0, :] > 0.0
    ratio_u = ratio_v = None
    for layer_index in range(NZ):
        pivot_u = coef[INV_U, :, layer_index, :]
        pivot_v = coef[INV_V, :, layer_index, :]
        if layer_index > 0:
            low = coef[LOW, :, layer_index, :]
            pivot_u = pivot_u - low * ratio_u
            pivot_v = pivot_v - low * ratio_v
        inverse_u = jnp.where(inside, 1.0 / pivot_u, 0.0)
        inverse_v = jnp.where(inside, 1.0 / pivot_v, 0.0)
        up = upper[:, layer_index, :]
        ratio_u = up * inverse_u
        ratio_v = up * inverse_v
        coef[INV_U, :, layer_index, :] = inverse_u
        coef[INV_V, :, layer_index, :] = inverse_v
        coef[Q_U, :, layer_index, :] = ratio_u
        coef[Q_V, :, layer_index, :] = ratio_v


def run_sweeps(coef, load, fields, load_layer, finish):
    far = NZ - 1 if load_layer == 0 else 0

    def take(which, i, layer_index):
        return jnp.broadcast_to(coef[which, i, layer_index : layer_index + 1, :], (KD, NY))

    def solve(i, right_u, right_v, last):
        forward_u, forward_v = [], []
        for k in range(NZ):
            u, v = right_u(k), right_v(k)
            if k == load_layer:
                u = load[i, 0] if u is None else u + load[i, 0]
                v = load[i, 1] if v is None else v + load[i, 1]
            if k > 0 and forward_u[-1] is not None:
                low = take(LOW, i, k)
                below_u, below_v = low * forward_u[-1], low * forward_v[-1]
                u = below_u if u is None else u + below_u
                v = below_v if v is None else v + below_v
            forward_u.append(None if u is None else u * take(INV_U, i, k))
            forward_v.append(None if v is None else v * take(INV_V, i, k))
        solved_u, solved_v = [None] * NZ, [None] * NZ
        solved_u[-1], solved_v[-1] = forward_u[-1], forward_v[-1]
        if not (last and far == NZ - 1):
            for k in range(NZ - 2, -1, -1):
                u = take(Q_U, i, k) * solved_u[k + 1]
                v = take(Q_V, i, k) * solved_v[k + 1]
                solved_u[k] = u if forward_u[k] is None else forward_u[k] + u
                solved_v[k] = v if forward_v[k] is None else forward_v[k] + v
        return solved_u, solved_v

    for sweep in range(SWEEPS):
        source, target = fields[(sweep + 1) % 2], fields[sweep % 2]
        last = sweep == SWEEPS - 1

        def row(i, carry, sweep=sweep, source=source, target=target, last=last):
            if sweep == 0:
                nothing = lambda k: None
                solved_u, solved_v = solve(i, nothing, nothing, last)
            else:

                def sides(component, k, along):
                    other = 1 - component
                    mine, east, west = (source[i + d, component, k] for d in (0, 1, -1))
                    cross_e, cross_w = (source[i + d, other, k] for d in (1, -1))
                    direct = take(F_E, i, k) * east + take(F_W, i, k) * west
                    if along:
                        direct = 4.0 * direct
                        scaled = mine
                    else:
                        scaled = 4.0 * mine
                    north = take(A_N, i, k) * scaled + (
                        take(C_PP, i, k) * cross_e + take(C_MP, i, k) * cross_w
                    )
                    south = take(A_S, i, k) * scaled + (
                        take(C_PM, i, k) * cross_e + take(C_MM, i, k) * cross_w
                    )
                    return direct + (pltpu.roll(north, NY - 1, 1) + pltpu.roll(south, 1, 1))

                solved_u, solved_v = solve(
                    i,
                    lambda k: sides(0, k, True),
                    lambda k: sides(1, k, False),
                    last,
                )
            if last:
                finish(i - CX, solved_u[far], solved_v[far])
            else:
                for k in range(NZ):
                    target[i, 0, k] = solved_u[k]
                    target[i, 1, k] = solved_v[k]
            return carry

        lax.fori_loop(sweep, ROWS - sweep, row, 0)


V_AT, P_AT, B_AT, F_AT, PACK = 0, CX * NZ, CX * (NZ + KD), CX * (NZ + KD + 2), 112


def state_kernel(
    own, left, right, far_left, far_right, surface, coef, gain, visc, upper, fric, load, field_a, field_b
):
    visc[0] = far_left[...]
    visc[ROWS + 1] = far_right[...]
    for part, packed in enumerate((left, own, right)):
        for x in range(CX):
            i = part * CX + x
            visc[i + 1] = packed[V_AT + x * NZ : V_AT + (x + 1) * NZ, :]
            friction = packed[F_AT + x : F_AT + x + 1, :]
            fric[i] = friction
            probes = packed[P_AT + x * KD : P_AT + (x + 1) * KD, :]
            for m in range(2):
                basal = -(friction * packed[B_AT + 2 * x + m : B_AT + 2 * x + m + 1, :])
                if part == 1:
                    gain[m, x : x + 1, :] = basal
                load[i, m] = basal * probes
    build_coefs(visc, fric, coef, upper)

    def finish(x, u, v):
        surface[0, x] = u
        surface[1, x] = v

    run_sweeps(coef, load, (field_a, field_b), 0, finish)


def adjoint_kernel(
    own, left, right, coef, gain, panel_high, panel_low, hessian, moments, load, field_a, field_b
):
    for part, packed in enumerate((left, own, right)):
        for x in range(CX):
            for m in range(2):
                load[part * CX + x, m] = packed[m * KD : (m + 1) * KD, x * NY : (x + 1) * NY]

    def finish(x, u, v):
        hessian[x] = gain[0, pl.ds(x, 1), :] * u + gain[1, pl.ds(x, 1), :] * v

    run_sweeps(coef, load, (field_a, field_b), NZ - 1, finish)
    whole = jnp.concatenate([hessian[x] for x in range(CX)], axis=1)
    moments[...] = dot3(split2(whole), (panel_high[...], panel_low[...]), NT)


def gram_kernel(me_ref, own, near, across, back, panel_high, panel_low, part):
    me = me_ref[0]
    count = own.shape[0] // CX
    mine = None
    for shift, block in enumerate((own, near, across, back)):
        source = lax.rem(me - shift + 4, 4)
        flat = jnp.concatenate(
            [block[pl.ds(x, count, stride=CX), :] for x in range(CX)], axis=1
        )
        high, low = split2(flat)
        if shift == 0:
            mine = (high, low)
        at = pl.ds(pl.multiple_of(source * count, count), count)
        panel_high[at, :] = high
        panel_low[at, :] = low
    part[...] = dot3(mine, (panel_high[...], panel_low[...]), NT)


def invert_block(block):
    size = block.shape[0]
    row_of = iota(block.shape, 0)
    lane_of = iota(block.shape, 1)
    for k in range(size):
        column = jnp.broadcast_to(block[:, k : k + 1], block.shape)
        inverse = 1.0 / jnp.broadcast_to(column[k : k + 1, :], (1, size))
        pivot_row = jnp.where(lane_of[0:1, :] == k, 1.0, block[k : k + 1, :]) * inverse
        column = jnp.where(row_of == k, -1.0, column)
        block = jnp.where((row_of == k) | (lane_of == k), 0.0, block) - column * pivot_row
    return block


def dot_f32(a, b):
    a1, a2, a3 = split3(a)
    b1, b2, b3 = split3(b)
    small = dot(a1, b3, NN) + dot(a3, b1, NN) + dot(a2, b2, NN)
    return dot(a1, b1, NN) + ((dot(a1, b2, NN) + dot(a2, b1, NN)) + small)


def eliminate(matrix, number):
    size = matrix.shape[0]
    at = slice(number * BLOCK, (number + 1) * BLOCK)
    inverse = invert_block(matrix[at, at])
    panel = matrix[at, :]
    columns = matrix[:, at]
    lanes = iota((BLOCK, size), 1)
    own_lanes = (lanes >= number * BLOCK) & (lanes < (number + 1) * BLOCK)
    identity = (iota((BLOCK, size), 0) + number * BLOCK == lanes).astype(f32)
    rows = dot_f32(inverse, jnp.where(own_lanes, identity, panel))
    rest = matrix[...]
    all_lanes = iota((size, size), 1)
    inside = (all_lanes >= number * BLOCK) & (all_lanes < (number + 1) * BLOCK)
    matrix[...] = jnp.where(inside, 0.0, rest) - dot_f32(columns, rows)
    matrix[at, :] = rows


def first_kernel(me_ref, own, near, across, back, matrix):
    me = me_ref[0]
    count = own.shape[0]
    for shift, block in enumerate((own, near, across, back)):
        source = lax.rem(me - shift + 4, 4)
        matrix[pl.ds(pl.multiple_of(source * count, count), count), :] = block[...]
    eliminate(matrix, 0)


def next_kernel(number, before, matrix):
    matrix[...] = before[...]
    eliminate(matrix, number)


def slot_rows(meta):
    wide = jnp.concatenate([meta[...], jnp.zeros((128 - TILES, 128), f32)], axis=0)
    turned = jnp.transpose(wide)
    half = CAP // 2

    def paired(at):
        return turned[at : at + half] + pltpu.roll(turned[at + half : at + CAP], TILES, 1)

    return paired(0), paired(CAP), paired(2 * CAP)


def slot_one_hot(cells):
    index = cells.astype(jnp.int32)
    at = iota((CX * NY, 128), 0)
    return jnp.concatenate(
        [(at == index[j : j + 1, :]).astype(f32).astype(bf16) for j in range(CAP // 2)], axis=1
    )


def gather_kernel(meta, surface, gram_part, payload):
    cells, sight_u, sight_v = slot_rows(meta)
    one_hot = slot_one_hot(cells)
    both = jnp.concatenate(
        [jnp.concatenate([surface[m, x] for x in range(CX)], axis=1) for m in range(2)], axis=0
    )
    picked = dot(jnp.concatenate(split3(both), axis=0), one_hot, NN)
    n = 2 * KD
    picked = picked[0:n] + (picked[n : 2 * n] + picked[2 * n : 3 * n])
    chunks = []
    for j in range(CAP // 2):
        at = slice(j * 128, (j + 1) * 128)
        chunks.append(
            sight_u[j : j + 1, :] * picked[0:KD, at] + sight_v[j : j + 1, :] * picked[KD:n, at]
        )
    chunks.append(jnp.zeros((128 - TILES, 128), f32))
    turned = jnp.transpose(jnp.concatenate(chunks, axis=0))
    payload[pl.ds(0, TILES, stride=4), :] = turned[0:TILES] + pltpu.roll(turned[TILES:], TILES, 1)
    payload[pl.ds(1, TILES, stride=4), :] = gram_part[:, 0:128]
    payload[pl.ds(2, TILES, stride=4), :] = gram_part[:, 128:256]
    payload[pl.ds(3, TILES, stride=4), :] = jnp.zeros((TILES, 128), f32)


def precision_kernel(arrived, tile_ref, rank_ref, precision, payload):
    rows = tile_ref.shape[1]
    one_hot = (iota((128, rows), 0) == tile_ref[...]).astype(f32).astype(bf16)
    rank = rank_ref[...]
    mine = arrived[pl.ds(0, TILES, stride=4), :]
    turned = jnp.transpose(jnp.concatenate([mine, jnp.zeros((128 - TILES, 128), f32)], axis=0))
    spread = [dot(part, one_hot, NN) for part in split3(turned)]
    spread = spread[0] + (spread[1] + spread[2])
    predicted = jnp.zeros((KD, rows), f32)
    for s in range(CAP):
        predicted = predicted + jnp.where(rank == s, spread[s * KD : (s + 1) * KD], 0.0)
    weighted = dot3(split2(predicted), split2(precision[...]), NN)
    slots = jnp.concatenate([jnp.where(rank == s, weighted, 0.0) for s in range(CAP)], axis=0)
    sent = [dot(one_hot, part, NT) for part in split3(slots)]
    sent = sent[0] + (sent[1] + sent[2])
    payload[pl.ds(0, TILES, stride=4), :] = sent[0:TILES]
    for k in (1, 2):
        total = jnp.sum(arrived[pl.ds(k, TILES, stride=4), :], axis=0, keepdims=True)
        payload[pl.ds(k, TILES, stride=4), :] = jnp.broadcast_to(total, (TILES, 128))
    payload[pl.ds(3, TILES, stride=4), :] = jnp.zeros((TILES, 128), f32)


def scatter_kernel(returned, meta, top, gram_rows):
    cells, sight_u, sight_v = slot_rows(meta)
    one_hot = slot_one_hot(cells)
    mine = returned[pl.ds(0, TILES, stride=4), :]
    turned = jnp.transpose(jnp.concatenate([mine, pltpu.roll(mine, TILES, 1)], axis=0))
    loads = []
    for sight in (sight_u, sight_v):
        loads.append(
            jnp.concatenate(
                [turned[j * KD : (j + 1) * KD] * sight[j : j + 1, :] for j in range(CAP // 2)],
                axis=1,
            )
        )
    parts = dot(jnp.concatenate(split3(jnp.concatenate(loads, axis=0)), axis=0), one_hot, NT)
    n = 2 * KD
    top[...] = parts[0:n] + (parts[n : 2 * n] + parts[2 * n : 3 * n])
    gram_rows[:, 0:128] = returned[pl.ds(1, TILES, stride=4), :]
    gram_rows[:, 128:256] = returned[pl.ds(2, TILES, stride=4), :]


def final_kernel(moments, inverse, panel_high, panel_low, hessian, filtered, coefficients):
    solved = dot_f32(moments[...], inverse[...])
    coefficients[...] = solved
    removed = dot3(split2(solved), (panel_high[...], panel_low[...]), NN)
    for x in range(CX):
        filtered[x] = hessian[x] - removed[:, x * NY : (x + 1) * NY]


def along(value, axis, shift):
    count = lax.axis_size(axis)
    return lax.ppermute(
        value, axis, [(i, i + shift) for i in range(count) if 0 <= i + shift < count]
    )


def around(value, axis, shift):
    count = lax.axis_size(axis)
    return lax.ppermute(value, axis, [(i, (i + shift) % count) for i in range(count)])


def per_device(
    probes, viscosity, friction, base_velocity, obs_tile, obs_cell, sight_lines, obs_precision, basis
):
    cells = CX * NY
    me = lax.axis_index("probe").astype(jnp.int32).reshape(1)
    packed = jnp.concatenate(
        [
            viscosity.reshape(CX * NZ, NY),
            probes.reshape(CX * KD, NY),
            base_velocity.reshape(CX * 2, NY),
            friction,
            jnp.zeros((PACK - F_AT - CX, NY), f32),
        ],
        axis=0,
    )
    left = along(packed, "tile", 1)
    right = along(packed, "tile", -1)
    far_left = along(viscosity[CX - 1], "tile", 2)
    far_right = along(viscosity[0], "tile", -2)

    tile_row = obs_tile.reshape(1, -1)
    rows = tile_row.shape[1]
    asked, rank = call(
        meta_kernel,
        [sds((TILES, 128)), sds((1, rows), jnp.int32)],
        [tile_row, obs_cell.reshape(1, -1), sight_lines],
        flops=2 * 64 * 512 * 1000,
        moved=10000,
    )
    meta = lax.all_to_all(asked, "tile", split_axis=0, concat_axis=0, tiled=True)

    own_basis = basis.reshape(-1, NY)
    others = [around(own_basis, "probe", d) for d in (1, 2, 3)]

    field = pltpu.VMEM((ROWS, 2, NZ, KD, NY), f32)
    load = pltpu.VMEM((ROWS, 2, KD, NY), f32)
    surface, coef, gain = call(
        state_kernel,
        [sds((2, CX, KD, NY)), sds((N_COEF, ROWS, NZ, NY)), sds((2, CX, NY))],
        [packed, left, right, far_left, far_right],
        scratch=[
            pltpu.VMEM((ROWS + 2, NZ, NY), f32),
            pltpu.VMEM((ROWS, NZ, NY), f32),
            pltpu.VMEM((ROWS, 1, NY), f32),
            load,
            field,
            field,
        ],
        flops=40 * 16 * 44 * 1024,
        moved=2000000,
    )
    n_basis = 4 * basis.shape[0]
    panel_high, panel_low, gram_part = call(
        gram_kernel,
        [sds((n_basis, cells), bf16), sds((n_basis, cells), bf16), sds((TILES, n_basis))],
        [me, own_basis, *others],
        scalars=1,
        flops=6 * 64 * 512 * 256,
        moved=1500000,
    )
    payload = call(
        gather_kernel,
        sds((TILES * 4, 128)),
        [meta, surface, gram_part],
        flops=2 * 48 * 512 * 1024,
        moved=300000,
    )

    def exchange(value):
        return lax.all_to_all(
            value.reshape(TILES, 4, 128), "tile", split_axis=0, concat_axis=0, tiled=True
        ).reshape(TILES * 4, 128)

    arrived = exchange(payload)
    outgoing = call(
        precision_kernel,
        sds((TILES * 4, 128)),
        [arrived, tile_row, rank, obs_precision],
        flops=2 * 512 * 512 * 64,
        moved=1500000,
    )
    returned = exchange(outgoing)
    top, gram_rows = call(
        scatter_kernel,
        [sds((2 * KD, cells)), sds((TILES, n_basis))],
        [returned, meta],
        flops=2 * 48 * 512 * 1024,
        moved=300000,
    )
    top_left = along(top, "tile", 1)
    top_right = along(top, "tile", -1)
    quarters = [around(gram_rows, "probe", d) for d in (1, 2, 3)]
    hessian, moments = call(
        adjoint_kernel,
        [sds((CX, KD, NY)), sds((KD, n_basis))],
        [top, top_left, top_right, coef, gain, panel_high, panel_low],
        scratch=[load, field, field],
        flops=40 * 16 * 44 * 1024,
        moved=2000000,
    )
    matrix = call(
        first_kernel,
        sds((n_basis, n_basis)),
        [me, gram_rows, *quarters],
        scalars=1,
        flops=12 * 64 * 256 * 256,
        moved=500000,
    )
    for number in range(1, n_basis // BLOCK):
        matrix = call(
            functools.partial(next_kernel, number),
            sds((n_basis, n_basis)),
            [matrix],
            flops=12 * 64 * 256 * 256,
            moved=500000,
        )
    step = 1
    while step < TILES:
        moments = moments + lax.ppermute(moments, "tile", [(i, i ^ step) for i in range(TILES)])
        step *= 2
    filtered, coefficients = call(
        final_kernel,
        [sds((CX, KD, NY)), sds((KD, n_basis))],
        [moments, matrix, panel_high, panel_low, hessian],
        flops=12 * 8 * 256 * 512,
        moved=800000,
    )
    return filtered, coefficients


def solution(mesh):
    in_specs = (
        P("tile", "probe", None),
        P("tile", None, None),
        P("tile", None),
        P("tile", None, None),
        P("tile", None),
        P("tile"),
        P(None, "tile"),
        P("tile", None),
        P("probe", "tile", None),
    )
    out_specs = (P("tile", "probe", None), P("probe", None))
    return jax.shard_map(
        per_device, mesh=mesh, in_specs=in_specs, out_specs=out_specs, check_vma=False
    )
```

time: 629 us -> 145 us (0.23)
  the two profiles are of different devices: /device:TPU:128 before, /device:TPU:2 now
where the time goes in v1:
time: 145 us; the launch traced here: 144 us
  starting transfers between devices  50 us (34%)
  Pallas kernels  41.8 us (29%)
  blocking collectives  35.2 us (24%)
  waiting for transfers between devices  9.11 us (6%)
  local copies, waits for them, and re-layouts  7.21 us (5%)
    pallas_call x12, Pallas kernels, call(): pl.pallas_call(kernel, out_shape=shapes, in_specs=[SM] * scalars + [VM] *...  41.8 us
    all_to_all x2, blocking collectives, exchange(): lax.all_to_all(value.reshape(TILES, 4, 128), 'tile', split_axis=0, concat...  35.2 us
    all_to_all x1, starting transfers between devices, per_device(): lax.all_to_all(asked, 'tile', split_axis=0, concat_axis=0, tiled=True)  15.4 us
    ppermute x6, starting transfers between devices, along(): lax.ppermute(value, axis, [(i, i + shift) for i in range(count) if 0 <= i...  14.5 us
    ppermute x6, starting transfers between devices, per_device(): lax.ppermute(moments, 'tile', [(i, i ^ step) for i in range(TILES)])  11.2 us
    ppermute x6, starting transfers between devices, around(): lax.ppermute(value, axis, [(i, (i + shift) % count) for i in range(count)])  8.95 us
    ppermute x6, waiting for transfers between devices, per_device(): lax.ppermute(moments, 'tile', [(i, i ^ step) for i in range(TILES)])  8.18 us
    unnamed x12, local copies, waits for them, and re-layouts  3.63 us
  transfers between devices with their start and end apart: 19, of which 5 were waited for; matrix products, arithmetic and copies ran while one was open for 2% of the time, Pallas kernels for 27%

profile of v1, /device:TPU:2, one launch (start us, length us, event | category | flops | bytes accessed | tf_op | source)
XLA Modules:
  0.0 144.2 jit_solution(4107010950901305497)
XLA Ops:
  0.6 2.3 %collective-permute-start.6 = (f32[256,128]{1,0:T(8,128)}, f32[256,128]{1,0:T(8,128)S(1)}, u32[]{:S(2)}, u32[]{:S(2)}) collective-permute-start(f32[256,128]{1,0:T(8,128)} %bitcast.22), channel_id=1, source_target_pairs={{0,3},{1,0},{2,1},{3,2},{4,7},{5,4},{6,5},{7,6},{8,11},{9,8},{10,9... | collective-permute-start | bytes 393224 | tf_op jit(solution)/shard_map/ppermute | solution.py:450
  3.0 0.7 collective-permute-start.5
  3.7 1.8 %collective-permute-start.4 = (f32[256,128]{1,0:T(8,128)}, f32[256,128]{1,0:T(8,128)S(1)}, u32[]{:S(2)}, u32[]{:S(2)}) collective-permute-start(f32[256,128]{1,0:T(8,128)} %bitcast.24), channel_id=1, source_target_pairs={{0,1},{1,2},{2,3},{3,0},{4,5},{5,6},{6,7},{7,4},{8,9},{9,10},{10,1... | collective-permute-start | bytes 393224 | tf_op jit(solution)/shard_map/ppermute | solution.py:450
  5.5 0.7 slice_bitcast_fusion
  6.2 1.3 collective-permute-start.3
  7.5 4.5 %collective-permute-start.2 = (f32[16,128]{1,0:T(8,128)S(1)}, f32[16,128]{1,0:T(8,128)S(1)}, u32[]{:S(2)}, u32[]{:S(2)}) collective-permute-start(f32[16,128]{1,0:T(8,128)S(1)} %get-tuple-element.27), channel_id=1, source_target_pairs={{0,8},{4,12},{8,16},{12,20},{16,24},{20,28},{24,32},{28,36},{32,40... | collective-permute-start | bytes 24584 | tf_op jit(solution)/shard_map/ppermute | solution.py:443
  12.0 2.9 %concatenate.3.own = f32[112,128]{1,0:T(8,128)S(1)} concatenate(f32[64,128]{1,0:T(8,128)} %bitcast.32, f32[32,128]{1,0:T(8,128)} %bitcast.33, f32[8,128]{1,0:T(8,128)} %bitcast.34, f32[4,128]{1,0:T(4,128)} %param.11, f32[4,128]{1,0:T(4,128)S(1)} %broadcast_in_dim.3), dimensions={0} | concatenate | bytes 114688 | tf_op jit(solution)/shard_map/concatenate | solution.py:458
  14.9 1.3 collective-permute-start.1
  16.2 3.0 %collective-permute-start = (f32[112,128]{1,0:T(8,128)S(1)}, f32[112,128]{1,0:T(8,128)S(1)}, u32[]{:S(2)}, u32[]{:S(2)}) collective-permute-start(f32[112,128]{1,0:T(8,128)S(1)} %concatenate.3.own), channel_id=1, source_target_pairs={{0,4},{4,8},{8,12},{12,16},{16,20},{20,24},{24,28},{28,32},{32,36}... | collective-permute-start | bytes 172040 | tf_op jit(solution)/shard_map/ppermute | solution.py:443
  19.3 0.0 copy-start.2
  19.3 0.7 copy-done.2
  19.9 0.7 copy-done.4
  20.6 0.7 copy-done.5
  21.3 1.1 shard_map.104
  22.4 15.4 %all-to-all-start = ((f32[64,1,128]{2,1,0:T(1,128)}), f32[64,1,128]{2,1,0:T(1,128)S(1)}, u32[]{:S(2)}, u32[]{:S(2)}) async-start(f32[64,1,128]{2,1,0:T(1,128)} %bitcast.3), calls=%async_computation | async-start | bytes 65536 | tf_op jit(solution)/shard_map/all_to_all | solution.py:482
  37.9 0.0 collective-permute-done.1.right
  37.9 7.3 %shard_map.105 = (f32[2,4,8,128]{3,2,1,0:T(8,128)S(1)}, f32[13,12,16,128]{3,2,1,0:T(8,128)S(1)}, f32[2,4,128]{2,1,0:T(4,128)S(1)}) custom-call(f32[112,128]{1,0:T(8,128)S(1)} %concatenate.3.own, f32[112,128]{1,0:T(8,128)S(1)} %collective-permute-done.left, f32[112,128]{1,0:T(8,128)S(1)} %collective-permute-done.1.right, ...), custom_call_target="tpu_custom_call" | custom-call | flops 28835840 | bytes 2000000 | tf_op jit(solution)/shard_map/pallas_call | solution.py:35
  45.2 0.0 copy-start.1
  45.3 0.9 copy-done.1
  46.1 0.4 shard_map.106
  46.6 0.9 all-to-all-done
  47.5 0.6 shard_map.107
  48.1 20.3 %all_to_all.21 = f32[64,4,128]{2,1,0:T(4,128)S(1)} all-to-all(f32[64,4,128]{2,1,0:T(4,128)S(1)} %bitcast.21), channel_id=1, replica_groups=mesh['tile'=64,'probe'=4] {'tile'}, dimensions={0} | all-to-all | bytes 262144 | tf_op jit(solution)/shard_map/all_to_all | solution.py:522
  68.3 0.7 copy-done.3
  69.0 1.0 shard_map.108
  70.0 14.9 %all_to_all.22 = f32[64,4,128]{2,1,0:T(4,128)S(1)} all-to-all(f32[64,4,128]{2,1,0:T(4,128)S(1)} %bitcast.20), channel_id=1, replica_groups=mesh['tile'=64,'probe'=4] {'tile'}, dimensions={0} | all-to-all | bytes 262144 | tf_op jit(solution)/shard_map/all_to_all | solution.py:522
  84.9 0.5 shard_map.109
  85.5 1.3 collective-permute-start.8
  86.8 3.0 %collective-permute-start.7 = (f32[16,512]{1,0:T(8,128)S(1)}, f32[16,512]{1,0:T(8,128)S(1)}, u32[]{:S(2)}, u32[]{:S(2)}) collective-permute-start(f32[16,512]{1,0:T(8,128)S(1)} %get-tuple-element.18.own), channel_id=1, source_target_pairs={{0,4},{4,8},{8,12},{12,16},{16,20},{20,24},{24,28},{28,32},{32,36}... | collective-permute-start | bytes 98312 | tf_op jit(solution)/shard_map/ppermute | solution.py:443
  89.8 0.3 collective-permute-start.17
  90.1 1.5 %collective-permute-start.16 = (f32[64,256]{1,0:T(8,128)S(1)}, f32[64,256]{1,0:T(8,128)S(1)}, u32[]{:S(2)}, u32[]{:S(2)}) collective-permute-start(f32[64,256]{1,0:T(8,128)S(1)} %get-tuple-element.24.own), channel_id=1, source_target_pairs={{0,2},{1,3},{2,0},{3,1},{4,6},{5,7},{6,4},{7,5},{8,10},{9,11},{10,... | collective-permute-start | bytes 196616 | tf_op jit(solution)/shard_map/ppermute | solution.py:450
  91.7 2.3 %collective-permute-start.15 = (f32[64,256]{1,0:T(8,128)S(1)}, f32[64,256]{1,0:T(8,128)S(1)}, u32[]{:S(2)}, u32[]{:S(2)}) collective-permute-start(f32[64,256]{1,0:T(8,128)S(1)} %get-tuple-element.24.own), channel_id=1, source_target_pairs={{0,1},{1,2},{2,3},{3,0},{4,5},{5,6},{6,7},{7,4},{8,9},{9,10},{10,1... | collective-permute-start | bytes 196616 | tf_op jit(solution)/shard_map/ppermute | solution.py:450
  94.0 5.7 %shard_map.110 = (f32[4,8,128]{2,1,0:T(8,128)S(1)}, f32[8,256]{1,0:T(8,128)S(1)}) custom-call(f32[16,512]{1,0:T(8,128)S(1)} %get-tuple-element.18.own, f32[16,512]{1,0:T(8,128)S(1)} %collective-permute-done.7.left, f32[16,512]{1,0:T(8,128)S(1)} %collective-permute-done.8.right, f32[13,12,16,128]{3,2,1,0:T(8,128)S(1)} %get-tuple-element.19.coef, ...), custom_call_target="tpu_custom_call" | custom-call | flops 28835840 | bytes 2000000 | tf_op jit(solution)/shard_map/pallas_call | solution.py:35
  99.7 0.5 collective-permute-start.9
  100.2 0.8 collective-permute-done.9
  101.0 1.1 collective-permute-start.10
  102.1 2.6 %collective-permute-done.10 = f32[8,256]{1,0:T(8,128)S(1)} collective-permute-done((f32[8,256]{1,0:T(8,128)S(1)}, f32[8,256]{1,0:T(8,128)S(1)}, u32[]{:S(2)}, u32[]{:S(2)}) %collective-permute-start.10) | collective-permute-done | bytes 8224 | tf_op jit(solution)/shard_map/ppermute | solution.py:571
  104.7 2.0 %collective-permute-start.11 = (f32[8,256]{1,0:T(8,128)S(1)}, f32[8,256]{1,0:T(8,128)S(1)}, u32[]{:S(2)}, u32[]{:S(2)}) collective-permute-start(f32[8,256]{1,0:T(8,128)S(1)} %add.19), channel_id=1, source_target_pairs={{0,16},{4,20},{8,24},{12,28},{16,0},{20,4},{24,8},{28,12},{32,48},... | collective-permute-start | bytes 24584 | tf_op jit(solution)/shard_map/ppermute | solution.py:571
  106.7 3.1 %collective-permute-done.11 = f32[8,256]{1,0:T(8,128)S(1)} collective-permute-done((f32[8,256]{1,0:T(8,128)S(1)}, f32[8,256]{1,0:T(8,128)S(1)}, u32[]{:S(2)}, u32[]{:S(2)}) %collective-permute-start.11) | collective-permute-done | bytes 8224 | tf_op jit(solution)/shard_map/ppermute | solution.py:571
  109.8 2.3 %collective-permute-start.12 = (f32[8,256]{1,0:T(8,128)S(1)}, f32[8,256]{1,0:T(8,128)S(1)}, u32[]{:S(2)}, u32[]{:S(2)}) collective-permute-start(f32[8,256]{1,0:T(8,128)S(1)} %add.20), channel_id=1, source_target_pairs={{0,32},{4,36},{8,40},{12,44},{16,48},{20,52},{24,56},{28,60},{32,0... | collective-permute-start | bytes 24584 | tf_op jit(solution)/shard_map/ppermute | solution.py:571
  112.1 1.6 %collective-permute-done.12 = f32[8,256]{1,0:T(8,128)S(1)} collective-permute-done((f32[8,256]{1,0:T(8,128)S(1)}, f32[8,256]{1,0:T(8,128)S(1)}, u32[]{:S(2)}, u32[]{:S(2)}) %collective-permute-start.12) | collective-permute-done | bytes 8224 | tf_op jit(solution)/shard_map/ppermute | solution.py:571
  113.7 2.5 %collective-permute-start.13 = (f32[8,256]{1,0:T(8,128)S(1)}, f32[8,256]{1,0:T(8,128)S(1)}, u32[]{:S(2)}, u32[]{:S(2)}) collective-permute-start(f32[8,256]{1,0:T(8,128)S(1)} %add.21), channel_id=1, source_target_pairs={{0,64},{4,68},{8,72},{12,76},{16,80},{20,84},{24,88},{28,92},{32,9... | collective-permute-start | bytes 24584 | tf_op jit(solution)/shard_map/ppermute | solution.py:571
  116.2 6.0 %shard_map.111.before = f32[256,256]{1,0:T(8,128)S(1)} custom-call(s32[1]{0:T(128)} %bitcast.10.me_ref, f32[64,256]{1,0:T(8,128)S(1)} %get-tuple-element.24.own, f32[64,256]{1,0:T(8,128)S(1)} %collective-permute-done.15.near, f32[64,256]{1,0:T(8,128)S(1)} %collective-permute-done.16.across, f32[64,256]{1,0:T(8,128)S(1)} %collective-permute-done.17.back), custom_call_target="tpu_custom_call" | custom-call | flops 50331648 | bytes 500000 | tf_op jit(solution)/shard_map/pallas_call | solution.py:35
  122.2 6.0 %shard_map.112.before = f32[256,256]{1,0:T(8,128)S(1)} custom-call(f32[256,256]{1,0:T(8,128)S(1)} %shard_map.111.before), custom_call_target="tpu_custom_call" | custom-call | flops 50331648 | bytes 500000 | tf_op jit(solution)/shard_map/pallas_call | solution.py:35
  128.2 2.8 %collective-permute-start.14 = (f32[8,256]{1,0:T(8,128)S(1)}, f32[8,256]{1,0:T(8,128)S(1)}, u32[]{:S(2)}, u32[]{:S(2)}) collective-permute-start(f32[8,256]{1,0:T(8,128)S(1)} %add.22), channel_id=1, source_target_pairs={{0,128},{4,132},{8,136},{12,140},{16,144},{20,148},{24,152},{28,15... | collective-permute-start | bytes 24584 | tf_op jit(solution)/shard_map/ppermute | solution.py:571
  131.0 6.0 %shard_map.113.before = f32[256,256]{1,0:T(8,128)S(1)} custom-call(f32[256,256]{1,0:T(8,128)S(1)} %shard_map.112.before), custom_call_target="tpu_custom_call" | custom-call | flops 50331648 | bytes 500000 | tf_op jit(solution)/shard_map/pallas_call | solution.py:35
  137.0 6.0 %shard_map.114.inverse = f32[256,256]{1,0:T(8,128)S(1)} custom-call(f32[256,256]{1,0:T(8,128)S(1)} %shard_map.113.before), custom_call_target="tpu_custom_call" | custom-call | flops 50331648 | bytes 500000 | tf_op jit(solution)/shard_map/pallas_call | solution.py:35
  143.0 1.2 shard_map.115
  (25 shorter events, 0.1 us)
Async XLA Ops:
  0.6 67.7 %copy-start = (f32[512,512]{1,0:T(8,128)S(1)}, f32[512,512]{1,0:T(8,128)}, u32[]{:S(2)}) copy-start(f32[512,512]{1,0:T(8,128)} %precision.1) | copy-start | bytes 3145732
  0.6 44.6 %collective-permute-start.6 = (f32[256,128]{1,0:T(8,128)}, f32[256,128]{1,0:T(8,128)S(1)}, u32[]{:S(2)}, u32[]{:S(2)}) collective-permute-start(f32[256,128]{1,0:T(8,128)} %bitcast.22), channel_id=1, source_target_pairs={{0,3},{1,0},{2,1},{3,2},{4,7},{5,4},{6,5},{7,6},{8,11},{9,8},{10,9... | collective-permute-start | bytes 393224 | tf_op jit(solution)/shard_map/ppermute | solution.py:450
  3.0 42.2 %collective-permute-start.5 = (f32[256,128]{1,0:T(8,128)}, f32[256,128]{1,0:T(8,128)S(1)}, u32[]{:S(2)}, u32[]{:S(2)}) collective-permute-start(f32[256,128]{1,0:T(8,128)} %bitcast.23), channel_id=1, source_target_pairs={{0,2},{1,3},{2,0},{3,1},{4,6},{5,7},{6,4},{7,5},{8,10},{9,11},{10,... | collective-permute-start | bytes 393224 | tf_op jit(solution)/shard_map/ppermute | solution.py:450
  3.7 41.6 %collective-permute-start.4 = (f32[256,128]{1,0:T(8,128)}, f32[256,128]{1,0:T(8,128)S(1)}, u32[]{:S(2)}, u32[]{:S(2)}) collective-permute-start(f32[256,128]{1,0:T(8,128)} %bitcast.24), channel_id=1, source_target_pairs={{0,1},{1,2},{2,3},{3,0},{4,5},{5,6},{6,7},{7,4},{8,9},{9,10},{10,1... | collective-permute-start | bytes 393224 | tf_op jit(solution)/shard_map/ppermute | solution.py:450
  6.2 8.7 %collective-permute-start.3 = (f32[16,128]{1,0:T(8,128)S(1)}, f32[16,128]{1,0:T(8,128)S(1)}, u32[]{:S(2)}, u32[]{:S(2)}) collective-permute-start(f32[16,128]{1,0:T(8,128)S(1)} %get-tuple-element.26), channel_id=1, source_target_pairs={{8,0},{12,4},{16,8},{20,12},{24,16},{28,20},{32,24},{36,28},{40,32... | collective-permute-start | bytes 24584 | tf_op jit(solution)/shard_map/ppermute | solution.py:443
  7.5 8.7 %collective-permute-start.2 = (f32[16,128]{1,0:T(8,128)S(1)}, f32[16,128]{1,0:T(8,128)S(1)}, u32[]{:S(2)}, u32[]{:S(2)}) collective-permute-start(f32[16,128]{1,0:T(8,128)S(1)} %get-tuple-element.27), channel_id=1, source_target_pairs={{0,8},{4,12},{8,16},{12,20},{16,24},{20,28},{24,32},{28,36},{32,40... | collective-permute-start | bytes 24584 | tf_op jit(solution)/shard_map/ppermute | solution.py:443
  14.9 23.0 %collective-permute-start.1 = (f32[112,128]{1,0:T(8,128)S(1)}, f32[112,128]{1,0:T(8,128)S(1)}, u32[]{:S(2)}, u32[]{:S(2)}) collective-permute-start(f32[112,128]{1,0:T(8,128)S(1)} %concatenate.3.own), channel_id=1, source_target_pairs={{4,0},{8,4},{12,8},{16,12},{20,16},{24,20},{28,24},{32,28},{36,32}... | collective-permute-start | bytes 172040 | tf_op jit(solution)/shard_map/ppermute | solution.py:443
  16.2 21.7 %collective-permute-start = (f32[112,128]{1,0:T(8,128)S(1)}, f32[112,128]{1,0:T(8,128)S(1)}, u32[]{:S(2)}, u32[]{:S(2)}) collective-permute-start(f32[112,128]{1,0:T(8,128)S(1)} %concatenate.3.own), channel_id=1, source_target_pairs={{0,4},{4,8},{8,12},{12,16},{16,20},{20,24},{24,28},{28,32},{32,36}... | collective-permute-start | bytes 172040 | tf_op jit(solution)/shard_map/ppermute | solution.py:443
  19.3 0.7 copy-start.2
  19.9 0.7 copy-start.4
  20.6 0.7 copy-start.5
  22.4 25.0 %all-to-all-start = ((f32[64,1,128]{2,1,0:T(1,128)}), f32[64,1,128]{2,1,0:T(1,128)S(1)}, u32[]{:S(2)}, u32[]{:S(2)}) async-start(f32[64,1,128]{2,1,0:T(1,128)} %bitcast.3), calls=%async_computation | async-start | bytes 65536 | tf_op jit(solution)/shard_map/all_to_all | solution.py:482
  45.2 0.9 copy-start.1
  68.3 0.7 copy-start.3
  85.5 8.5 %collective-permute-start.8 = (f32[16,512]{1,0:T(8,128)S(1)}, f32[16,512]{1,0:T(8,128)S(1)}, u32[]{:S(2)}, u32[]{:S(2)}) collective-permute-start(f32[16,512]{1,0:T(8,128)S(1)} %get-tuple-element.18.own), channel_id=1, source_target_pairs={{4,0},{8,4},{12,8},{16,12},{20,16},{24,20},{28,24},{32,28},{36,32}... | collective-permute-start | bytes 98312 | tf_op jit(solution)/shard_map/ppermute | solution.py:443
  86.8 7.2 %collective-permute-start.7 = (f32[16,512]{1,0:T(8,128)S(1)}, f32[16,512]{1,0:T(8,128)S(1)}, u32[]{:S(2)}, u32[]{:S(2)}) collective-permute-start(f32[16,512]{1,0:T(8,128)S(1)} %get-tuple-element.18.own), channel_id=1, source_target_pairs={{0,4},{4,8},{8,12},{12,16},{16,20},{20,24},{24,28},{28,32},{32,36}... | collective-permute-start | bytes 98312 | tf_op jit(solution)/shard_map/ppermute | solution.py:443
  89.8 26.4 %collective-permute-start.17 = (f32[64,256]{1,0:T(8,128)S(1)}, f32[64,256]{1,0:T(8,128)S(1)}, u32[]{:S(2)}, u32[]{:S(2)}) collective-permute-start(f32[64,256]{1,0:T(8,128)S(1)} %get-tuple-element.24.own), channel_id=1, source_target_pairs={{0,3},{1,0},{2,1},{3,2},{4,7},{5,4},{6,5},{7,6},{8,11},{9,8},{10,9... | collective-permute-start | bytes 196616 | tf_op jit(solution)/shard_map/ppermute | solution.py:450
  90.1 26.1 %collective-permute-start.16 = (f32[64,256]{1,0:T(8,128)S(1)}, f32[64,256]{1,0:T(8,128)S(1)}, u32[]{:S(2)}, u32[]{:S(2)}) collective-permute-start(f32[64,256]{1,0:T(8,128)S(1)} %get-tuple-element.24.own), channel_id=1, source_target_pairs={{0,2},{1,3},{2,0},{3,1},{4,6},{5,7},{6,4},{7,5},{8,10},{9,11},{10,... | collective-permute-start | bytes 196616 | tf_op jit(solution)/shard_map/ppermute | solution.py:450
  91.7 24.5 %collective-permute-start.15 = (f32[64,256]{1,0:T(8,128)S(1)}, f32[64,256]{1,0:T(8,128)S(1)}, u32[]{:S(2)}, u32[]{:S(2)}) collective-permute-start(f32[64,256]{1,0:T(8,128)S(1)} %get-tuple-element.24.own), channel_id=1, source_target_pairs={{0,1},{1,2},{2,3},{3,0},{4,5},{5,6},{6,7},{7,4},{8,9},{9,10},{10,1... | collective-permute-start | bytes 196616 | tf_op jit(solution)/shard_map/ppermute | solution.py:450
  99.7 1.4 collective-permute-start.9
  101.0 3.7 %collective-permute-start.10 = (f32[8,256]{1,0:T(8,128)S(1)}, f32[8,256]{1,0:T(8,128)S(1)}, u32[]{:S(2)}, u32[]{:S(2)}) collective-permute-start(f32[8,256]{1,0:T(8,128)S(1)} %add.18), channel_id=1, source_target_pairs={{0,8},{4,12},{8,0},{12,4},{16,24},{20,28},{24,16},{28,20},{32,40},... | collective-permute-start | bytes 24584 | tf_op jit(solution)/shard_map/ppermute | solution.py:571
  104.7 5.2 %collective-permute-start.11 = (f32[8,256]{1,0:T(8,128)S(1)}, f32[8,256]{1,0:T(8,128)S(1)}, u32[]{:S(2)}, u32[]{:S(2)}) collective-permute-start(f32[8,256]{1,0:T(8,128)S(1)} %add.19), channel_id=1, source_target_pairs={{0,16},{4,20},{8,24},{12,28},{16,0},{20,4},{24,8},{28,12},{32,48},... | collective-permute-start | bytes 24584 | tf_op jit(solution)/shard_map/ppermute | solution.py:571
  109.8 3.9 %collective-permute-start.12 = (f32[8,256]{1,0:T(8,128)S(1)}, f32[8,256]{1,0:T(8,128)S(1)}, u32[]{:S(2)}, u32[]{:S(2)}) collective-permute-start(f32[8,256]{1,0:T(8,128)S(1)} %add.20), channel_id=1, source_target_pairs={{0,32},{4,36},{8,40},{12,44},{16,48},{20,52},{24,56},{28,60},{32,0... | collective-permute-start | bytes 24584 | tf_op jit(solution)/shard_map/ppermute | solution.py:571
  113.7 14.5 %collective-permute-start.13 = (f32[8,256]{1,0:T(8,128)S(1)}, f32[8,256]{1,0:T(8,128)S(1)}, u32[]{:S(2)}, u32[]{:S(2)}) collective-permute-start(f32[8,256]{1,0:T(8,128)S(1)} %add.21), channel_id=1, source_target_pairs={{0,64},{4,68},{8,72},{12,76},{16,80},{20,84},{24,88},{28,92},{32,9... | collective-permute-start | bytes 24584 | tf_op jit(solution)/shard_map/ppermute | solution.py:571
  128.2 14.8 %collective-permute-start.14 = (f32[8,256]{1,0:T(8,128)S(1)}, f32[8,256]{1,0:T(8,128)S(1)}, u32[]{:S(2)}, u32[]{:S(2)}) collective-permute-start(f32[8,256]{1,0:T(8,128)S(1)} %add.22), channel_id=1, source_target_pairs={{0,128},{4,132},{8,136},{12,140},{16,144},{20,148},{24,152},{28,15... | collective-permute-start | bytes 24584 | tf_op jit(solution)/shard_map/ppermute | solution.py:571

commit v2 on v1

--- a/solution.py
+++ b/solution.py
@@ -18,10 +18,14 @@
 ASPECT = 1024.0
 N_COEF = 13
 F_E, F_W, A_N, A_S, C_PP, C_MP, C_PM, C_MM, LOW, INV_U, INV_V, Q_U, Q_V = range(N_COEF)
-BLOCK = 64
+BLOCK = 32
+VMEM_PREP = 60
+PIVOTS = 4
+PIECES = (3, 4)
+V_AT, P_AT, B_AT, F_AT = 0, CX * NZ, CX * (NZ + KD), CX * (NZ + KD + 2)
+T_AT, R_AT, PACK = F_AT + CX, F_AT + 8, F_AT + 16
 f32 = jnp.float32
 bf16 = jnp.bfloat16
-PARAMS = pltpu.CompilerParams(vmem_limit_bytes=32 * 2**20)
 VM = pl.BlockSpec(memory_space=pltpu.VMEM)
 SM = pl.BlockSpec(memory_space=pltpu.SMEM)
 
@@ -29,17 +33,16 @@
 NT = (((1,), (1,)), ((), ()))
 
 
-def call(kernel, out_shape, args, scratch=(), scalars=0, flops=0, moved=0, aliases=None):
+def call(kernel, out_shape, args, scratch=(), scalars=0, flops=0, moved=0, places=None, vmem=14):
     single = not isinstance(out_shape, (list, tuple))
     shapes = [out_shape] if single else list(out_shape)
     out = pl.pallas_call(
         kernel,
         out_shape=shapes,
-        in_specs=[SM] * scalars + [VM] * (len(args) - scalars),
+        in_specs=places or [SM] * scalars + [VM] * (len(args) - scalars),
         out_specs=[VM] * len(shapes),
         scratch_shapes=list(scratch),
-        compiler_params=PARAMS,
-        input_output_aliases=aliases or {},
+        compiler_params=pltpu.CompilerParams(vmem_limit_bytes=int(vmem * 2**20)),
         cost_estimate=pl.CostEstimate(flops=flops, bytes_accessed=moved, transcendentals=0),
     )(*args)
     return out[0] if single else out
@@ -75,26 +78,56 @@
     return lax.broadcasted_iota(jnp.int32, shape, axis)
 
 
-def meta_kernel(tile_ref, cell_ref, sight_ref, payload_ref, rank_ref):
-    rows = tile_ref.shape[1]
-    one_hot = (iota((TILES, rows), 0) == tile_ref[...]).astype(f32)
+def prepare_kernel(
+    at_ref, visc, probes, base, fric, tile_row, cell_row, sight,
+    packed, edge_c, edge_d, asked,
+    fric_in, tile_in, cell_in, sight_in, sems,
+):
+    rows = tile_in.shape[1]
+    upper_pair = lax.rem(at_ref[0], 4) // 2
+    high_row = pl.multiple_of((CX - 1) * NZ * (1 - upper_pair), NZ)
+    low_row = pl.multiple_of((CX - 1) * NZ * upper_pair, NZ)
+    moves = [
+        (tile_row, tile_in),
+        (cell_row, cell_in),
+        (sight, sight_in),
+        (fric, fric_in),
+        (visc, packed.at[pl.ds(V_AT, CX * NZ), :]),
+        (probes, packed.at[pl.ds(P_AT, CX * KD), :]),
+        (base, packed.at[pl.ds(B_AT, CX * 2), :]),
+        (visc.at[pl.ds(high_row, NZ), :], edge_c),
+        (visc.at[pl.ds(low_row, NZ), :], edge_d),
+    ]
+    copies = [
+        pltpu.make_async_copy(source, target, sems.at[n])
+        for n, (source, target) in enumerate(moves)
+    ]
+    for copy in copies:
+        copy.start()
+    for copy in copies:
+        copy.wait()
+    one_hot = (iota((TILES, rows), 0) == tile_in[...]).astype(f32)
     before = (iota((rows, rows), 0) < iota((rows, rows), 1)).astype(f32).astype(bf16)
     one_hot_b = one_hot.astype(bf16)
     earlier = dot(one_hot_b, before, NN)
     rank = jnp.sum(one_hot * earlier, axis=0, keepdims=True).astype(jnp.int32)
-    rank_ref[...] = rank
+    tail = [fric_in[...]]
+    for values in (tile_in[...], rank):
+        tail += [values[:, n * 128 : (n + 1) * 128].astype(f32) for n in range(rows // 128)]
+    tail.append(jnp.zeros((PACK - F_AT - CX - 2 * rows // 128, NY), f32))
+    packed[F_AT:PACK, :] = jnp.concatenate(tail, axis=0)
     chosen = (iota((CAP, rows), 0) == rank).astype(f32)
     values = jnp.concatenate(
         [
-            chosen * cell_ref[...].astype(f32),
-            chosen * sight_ref[0:1, :],
-            chosen * sight_ref[1:2, :],
+            chosen * cell_in[...].astype(f32),
+            chosen * sight_in[0:1, :],
+            chosen * sight_in[1:2, :],
             jnp.zeros((128 - 3 * CAP, rows), f32),
         ],
         axis=0,
     )
     parts = [dot(one_hot_b, part, NT) for part in split3(values)]
-    payload_ref[...] = parts[0] + (parts[1] + parts[2])
+    asked[...] = parts[0] + (parts[1] + parts[2])
 
 
 def build_coefs(visc, fric, coef, upper):
@@ -229,18 +262,26 @@
                     target[i, 1, k] = solved_v[k]
             return carry
 
-        lax.fori_loop(sweep, ROWS - sweep, row, 0)
-
-
-V_AT, P_AT, B_AT, F_AT, PACK = 0, CX * NZ, CX * (NZ + KD), CX * (NZ + KD + 2), 112
+        def pair(j, carry, row=row, sweep=sweep):
+            return row(sweep + 2 * j + 1, row(sweep + 2 * j, carry))
+
+        lax.fori_loop(0, ROWS // 2 - sweep, pair, 0)
+
+
+def sides_of(at):
+    odd = lax.rem(at, 2)
+    return 2 - 2 * odd, 2 * odd
 
 
 def state_kernel(
-    own, left, right, far_left, far_right, surface, coef, gain, visc, upper, fric, load, field_a, field_b
+    at_ref, own, swap_a, swap_b, edge_c, edge_d, surface, coef, gain, visc, upper, fric, load, field_a, field_b
 ):
-    visc[0] = far_left[...]
-    visc[ROWS + 1] = far_right[...]
-    for part, packed in enumerate((left, own, right)):
+    at = at_ref[0]
+    part_a, part_b = sides_of(at)
+    upper_pair = lax.rem(at, 4) // 2
+    visc[(ROWS + 1) * (1 - upper_pair)] = edge_c[...]
+    visc[(ROWS + 1) * upper_pair] = edge_d[...]
+    for part, packed in ((part_a, swap_a), (1, own), (part_b, swap_b)):
         for x in range(CX):
             i = part * CX + x
             visc[i + 1] = packed[V_AT + x * NZ : V_AT + (x + 1) * NZ, :]
@@ -249,7 +290,7 @@
             probes = packed[P_AT + x * KD : P_AT + (x + 1) * KD, :]
             for m in range(2):
                 basal = -(friction * packed[B_AT + 2 * x + m : B_AT + 2 * x + m + 1, :])
-                if part == 1:
+                if packed is own:
                     gain[m, x : x + 1, :] = basal
                 load[i, m] = basal * probes
     build_coefs(visc, fric, coef, upper)
@@ -262,12 +303,15 @@
 
 
 def adjoint_kernel(
-    own, left, right, coef, gain, panel_high, panel_low, hessian, moments, load, field_a, field_b
+    returned, meta, coef, gain, panel_high, panel_low, hessian, moments, load, field_a, field_b
 ):
-    for part, packed in enumerate((left, own, right)):
+    beside = meta[pl.ds(3, TILES, stride=4), :]
+    metas = (beside, meta[pl.ds(0, TILES, stride=4), :], pltpu.roll(beside, TILES, 1))
+    for part, k in enumerate((1, 0, 2)):
+        top = top_load(returned[pl.ds(k, TILES, stride=4), :], metas[part])
         for x in range(CX):
             for m in range(2):
-                load[part * CX + x, m] = packed[m * KD : (m + 1) * KD, x * NY : (x + 1) * NY]
+                load[part * CX + x, m] = top[m * KD : (m + 1) * KD, x * NY : (x + 1) * NY]
 
     def finish(x, u, v):
         hessian[x] = gain[0, pl.ds(x, 1), :] * u + gain[1, pl.ds(x, 1), :] * v
@@ -277,12 +321,18 @@
     moments[...] = dot3(split2(whole), (panel_high[...], panel_low[...]), NT)
 
 
-def gram_kernel(me_ref, own, near, across, back, panel_high, panel_low, part):
+def from_tile(value, shift):
+    moved = pltpu.roll(value, -shift % TILES, 0)
+    edge = TILES - 1 if shift > 0 else 0
+    return jnp.where(iota(value.shape, 0) == edge, 0.0, moved)
+
+
+def gram_kernel(me_ref, own, near, across, back, asked, panel_high, panel_low, payload):
     me = me_ref[0]
     count = own.shape[0] // CX
     mine = None
     for shift, block in enumerate((own, near, across, back)):
-        source = lax.rem(me - shift + 4, 4)
+        source = me ^ shift
         flat = jnp.concatenate(
             [block[pl.ds(x, count, stride=CX), :] for x in range(CX)], axis=1
         )
@@ -292,19 +342,76 @@
         at = pl.ds(pl.multiple_of(source * count, count), count)
         panel_high[at, :] = high
         panel_low[at, :] = low
-    part[...] = dot3(mine, (panel_high[...], panel_low[...]), NT)
+    part = dot3(mine, (panel_high[...], panel_low[...]), NT)
+    here = asked[...]
+    payload[pl.ds(0, TILES, stride=4), :] = here
+    payload[pl.ds(1, TILES, stride=4), :] = part[:, 0:128]
+    payload[pl.ds(2, TILES, stride=4), :] = part[:, 128:256]
+    payload[pl.ds(3, TILES, stride=4), :] = from_tile(here, -1) + pltpu.roll(
+        from_tile(here, 1), TILES, 1
+    )
+
+
+def small_inverse(p):
+    size = len(p)
+    if size == 2:
+        (a, b), (_, d) = p
+        scale = 1.0 / (a * d - b * b)
+        off = -b * scale
+        return [[d * scale, off], [off, a * scale]]
+    h = size // 2
+
+    def times(x, y):
+        return [
+            [functools.reduce(lambda u, v: u + v, [x[i][k] * y[k][j] for k in range(h)]) for j in range(h)]
+            for i in range(h)
+        ]
+
+    a = [row[:h] for row in p[:h]]
+    b = [row[h:] for row in p[:h]]
+    c = [row[:h] for row in p[h:]]
+    d = [row[h:] for row in p[h:]]
+    a_inv = small_inverse(a)
+    x = times(a_inv, b)
+    cx = times(c, x)
+    s_inv = small_inverse([[d[i][j] - cx[i][j] for j in range(h)] for i in range(h)])
+    xs = times(x, s_inv)
+    x_t = [[x[j][i] for j in range(h)] for i in range(h)]
+    corner = times(xs, x_t)
+    top = [
+        [a_inv[i][j] + corner[i][j] for j in range(h)] + [-xs[i][j] for j in range(h)]
+        for i in range(h)
+    ]
+    bottom = [[-xs[j][i] for j in range(h)] + s_inv[i] for i in range(h)]
+    return top + bottom
 
 
 def invert_block(block):
     size = block.shape[0]
     row_of = iota(block.shape, 0)
     lane_of = iota(block.shape, 1)
-    for k in range(size):
-        column = jnp.broadcast_to(block[:, k : k + 1], block.shape)
-        inverse = 1.0 / jnp.broadcast_to(column[k : k + 1, :], (1, size))
-        pivot_row = jnp.where(lane_of[0:1, :] == k, 1.0, block[k : k + 1, :]) * inverse
-        column = jnp.where(row_of == k, -1.0, column)
-        block = jnp.where((row_of == k) | (lane_of == k), 0.0, block) - column * pivot_row
+    for k in range(0, size, PIVOTS):
+        columns = [jnp.broadcast_to(block[:, k + j : k + j + 1], block.shape) for j in range(PIVOTS)]
+        pivots = [[columns[j][k + i : k + i + 1, :] for j in range(PIVOTS)] for i in range(PIVOTS)]
+        inverse = small_inverse(pivots)
+        own_lane = (lane_of >= k) & (lane_of < k + PIVOTS)
+        own = own_lane | ((row_of >= k) & (row_of < k + PIVOTS))
+        rows = [
+            jnp.where(
+                own_lane[0:1, :],
+                jnp.where(lane_of[0:1, :] == k + j, 1.0, 0.0),
+                block[k + j : k + j + 1, :],
+            )
+            for j in range(PIVOTS)
+        ]
+        block = jnp.where(own, 0.0, block)
+        in_rows = (row_of >= k) & (row_of < k + PIVOTS)
+        for j in range(PIVOTS):
+            row = functools.reduce(
+                lambda u, v: u + v, [inverse[j][i] * rows[i] for i in range(PIVOTS)]
+            )
+            column = jnp.where(in_rows, jnp.where(row_of == k + j, -1.0, 0.0), columns[j])
+            block = block - column * row
     return block
 
 
@@ -334,10 +441,10 @@
 
 def first_kernel(me_ref, own, near, across, back, matrix):
     me = me_ref[0]
-    count = own.shape[0]
     for shift, block in enumerate((own, near, across, back)):
-        source = lax.rem(me - shift + 4, 4)
-        matrix[pl.ds(pl.multiple_of(source * count, count), count), :] = block[...]
+        at = pl.ds(pl.multiple_of((me ^ shift) * TILES, TILES), TILES)
+        matrix[at, 0:128] = block[pl.ds(1, TILES, stride=4), :]
+        matrix[at, 128:256] = block[pl.ds(2, TILES, stride=4), :]
     eliminate(matrix, 0)
 
 
@@ -347,7 +454,7 @@
 
 
 def slot_rows(meta):
-    wide = jnp.concatenate([meta[...], jnp.zeros((128 - TILES, 128), f32)], axis=0)
+    wide = jnp.concatenate([meta, jnp.zeros((128 - TILES, 128), f32)], axis=0)
     turned = jnp.transpose(wide)
     half = CAP // 2
 
@@ -365,8 +472,8 @@
     )
 
 
-def gather_kernel(meta, surface, gram_part, payload):
-    cells, sight_u, sight_v = slot_rows(meta)
+def gather_kernel(meta, surface, payload):
+    cells, sight_u, sight_v = slot_rows(meta[pl.ds(0, TILES, stride=4), :])
     one_hot = slot_one_hot(cells)
     both = jnp.concatenate(
         [jnp.concatenate([surface[m, x] for x in range(CX)], axis=1) for m in range(2)], axis=0
@@ -383,15 +490,26 @@
     chunks.append(jnp.zeros((128 - TILES, 128), f32))
     turned = jnp.transpose(jnp.concatenate(chunks, axis=0))
     payload[pl.ds(0, TILES, stride=4), :] = turned[0:TILES] + pltpu.roll(turned[TILES:], TILES, 1)
-    payload[pl.ds(1, TILES, stride=4), :] = gram_part[:, 0:128]
-    payload[pl.ds(2, TILES, stride=4), :] = gram_part[:, 128:256]
+    for k in (1, 2):
+        total = jnp.sum(meta[pl.ds(k, TILES, stride=4), :], axis=0, keepdims=True)
+        payload[pl.ds(k, TILES, stride=4), :] = jnp.broadcast_to(total, (TILES, 128))
     payload[pl.ds(3, TILES, stride=4), :] = jnp.zeros((TILES, 128), f32)
 
 
-def precision_kernel(arrived, tile_ref, rank_ref, precision, payload):
-    rows = tile_ref.shape[1]
-    one_hot = (iota((128, rows), 0) == tile_ref[...]).astype(f32).astype(bf16)
-    rank = rank_ref[...]
+def split_kernel(precision, high, low):
+    high[...], low[...] = split2(precision[...])
+
+
+def precision_kernel(arrived, packed, precision_high, precision_low, payload):
+    rows = precision_high.shape[0]
+
+    def line(at):
+        return jnp.concatenate(
+            [packed[at + n : at + n + 1, :] for n in range(rows // 128)], axis=1
+        ).astype(jnp.int32)
+
+    one_hot = (iota((128, rows), 0) == line(T_AT)).astype(f32).astype(bf16)
+    rank = line(R_AT)
     mine = arrived[pl.ds(0, TILES, stride=4), :]
     turned = jnp.transpose(jnp.concatenate([mine, jnp.zeros((128 - TILES, 128), f32)], axis=0))
     spread = [dot(part, one_hot, NN) for part in split3(turned)]
@@ -399,55 +517,46 @@
     predicted = jnp.zeros((KD, rows), f32)
     for s in range(CAP):
         predicted = predicted + jnp.where(rank == s, spread[s * KD : (s + 1) * KD], 0.0)
-    weighted = dot3(split2(predicted), split2(precision[...]), NN)
-    slots = jnp.concatenate([jnp.where(rank == s, weighted, 0.0) for s in range(CAP)], axis=0)
-    sent = [dot(one_hot, part, NT) for part in split3(slots)]
+    weighted = dot3(split2(predicted), (precision_high[...], precision_low[...]), NN)
+    spots = jnp.concatenate([jnp.where(rank == s, weighted, 0.0) for s in range(CAP)], axis=0)
+    sent = [dot(one_hot, part, NT) for part in split3(spots)]
     sent = sent[0] + (sent[1] + sent[2])
-    payload[pl.ds(0, TILES, stride=4), :] = sent[0:TILES]
-    for k in (1, 2):
-        total = jnp.sum(arrived[pl.ds(k, TILES, stride=4), :], axis=0, keepdims=True)
-        payload[pl.ds(k, TILES, stride=4), :] = jnp.broadcast_to(total, (TILES, 128))
+    sent = sent[0:TILES]
+    payload[pl.ds(0, TILES, stride=4), :] = sent
+    payload[pl.ds(1, TILES, stride=4), :] = from_tile(sent, -1)
+    payload[pl.ds(2, TILES, stride=4), :] = from_tile(sent, 1)
     payload[pl.ds(3, TILES, stride=4), :] = jnp.zeros((TILES, 128), f32)
 
 
-def scatter_kernel(returned, meta, top, gram_rows):
-    cells, sight_u, sight_v = slot_rows(meta)
+def top_load(mine, meta):
+    cells, *sights = slot_rows(meta)
     one_hot = slot_one_hot(cells)
-    mine = returned[pl.ds(0, TILES, stride=4), :]
     turned = jnp.transpose(jnp.concatenate([mine, pltpu.roll(mine, TILES, 1)], axis=0))
     loads = []
-    for sight in (sight_u, sight_v):
+    for m in range(2):
         loads.append(
             jnp.concatenate(
-                [turned[j * KD : (j + 1) * KD] * sight[j : j + 1, :] for j in range(CAP // 2)],
+                [turned[j * KD : (j + 1) * KD] * sights[m][j : j + 1, :] for j in range(CAP // 2)],
                 axis=1,
             )
         )
     parts = dot(jnp.concatenate(split3(jnp.concatenate(loads, axis=0)), axis=0), one_hot, NT)
     n = 2 * KD
-    top[...] = parts[0:n] + (parts[n : 2 * n] + parts[2 * n : 3 * n])
-    gram_rows[:, 0:128] = returned[pl.ds(1, TILES, stride=4), :]
-    gram_rows[:, 128:256] = returned[pl.ds(2, TILES, stride=4), :]
-
-
-def final_kernel(moments, inverse, panel_high, panel_low, hessian, filtered, coefficients):
-    solved = dot_f32(moments[...], inverse[...])
+    return parts[0:n] + (parts[n : 2 * n] + parts[2 * n : 3 * n])
+
+
+def final_kernel(parts, inverse, panel_high, panel_low, hessian, filtered, coefficients):
+    solved = dot_f32(jnp.sum(parts[...], axis=0), inverse[...])
     coefficients[...] = solved
     removed = dot3(split2(solved), (panel_high[...], panel_low[...]), NN)
     for x in range(CX):
         filtered[x] = hessian[x] - removed[:, x * NY : (x + 1) * NY]
 
 
-def along(value, axis, shift):
+def swap(value, axis, distance, offset=0):
     count = lax.axis_size(axis)
-    return lax.ppermute(
-        value, axis, [(i, i + shift) for i in range(count) if 0 <= i + shift < count]
-    )
-
-
-def around(value, axis, shift):
-    count = lax.axis_size(axis)
-    return lax.ppermute(value, axis, [(i, (i + shift) % count) for i in range(count)])
+    partner = [((i + offset) ^ distance) - offset for i in range(count)]
+    return lax.ppermute(value, axis, [(i, j) for i, j in enumerate(partner) if 0 <= j < count])
 
 
 def per_device(
@@ -455,41 +564,79 @@
 ):
     cells = CX * NY
     me = lax.axis_index("probe").astype(jnp.int32).reshape(1)
-    packed = jnp.concatenate(
+    at = lax.axis_index("tile").astype(jnp.int32).reshape(1)
+    rows = obs_cell.shape[0]
+    arguments = [
+        viscosity.reshape(CX * NZ, NY),
+        probes.reshape(CX * KD, NY),
+        base_velocity.reshape(CX * 2, NY),
+        friction,
+        obs_tile.reshape(1, -1),
+        obs_cell.reshape(1, -1),
+        sight_lines,
+    ]
+    own_basis = basis.reshape(-1, NY)
+    others = [swap(own_basis, "probe", d) for d in (1, 2, 3)]
+    packed, edge_c, edge_d, asked = call(
+        prepare_kernel,
         [
-            viscosity.reshape(CX * NZ, NY),
-            probes.reshape(CX * KD, NY),
-            base_velocity.reshape(CX * 2, NY),
-            friction,
-            jnp.zeros((PACK - F_AT - CX, NY), f32),
+            sds((PACK, NY)),
+            sds((NZ, NY)),
+            sds((NZ, NY)),
+            sds((TILES, 128)),
         ],
-        axis=0,
-    )
-    left = along(packed, "tile", 1)
-    right = along(packed, "tile", -1)
-    far_left = along(viscosity[CX - 1], "tile", 2)
-    far_right = along(viscosity[0], "tile", -2)
-
-    tile_row = obs_tile.reshape(1, -1)
-    rows = tile_row.shape[1]
-    asked, rank = call(
-        meta_kernel,
-        [sds((TILES, 128)), sds((1, rows), jnp.int32)],
-        [tile_row, obs_cell.reshape(1, -1), sight_lines],
+        [at, *arguments],
+        places=[SM] + [pl.BlockSpec(memory_space=pltpu.HBM)] * len(arguments),
+        scratch=[
+            pltpu.VMEM((CX, NY), f32),
+            pltpu.VMEM((1, rows), jnp.int32),
+            pltpu.VMEM((1, rows), jnp.int32),
+            pltpu.VMEM((2, rows), f32),
+            pltpu.SemaphoreType.DMA((9,)),
+        ],
         flops=2 * 64 * 512 * 1000,
-        moved=10000,
-    )
-    meta = lax.all_to_all(asked, "tile", split_axis=0, concat_axis=0, tiled=True)
-
-    own_basis = basis.reshape(-1, NY)
-    others = [around(own_basis, "probe", d) for d in (1, 2, 3)]
+        moved=400000,
+        vmem=VMEM_PREP,
+    )
+    swap_a = swap(packed, "tile", 1)
+    swap_b = swap(packed, "tile", 1, 1)
+    far_c = swap(edge_c, "tile", 2)
+    far_d = swap(edge_d, "tile", 2, 2)
+    asked, swap_a, swap_b, far_c, far_d = lax.optimization_barrier(
+        (asked, swap_a, swap_b, far_c, far_d)
+    )
+    n_basis = 4 * basis.shape[0]
+    panel_high, panel_low, request = call(
+        gram_kernel,
+        [sds((n_basis, cells), bf16), sds((n_basis, cells), bf16), sds((TILES * 4, 128))],
+        [me, own_basis, *others, asked],
+        scalars=1,
+        flops=20 * 10**9,
+        moved=1500000,
+    )
+
+    def exchange(value):
+        return lax.all_to_all(
+            value.reshape(TILES, 4, 128), "tile", split_axis=0, concat_axis=0, tiled=True
+        ).reshape(TILES * 4, 128)
+
+    meta = exchange(request)
+    precision_parts = call(
+        split_kernel,
+        [sds(obs_precision.shape, bf16), sds(obs_precision.shape, bf16)],
+        [obs_precision],
+        flops=2 * 10**9,
+        moved=2000000,
+    )
+    precision_parts, meta = lax.optimization_barrier((precision_parts, meta))
 
     field = pltpu.VMEM((ROWS, 2, NZ, KD, NY), f32)
     load = pltpu.VMEM((ROWS, 2, KD, NY), f32)
     surface, coef, gain = call(
         state_kernel,
         [sds((2, CX, KD, NY)), sds((N_COEF, ROWS, NZ, NY)), sds((2, CX, NY))],
-        [packed, left, right, far_left, far_right],
+        [at, packed, swap_a, swap_b, far_c, far_d],
+        scalars=1,
         scratch=[
             pltpu.VMEM((ROWS + 2, NZ, NY), f32),
             pltpu.VMEM((ROWS, NZ, NY), f32),
@@ -501,79 +648,73 @@
         flops=40 * 16 * 44 * 1024,
         moved=2000000,
     )
-    n_basis = 4 * basis.shape[0]
-    panel_high, panel_low, gram_part = call(
-        gram_kernel,
-        [sds((n_basis, cells), bf16), sds((n_basis, cells), bf16), sds((TILES, n_basis))],
-        [me, own_basis, *others],
-        scalars=1,
-        flops=6 * 64 * 512 * 256,
-        moved=1500000,
-    )
     payload = call(
         gather_kernel,
         sds((TILES * 4, 128)),
-        [meta, surface, gram_part],
+        [meta, surface],
         flops=2 * 48 * 512 * 1024,
         moved=300000,
     )
-
-    def exchange(value):
-        return lax.all_to_all(
-            value.reshape(TILES, 4, 128), "tile", split_axis=0, concat_axis=0, tiled=True
-        ).reshape(TILES * 4, 128)
-
     arrived = exchange(payload)
+    quarters = [swap(arrived, "probe", d) for d in (1, 2, 3)]
     outgoing = call(
         precision_kernel,
         sds((TILES * 4, 128)),
-        [arrived, tile_row, rank, obs_precision],
-        flops=2 * 512 * 512 * 64,
+        [arrived, packed, *precision_parts],
+        flops=20 * 10**9,
         moved=1500000,
     )
+    outgoing, *quarters = lax.optimization_barrier((outgoing, *quarters))
     returned = exchange(outgoing)
-    top, gram_rows = call(
-        scatter_kernel,
-        [sds((2 * KD, cells)), sds((TILES, n_basis))],
-        [returned, meta],
-        flops=2 * 48 * 512 * 1024,
-        moved=300000,
-    )
-    top_left = along(top, "tile", 1)
-    top_right = along(top, "tile", -1)
-    quarters = [around(gram_rows, "probe", d) for d in (1, 2, 3)]
+    matrix = call(
+        first_kernel,
+        sds((n_basis, n_basis)),
+        [me, arrived, *quarters],
+        scalars=1,
+        flops=12 * 64 * 256 * 256,
+        moved=500000,
+    )
+    number = 1
+
+    def invert(matrix, pieces):
+        nonlocal number
+        for _ in range(pieces):
+            matrix = call(
+                functools.partial(next_kernel, number),
+                sds((n_basis, n_basis)),
+                [matrix],
+                flops=12 * 64 * 256 * 256,
+                moved=500000,
+            )
+            number += 1
+        return matrix
+
+    matrix = invert(matrix, PIECES[0])
+    returned, matrix = lax.optimization_barrier((returned, matrix))
     hessian, moments = call(
         adjoint_kernel,
         [sds((CX, KD, NY)), sds((KD, n_basis))],
-        [top, top_left, top_right, coef, gain, panel_high, panel_low],
+        [returned, meta, coef, gain, panel_high, panel_low],
         scratch=[load, field, field],
         flops=40 * 16 * 44 * 1024,
         moved=2000000,
     )
-    matrix = call(
-        first_kernel,
-        sds((n_basis, n_basis)),
-        [me, gram_rows, *quarters],
-        scalars=1,
-        flops=12 * 64 * 256 * 256,
-        moved=500000,
-    )
-    for number in range(1, n_basis // BLOCK):
-        matrix = call(
-            functools.partial(next_kernel, number),
-            sds((n_basis, n_basis)),
-            [matrix],
-            flops=12 * 64 * 256 * 256,
-            moved=500000,
-        )
-    step = 1
-    while step < TILES:
-        moments = moments + lax.ppermute(moments, "tile", [(i, i ^ step) for i in range(TILES)])
-        step *= 2
+    moments, matrix = lax.optimization_barrier((moments, matrix))
+    moments = moments + swap(moments, "tile", 1)
+    half = TILES // 2
+    parts = lax.all_to_all(
+        jnp.broadcast_to(moments[None], (half, KD, n_basis)),
+        "tile",
+        split_axis=0,
+        concat_axis=0,
+        tiled=True,
+        axis_index_groups=[list(range(core, TILES, 2)) for core in range(2)],
+    )
+    matrix = invert(matrix, PIECES[1])
     filtered, coefficients = call(
         final_kernel,
         [sds((CX, KD, NY)), sds((KD, n_basis))],
-        [moments, matrix, panel_high, panel_low, hessian],
+        [parts, matrix, panel_high, panel_low, hessian],
         flops=12 * 8 * 256 * 512,
         moved=800000,
     )

time: 145 us -> 116 us (0.80)
  blocking collectives: 35.2 us -> 16.8 us
  waiting for transfers between devices: 9.11 us -> 22 us
  starting transfers between devices: 50 us -> 39.7 us
  Pallas kernels: 41.8 us -> 31.8 us
  local copies, waits for them, and re-layouts: 7.21 us -> 4.23 us
    ppermute x18 -> x11, starting transfers between devices: 34.6 us -> 15.1 us  [swap(): lax.ppermute(value, axis, [(i, j) for i, j in enumerate(partner) if 0 <=...]
    all_to_all x2 -> x1, blocking collectives: 35.2 us -> 16.8 us  [exchange(): lax.all_to_all(value.reshape(TILES, 4, 128), 'tile', split_axis=0, concat...]
    all_to_all x1 -> x3, waiting for transfers between devices: 0.9 us -> 14.5 us  [the longest x2 8.32 us: exchange(): lax.all_to_all(value.reshape(TILES, 4, 128), 'tile', split_axis=0, concat...]
    pallas_call x12 -> x16, Pallas kernels: 41.8 us -> 31.8 us  [call(): pl.pallas_call(kernel, out_shape=shapes, in_specs=places or [SM] * scalar...]
    all_to_all x1 -> x3, starting transfers between devices: 15.4 us -> 24.6 us  [the longest x2 19 us: exchange(): lax.all_to_all(value.reshape(TILES, 4, 128), 'tile', split_axis=0, concat...]
    concatenate x1 -> x0, local copies, waits for them, and re-layouts: 2.87 us -> none  [per_device(): jnp.concatenate([viscosity.reshape(CX * NZ, NY), probes.reshape(CX * KD,...]
    ppermute x18 -> x11, waiting for transfers between devices: 8.21 us -> 7.45 us  [swap(): lax.ppermute(value, axis, [(i, j) for i, j in enumerate(partner) if 0 <=...]
  transfers between devices with their start and end apart: 19 -> 14, of which waited for: 5 -> 9; matrix products, arithmetic and copies ran while one was open for 2% -> 0% of each run, Pallas kernels for 27% -> 20%
where the time goes in v2:
time: 116 us; the launch traced here: 115 us
  starting transfers between devices  39.7 us (34%)
  Pallas kernels  31.8 us (27%)
  waiting for transfers between devices  22 us (19%)
  blocking collectives  16.8 us (14%)
  local copies, waits for them, and re-layouts  4.23 us (4%)
    pallas_call x16, Pallas kernels, call(): pl.pallas_call(kernel, out_shape=shapes, in_specs=places or [SM] * scalar...  31.8 us
    all_to_all x2, starting transfers between devices, exchange(): lax.all_to_all(value.reshape(TILES, 4, 128), 'tile', split_axis=0, concat...  19 us
    all_to_all x1, blocking collectives, exchange(): lax.all_to_all(value.reshape(TILES, 4, 128), 'tile', split_axis=0, concat...  16.8 us
    ppermute x11, starting transfers between devices, swap(): lax.ppermute(value, axis, [(i, j) for i, j in enumerate(partner) if 0 <=...  15.1 us
    all_to_all x2, waiting for transfers between devices, exchange(): lax.all_to_all(value.reshape(TILES, 4, 128), 'tile', split_axis=0, concat...  8.32 us
    ppermute x11, waiting for transfers between devices, swap(): lax.ppermute(value, axis, [(i, j) for i, j in enumerate(partner) if 0 <=...  7.45 us
    all_to_all x1, waiting for transfers between devices, per_device(): lax.all_to_all(jnp.broadcast_to(moments[None], (half, KD, n_basis)), 'til...  6.23 us
    all_to_all x1, starting transfers between devices, per_device(): lax.all_to_all(jnp.broadcast_to(moments[None], (half, KD, n_basis)), 'til...  5.6 us
  transfers between devices with their start and end apart: 14, of which 9 were waited for; matrix products, arithmetic and copies ran while one was open for 0% of the time, Pallas kernels for 20%

profile of v2, /device:TPU:2, one launch (start us, length us, event | category | flops | bytes accessed | tf_op | source)
XLA Modules:
  0.0 115.2 jit_solution(753368260971679662)
XLA Ops:
  0.6 1.6 %collective-permute-start.2 = (f32[256,128]{1,0:T(8,128)}, f32[256,128]{1,0:T(8,128)S(1)}, u32[]{:S(2)}, u32[]{:S(2)}) collective-permute-start(f32[256,128]{1,0:T(8,128)} %bitcast.23), channel_id=1, source_target_pairs={{0,3},{1,2},{2,1},{3,0},{4,7},{5,6},{6,5},{7,4},{8,11},{9,10},{10,... | collective-permute-start | bytes 393224 | tf_op jit(solution)/shard_map/ppermute | solution.py:559
  2.2 2.8 %collective-permute-start.1 = (f32[256,128]{1,0:T(8,128)}, f32[256,128]{1,0:T(8,128)S(1)}, u32[]{:S(2)}, u32[]{:S(2)}) collective-permute-start(f32[256,128]{1,0:T(8,128)} %bitcast.24), channel_id=1, source_target_pairs={{0,2},{1,3},{2,0},{3,1},{4,6},{5,7},{6,4},{7,5},{8,10},{9,11},{10,... | collective-permute-start | bytes 393224 | tf_op jit(solution)/shard_map/ppermute | solution.py:559
  5.1 2.0 %shard_map.105 = (f32[120,128]{1,0:T(8,128)}, f32[16,128]{1,0:T(8,128)}, f32[16,128]{1,0:T(8,128)}, f32[64,128]{1,0:T(8,128)}) custom-call(s32[1]{0:T(128)} %bitcast.2.at_ref, f32[64,128]{1,0:T(8,128)} %bitcast.27, f32[32,128]{1,0:T(8,128)} %bitcast.28, f32[8,128]{1,0:T(8,128)} %bitcast.29, f32[4,128]{1,0:T(4,128)} %fric.1, s32[1,512]{1,0:T(1,128)} %bitcast.30, ...), custom_call_target="tpu_custom_call" | custom-call | flops 65536000 | bytes 400000 | tf_op jit(solution)/shard_map/pallas_call | solution.py:39
  7.1 1.4 %collective-permute-start.5 = (f32[16,128]{1,0:T(8,128)}, f32[16,128]{1,0:T(8,128)S(1)}, u32[]{:S(2)}, u32[]{:S(2)}) collective-permute-start(f32[16,128]{1,0:T(8,128)} %get-tuple-element.36), channel_id=1, source_target_pairs={{0,8},{4,12},{8,0},{12,4},{16,24},{20,28},{24,16},{28,20},{32,40},... | collective-permute-start | bytes 24584 | tf_op jit(solution)/shard_map/ppermute | solution.py:559
  8.5 0.6 collective-permute-start.6
  9.2 1.9 %collective-permute-done.5.edge_c = f32[16,128]{1,0:T(8,128)S(1)} collective-permute-done((f32[16,128]{1,0:T(8,128)}, f32[16,128]{1,0:T(8,128)S(1)}, u32[]{:S(2)}, u32[]{:S(2)}) %collective-permute-start.5) | collective-permute-done | bytes 8224 | tf_op jit(solution)/shard_map/ppermute | solution.py:559
  11.1 0.7 collective-permute-start.4
  11.7 0.0 collective-permute-done.6.edge_d
  11.7 3.7 %collective-permute-start.3 = (f32[120,128]{1,0:T(8,128)}, f32[120,128]{1,0:T(8,128)S(1)}, u32[]{:S(2)}, u32[]{:S(2)}) collective-permute-start(f32[120,128]{1,0:T(8,128)} %get-tuple-element.35.own.packed), channel_id=1, source_target_pairs={{0,4},{4,0},{8,12},{12,8},{16,20},{20,16},{24,28},{28,24},{32,36},... | collective-permute-start | bytes 184328 | tf_op jit(solution)/shard_map/ppermute | solution.py:559
  15.4 1.1 collective-permute-done.3.swap_a
  16.5 0.0 collective-permute-done.2.back
  16.5 0.0 collective-permute-done.1.across
  16.5 0.0 copy-start.2
  16.6 0.9 copy-done.2
  17.5 0.8 copy-done.3
  18.2 1.1 shard_map.106
  19.3 14.2 %all-to-all-start = ((f32[64,4,128]{2,1,0:T(4,128)}), f32[64,4,128]{2,1,0:T(4,128)S(1)}, u32[]{:S(2)}, u32[]{:S(2)}) async-start(f32[64,4,128]{2,1,0:T(4,128)} %bitcast.8), calls=%async_computation | async-start | bytes 262144 | tf_op jit(solution)/shard_map/all_to_all | solution.py:619
  33.5 0.1 shard_map.104
  33.7 0.8 copy-done.4
  34.5 5.7 %shard_map.107 = (f32[2,4,8,128]{3,2,1,0:T(8,128)S(1)}, f32[13,12,16,128]{3,2,1,0:T(8,128)S(1)}, f32[2,4,128]{2,1,0:T(4,128)S(1)}) custom-call(s32[1]{0:T(128)} %bitcast.2.at_ref, f32[120,128]{1,0:T(8,128)S(1)} %copy-done, f32[120,128]{1,0:T(8,128)S(1)} %collective-permute-done.3.swap_a, f32[120,128]{1,0:T(8,128)S(1)} %collective-permute-done.4.swap_b, ...), custom_call_target="tpu_custom_call" | custom-call | flops 28835840 | bytes 2000000 | tf_op jit(solution)/shard_map/pallas_call | solution.py:39
  40.2 4.4 %all-to-all-done = f32[64,4,128]{2,1,0:T(4,128)S(1)} async-done(((f32[64,4,128]{2,1,0:T(4,128)}), f32[64,4,128]{2,1,0:T(4,128)S(1)}, u32[]{:S(2)}, u32[]{:S(2)}) %all-to-all-start) | async-done | bytes 131104 | tf_op jit(solution)/shard_map/all_to_all | solution.py:619
  44.6 0.6 shard_map.108
  45.2 16.8 %all_to_all.20 = f32[64,4,128]{2,1,0:T(4,128)S(1)} all-to-all(f32[64,4,128]{2,1,0:T(4,128)S(1)} %bitcast.17), channel_id=1, replica_groups=mesh['tile'=64,'probe'=4] {'tile'}, dimensions={0} | all-to-all | bytes 262144 | tf_op jit(solution)/shard_map/all_to_all | solution.py:619
  61.9 1.5 %collective-permute-start.9 = (f32[256,128]{1,0:T(8,128)S(1)}, f32[256,128]{1,0:T(8,128)S(1)}, u32[]{:S(2)}, u32[]{:S(2)}) collective-permute-start(f32[256,128]{1,0:T(8,128)S(1)} %bitcast.18), channel_id=1, source_target_pairs={{0,3},{1,2},{2,1},{3,0},{4,7},{5,6},{6,5},{7,4},{8,11},{9,10},{10,... | collective-permute-start | bytes 393224 | tf_op jit(solution)/shard_map/ppermute | solution.py:559
  63.4 1.1 collective-permute-start.8
  64.5 1.5 %collective-permute-start.7 = (f32[256,128]{1,0:T(8,128)S(1)}, f32[256,128]{1,0:T(8,128)S(1)}, u32[]{:S(2)}, u32[]{:S(2)}) collective-permute-start(f32[256,128]{1,0:T(8,128)S(1)} %bitcast.20), channel_id=1, source_target_pairs={{0,1},{1,0},{2,3},{3,2},{4,5},{5,4},{6,7},{7,6},{8,9},{9,8},{10,11... | collective-permute-start | bytes 393224 | tf_op jit(solution)/shard_map/ppermute | solution.py:559
  66.0 1.0 copy-done.5
  67.0 1.6 %shard_map.109 = f32[256,128]{1,0:T(8,128)} custom-call(f32[256,128]{1,0:T(8,128)S(1)} %bitcast.21, f32[120,128]{1,0:T(8,128)S(1)} %copy-done, bf16[512,512]{1,0:T(8,128)(2,1)S(1)} %get-tuple-element.46.precision_high, bf16[512,512]{1,0:T(8,128)(2,1)S(1)} %copy-done.5), custom_call_target="tpu_custom_call" | custom-call | flops 20000000000 | bytes 1500000 | tf_op jit(solution)/shard_map/pallas_call | solution.py:39
  68.7 0.3 collective-permute-done.9.back
  69.0 2.3 %collective-permute-done.8.across = f32[256,128]{1,0:T(8,128)S(1)} collective-permute-done((f32[256,128]{1,0:T(8,128)S(1)}, f32[256,128]{1,0:T(8,128)S(1)}, u32[]{:S(2)}, u32[]{:S(2)}) %collective-permute-start.8) | collective-permute-done | bytes 131104 | tf_op jit(solution)/shard_map/ppermute | solution.py:559
  71.3 0.8 collective-permute-done.7.near
  72.1 4.8 %all-to-all-start.2 = ((f32[64,4,128]{2,1,0:T(4,128)}), f32[64,4,128]{2,1,0:T(4,128)S(1)}, u32[]{:S(2)}, u32[]{:S(2)}) async-start(f32[64,4,128]{2,1,0:T(4,128)} %bitcast.12), calls=%async_computation.2 | async-start | bytes 262144 | tf_op jit(solution)/shard_map/all_to_all | solution.py:619
  76.9 1.8 %shard_map.110.before = f32[256,256]{1,0:T(8,128)S(1)} custom-call(s32[1]{0:T(128)} %bitcast.me_ref, f32[256,128]{1,0:T(8,128)S(1)} %bitcast.22, f32[256,128]{1,0:T(8,128)S(1)} %collective-permute-done.7.near, f32[256,128]{1,0:T(8,128)S(1)} %collective-permute-done.8.across, f32[256,128]{1,0:T(8,128)S(1)} %collective-permute-done.9.back), custom_call_target="tpu_custom_call" | custom-call | flops 50331648 | bytes 500000 | tf_op jit(solution)/shard_map/pallas_call | solution.py:39
  78.7 1.8 %shard_map.111.before = f32[256,256]{1,0:T(8,128)S(1)} custom-call(f32[256,256]{1,0:T(8,128)S(1)} %shard_map.110.before), custom_call_target="tpu_custom_call" | custom-call | flops 50331648 | bytes 500000 | tf_op jit(solution)/shard_map/pallas_call | solution.py:39
  80.4 1.8 %shard_map.112.before = f32[256,256]{1,0:T(8,128)S(1)} custom-call(f32[256,256]{1,0:T(8,128)S(1)} %shard_map.111.before), custom_call_target="tpu_custom_call" | custom-call | flops 50331648 | bytes 500000 | tf_op jit(solution)/shard_map/pallas_call | solution.py:39
  82.2 1.8 %shard_map.113.before = f32[256,256]{1,0:T(8,128)S(1)} custom-call(f32[256,256]{1,0:T(8,128)S(1)} %shard_map.112.before), custom_call_target="tpu_custom_call" | custom-call | flops 50331648 | bytes 500000 | tf_op jit(solution)/shard_map/pallas_call | solution.py:39
  83.9 3.9 %all-to-all-done.2 = f32[64,4,128]{2,1,0:T(4,128)S(1)} async-done(((f32[64,4,128]{2,1,0:T(4,128)}), f32[64,4,128]{2,1,0:T(4,128)S(1)}, u32[]{:S(2)}, u32[]{:S(2)}) %all-to-all-start.2) | async-done | bytes 131104 | tf_op jit(solution)/shard_map/all_to_all | solution.py:619
  87.9 5.3 %shard_map.114 = (f32[4,8,128]{2,1,0:T(8,128)S(1)}, f32[8,256]{1,0:T(8,128)S(1)}) custom-call(f32[256,128]{1,0:T(8,128)S(1)} %bitcast.16, f32[256,128]{1,0:T(8,128)S(1)} %bitcast.15, f32[13,12,16,128]{3,2,1,0:T(8,128)S(1)} %get-tuple-element.53.coef, f32[2,4,128]{2,1,0:T(4,128)S(1)} %get-tuple-element.54.gain, ...), custom_call_target="tpu_custom_call" | custom-call | flops 28835840 | bytes 2000000 | tf_op jit(solution)/shard_map/pallas_call | solution.py:39
  93.2 0.1 collective-permute-start.10
  93.3 1.1 collective-permute-done.10
  94.4 0.7 broadcast_in_dim.2
  95.1 5.6 %all-to-all-start.3 = ((f32[32,8,256]{2,1,0:T(8,128)}), f32[32,8,256]{2,1,0:T(8,128)S(1)}, u32[]{:S(2)}, u32[]{:S(2)}) async-start(f32[32,8,256]{2,1,0:T(8,128)} %broadcast_in_dim.2), calls=%async_computation.3 | async-start | bytes 524288 | tf_op jit(solution)/shard_map/all_to_all | solution.py:705
  100.7 1.8 %shard_map.115.before = f32[256,256]{1,0:T(8,128)S(1)} custom-call(f32[256,256]{1,0:T(8,128)S(1)} %shard_map.113.before), custom_call_target="tpu_custom_call" | custom-call | flops 50331648 | bytes 500000 | tf_op jit(solution)/shard_map/pallas_call | solution.py:39
  102.5 1.7 %shard_map.116.before = f32[256,256]{1,0:T(8,128)S(1)} custom-call(f32[256,256]{1,0:T(8,128)S(1)} %shard_map.115.before), custom_call_target="tpu_custom_call" | custom-call | flops 50331648 | bytes 500000 | tf_op jit(solution)/shard_map/pallas_call | solution.py:39
  104.3 1.8 %shard_map.117.before = f32[256,256]{1,0:T(8,128)S(1)} custom-call(f32[256,256]{1,0:T(8,128)S(1)} %shard_map.116.before), custom_call_target="tpu_custom_call" | custom-call | flops 50331648 | bytes 500000 | tf_op jit(solution)/shard_map/pallas_call | solution.py:39
  106.0 1.7 %shard_map.118.inverse = f32[256,256]{1,0:T(8,128)S(1)} custom-call(f32[256,256]{1,0:T(8,128)S(1)} %shard_map.117.before), custom_call_target="tpu_custom_call" | custom-call | flops 50331648 | bytes 500000 | tf_op jit(solution)/shard_map/pallas_call | solution.py:39
  107.8 6.2 %all-to-all-done.3.parts = f32[32,8,256]{2,1,0:T(8,128)S(1)} async-done(((f32[32,8,256]{2,1,0:T(8,128)}), f32[32,8,256]{2,1,0:T(8,128)S(1)}, u32[]{:S(2)}, u32[]{:S(2)}) %all-to-all-start.3) | async-done | bytes 262176 | tf_op jit(solution)/shard_map/all_to_all | solution.py:705
  114.0 1.2 %shard_map.119 = (f32[4,8,128]{2,1,0:T(8,128)}, f32[8,256]{1,0:T(8,128)}) custom-call(f32[32,8,256]{2,1,0:T(8,128)S(1)} %all-to-all-done.3.parts, f32[256,256]{1,0:T(8,128)S(1)} %shard_map.118.inverse, bf16[256,512]{1,0:T(8,128)(2,1)S(1)} %get-tuple-element.55.panel_high, bf16[256,512]{1,0:T(8,128)(2,1)S(1)} %get-tuple-element.56.panel_low, ...), custom_call_target="tpu_custom_call" | custom-call | flops 12582912 | bytes 800000 | tf_op jit(solution)/shard_map/pallas_call | solution.py:39
  (11 shorter events, 0.0 us)
Async XLA Ops:
  0.6 15.9 %collective-permute-start.2 = (f32[256,128]{1,0:T(8,128)}, f32[256,128]{1,0:T(8,128)S(1)}, u32[]{:S(2)}, u32[]{:S(2)}) collective-permute-start(f32[256,128]{1,0:T(8,128)} %bitcast.23), channel_id=1, source_target_pairs={{0,3},{1,2},{2,1},{3,0},{4,7},{5,6},{6,5},{7,4},{8,11},{9,10},{10,... | collective-permute-start | bytes 393224 | tf_op jit(solution)/shard_map/ppermute | solution.py:559
  2.2 14.3 %collective-permute-start.1 = (f32[256,128]{1,0:T(8,128)}, f32[256,128]{1,0:T(8,128)S(1)}, u32[]{:S(2)}, u32[]{:S(2)}) collective-permute-start(f32[256,128]{1,0:T(8,128)} %bitcast.24), channel_id=1, source_target_pairs={{0,2},{1,3},{2,0},{3,1},{4,6},{5,7},{6,4},{7,5},{8,10},{9,11},{10,... | collective-permute-start | bytes 393224 | tf_op jit(solution)/shard_map/ppermute | solution.py:559
  5.1 11.5 %collective-permute-start = (f32[256,128]{1,0:T(8,128)}, f32[256,128]{1,0:T(8,128)S(1)}, u32[]{:S(2)}, u32[]{:S(2)}) collective-permute-start(f32[256,128]{1,0:T(8,128)} %bitcast.25), channel_id=1, source_target_pairs={{0,1},{1,0},{2,3},{3,2},{4,5},{5,4},{6,7},{7,6},{8,9},{9,8},{10,11... | collective-permute-start | bytes 393224 | tf_op jit(solution)/shard_map/ppermute | solution.py:559
  7.1 3.9 %collective-permute-start.5 = (f32[16,128]{1,0:T(8,128)}, f32[16,128]{1,0:T(8,128)S(1)}, u32[]{:S(2)}, u32[]{:S(2)}) collective-permute-start(f32[16,128]{1,0:T(8,128)} %get-tuple-element.36), channel_id=1, source_target_pairs={{0,8},{4,12},{8,0},{12,4},{16,24},{20,28},{24,16},{28,20},{32,40},... | collective-permute-start | bytes 24584 | tf_op jit(solution)/shard_map/ppermute | solution.py:559
  8.5 3.2 %collective-permute-start.6 = (f32[16,128]{1,0:T(8,128)}, f32[16,128]{1,0:T(8,128)S(1)}, u32[]{:S(2)}, u32[]{:S(2)}) collective-permute-start(f32[16,128]{1,0:T(8,128)} %get-tuple-element.37), channel_id=1, source_target_pairs={{8,16},{12,20},{16,8},{20,12},{24,32},{28,36},{32,24},{36,28},{40,... | collective-permute-start | bytes 24584 | tf_op jit(solution)/shard_map/ppermute | solution.py:559
  11.1 4.4 %collective-permute-start.4 = (f32[120,128]{1,0:T(8,128)}, f32[120,128]{1,0:T(8,128)S(1)}, u32[]{:S(2)}, u32[]{:S(2)}) collective-permute-start(f32[120,128]{1,0:T(8,128)} %get-tuple-element.35.own.packed), channel_id=1, source_target_pairs={{4,8},{8,4},{12,16},{16,12},{20,24},{24,20},{28,32},{32,28},{36,40... | collective-permute-start | bytes 184328 | tf_op jit(solution)/shard_map/ppermute | solution.py:559
  11.7 4.8 %collective-permute-start.3 = (f32[120,128]{1,0:T(8,128)}, f32[120,128]{1,0:T(8,128)S(1)}, u32[]{:S(2)}, u32[]{:S(2)}) collective-permute-start(f32[120,128]{1,0:T(8,128)} %get-tuple-element.35.own.packed), channel_id=1, source_target_pairs={{0,4},{4,0},{8,12},{12,8},{16,20},{20,16},{24,28},{28,24},{32,36},... | collective-permute-start | bytes 184328 | tf_op jit(solution)/shard_map/ppermute | solution.py:559
  16.5 0.9 copy-start.2
  17.5 0.8 copy-start.3
  18.2 15.3 %copy-start.1 = (f32[512,512]{1,0:T(8,128)S(1)}, f32[512,512]{1,0:T(8,128)}, u32[]{:S(2)}) copy-start(f32[512,512]{1,0:T(8,128)} %precision.1) | copy-start | bytes 3145732
  19.3 25.2 %all-to-all-start = ((f32[64,4,128]{2,1,0:T(4,128)}), f32[64,4,128]{2,1,0:T(4,128)S(1)}, u32[]{:S(2)}, u32[]{:S(2)}) async-start(f32[64,4,128]{2,1,0:T(4,128)} %bitcast.8), calls=%async_computation | async-start | bytes 262144 | tf_op jit(solution)/shard_map/all_to_all | solution.py:619
  33.5 1.0 copy-start
  33.7 0.8 copy-start.4
  61.9 7.1 %collective-permute-start.9 = (f32[256,128]{1,0:T(8,128)S(1)}, f32[256,128]{1,0:T(8,128)S(1)}, u32[]{:S(2)}, u32[]{:S(2)}) collective-permute-start(f32[256,128]{1,0:T(8,128)S(1)} %bitcast.18), channel_id=1, source_target_pairs={{0,3},{1,2},{2,1},{3,0},{4,7},{5,6},{6,5},{7,4},{8,11},{9,10},{10,... | collective-permute-start | bytes 393224 | tf_op jit(solution)/shard_map/ppermute | solution.py:559
  63.4 7.9 %collective-permute-start.8 = (f32[256,128]{1,0:T(8,128)S(1)}, f32[256,128]{1,0:T(8,128)S(1)}, u32[]{:S(2)}, u32[]{:S(2)}) collective-permute-start(f32[256,128]{1,0:T(8,128)S(1)} %bitcast.19), channel_id=1, source_target_pairs={{0,2},{1,3},{2,0},{3,1},{4,6},{5,7},{6,4},{7,5},{8,10},{9,11},{10,... | collective-permute-start | bytes 393224 | tf_op jit(solution)/shard_map/ppermute | solution.py:559
  64.5 7.6 %collective-permute-start.7 = (f32[256,128]{1,0:T(8,128)S(1)}, f32[256,128]{1,0:T(8,128)S(1)}, u32[]{:S(2)}, u32[]{:S(2)}) collective-permute-start(f32[256,128]{1,0:T(8,128)S(1)} %bitcast.20), channel_id=1, source_target_pairs={{0,1},{1,0},{2,3},{3,2},{4,5},{5,4},{6,7},{7,6},{8,9},{9,8},{10,11... | collective-permute-start | bytes 393224 | tf_op jit(solution)/shard_map/ppermute | solution.py:559
  66.0 1.0 copy-start.5
  72.1 15.8 %all-to-all-start.2 = ((f32[64,4,128]{2,1,0:T(4,128)}), f32[64,4,128]{2,1,0:T(4,128)S(1)}, u32[]{:S(2)}, u32[]{:S(2)}) async-start(f32[64,4,128]{2,1,0:T(4,128)} %bitcast.12), calls=%async_computation.2 | async-start | bytes 262144 | tf_op jit(solution)/shard_map/all_to_all | solution.py:619
  93.2 1.2 %collective-permute-start.10 = (f32[8,256]{1,0:T(8,128)S(1)}, f32[8,256]{1,0:T(8,128)S(1)}, u32[]{:S(2)}, u32[]{:S(2)}) collective-permute-start(f32[8,256]{1,0:T(8,128)S(1)} %get-tuple-element.59), channel_id=1, source_target_pairs={{0,4},{4,0},{8,12},{12,8},{16,20},{20,16},{24,28},{28,24},{32,36},... | collective-permute-start | bytes 24584 | tf_op jit(solution)/shard_map/ppermute | solution.py:559
  95.1 18.9 %all-to-all-start.3 = ((f32[32,8,256]{2,1,0:T(8,128)}), f32[32,8,256]{2,1,0:T(8,128)S(1)}, u32[]{:S(2)}, u32[]{:S(2)}) async-start(f32[32,8,256]{2,1,0:T(8,128)} %broadcast_in_dim.2), calls=%async_computation.3 | async-start | bytes 524288 | tf_op jit(solution)/shard_map/all_to_all | solution.py:705

commit v3 on v2

--- a/solution.py
+++ b/solution.py
@@ -13,6 +13,7 @@
 NZ = 16
 KD = 8
 CAP = 16
+HALF = 128
 TILES = 64
 ROWS = CX * 3
 ASPECT = 1024.0
@@ -21,7 +22,7 @@
 BLOCK = 32
 VMEM_PREP = 60
 PIVOTS = 4
-PIECES = (3, 4)
+PIECES = (3, 3)
 V_AT, P_AT, B_AT, F_AT = 0, CX * NZ, CX * (NZ + KD), CX * (NZ + KD + 2)
 T_AT, R_AT, PACK = F_AT + CX, F_AT + 8, F_AT + 16
 f32 = jnp.float32
@@ -305,8 +306,8 @@
 def adjoint_kernel(
     returned, meta, coef, gain, panel_high, panel_low, hessian, moments, load, field_a, field_b
 ):
-    beside = meta[pl.ds(3, TILES, stride=4), :]
-    metas = (beside, meta[pl.ds(0, TILES, stride=4), :], pltpu.roll(beside, TILES, 1))
+    beside = meta[:, 1, :]
+    metas = (beside, meta[:, 0, :], pltpu.roll(beside, TILES, 1))
     for part, k in enumerate((1, 0, 2)):
         top = top_load(returned[pl.ds(k, TILES, stride=4), :], metas[part])
         for x in range(CX):
@@ -327,29 +328,32 @@
     return jnp.where(iota(value.shape, 0) == edge, 0.0, moved)
 
 
-def gram_kernel(me_ref, own, near, across, back, asked, panel_high, panel_low, payload):
+def gram_kernel(
+    me_ref, own, near, across, back, asked, panel_high, panel_low, payload, gram_11, gram_12, gram_22
+):
     me = me_ref[0]
     count = own.shape[0] // CX
-    mine = None
     for shift, block in enumerate((own, near, across, back)):
         source = me ^ shift
         flat = jnp.concatenate(
             [block[pl.ds(x, count, stride=CX), :] for x in range(CX)], axis=1
         )
-        high, low = split2(flat)
-        if shift == 0:
-            mine = (high, low)
         at = pl.ds(pl.multiple_of(source * count, count), count)
-        panel_high[at, :] = high
-        panel_low[at, :] = low
-    part = dot3(mine, (panel_high[...], panel_low[...]), NT)
+        panel_high[at, :], panel_low[at, :] = split2(flat)
+    upper = panel_high[0:HALF, :], panel_low[0:HALF, :]
+    lower = panel_high[HALF:, :], panel_low[HALF:, :]
+    gram_11[...] = dot3(upper, upper, NT)
+    gram_12[...] = dot3(upper, lower, NT)
+    gram_22[...] = dot3(lower, lower, NT)
     here = asked[...]
-    payload[pl.ds(0, TILES, stride=4), :] = here
-    payload[pl.ds(1, TILES, stride=4), :] = part[:, 0:128]
-    payload[pl.ds(2, TILES, stride=4), :] = part[:, 128:256]
-    payload[pl.ds(3, TILES, stride=4), :] = from_tile(here, -1) + pltpu.roll(
-        from_tile(here, 1), TILES, 1
-    )
+    payload[:, 0, :] = here
+    payload[:, 1, :] = from_tile(here, -1) + pltpu.roll(from_tile(here, 1), TILES, 1)
+    for k, n, block in gram_lines(gram_11, gram_12, gram_22):
+        payload[:, k, :] = block[pl.ds(n, TILES, stride=2), :]
+
+
+def gram_lines(gram_11, gram_12, gram_22):
+    return (2, 0, gram_11), (3, 0, gram_12), (4, 1, gram_11), (5, 1, gram_12), (6, 0, gram_22), (7, 1, gram_22)
 
 
 def small_inverse(p):
@@ -439,12 +443,13 @@
     matrix[at, :] = rows
 
 
-def first_kernel(me_ref, own, near, across, back, matrix):
-    me = me_ref[0]
-    for shift, block in enumerate((own, near, across, back)):
-        at = pl.ds(pl.multiple_of((me ^ shift) * TILES, TILES), TILES)
-        matrix[at, 0:128] = block[pl.ds(1, TILES, stride=4), :]
-        matrix[at, 128:256] = block[pl.ds(2, TILES, stride=4), :]
+def first_kernel(arrived, matrix, gram_11, gram_12, gram_22):
+    for k, n, block in gram_lines(gram_11, gram_12, gram_22):
+        block[pl.ds(n, TILES, stride=2), :] = arrived[:, k, :]
+    matrix[0:HALF, 0:HALF] = gram_11[...]
+    matrix[0:HALF, HALF:] = gram_12[...]
+    matrix[HALF:, 0:HALF] = jnp.transpose(gram_12[...])
+    matrix[HALF:, HALF:] = gram_22[...]
     eliminate(matrix, 0)
 
 
@@ -473,7 +478,7 @@
 
 
 def gather_kernel(meta, surface, payload):
-    cells, sight_u, sight_v = slot_rows(meta[pl.ds(0, TILES, stride=4), :])
+    cells, sight_u, sight_v = slot_rows(meta[:, 0, :])
     one_hot = slot_one_hot(cells)
     both = jnp.concatenate(
         [jnp.concatenate([surface[m, x] for x in range(CX)], axis=1) for m in range(2)], axis=0
@@ -489,11 +494,8 @@
         )
     chunks.append(jnp.zeros((128 - TILES, 128), f32))
     turned = jnp.transpose(jnp.concatenate(chunks, axis=0))
-    payload[pl.ds(0, TILES, stride=4), :] = turned[0:TILES] + pltpu.roll(turned[TILES:], TILES, 1)
-    for k in (1, 2):
-        total = jnp.sum(meta[pl.ds(k, TILES, stride=4), :], axis=0, keepdims=True)
-        payload[pl.ds(k, TILES, stride=4), :] = jnp.broadcast_to(total, (TILES, 128))
-    payload[pl.ds(3, TILES, stride=4), :] = jnp.zeros((TILES, 128), f32)
+    payload[...] = jnp.broadcast_to(jnp.sum(meta[...], axis=0, keepdims=True), payload.shape)
+    payload[:, 0, :] = turned[0:TILES] + pltpu.roll(turned[TILES:], TILES, 1)
 
 
 def split_kernel(precision, high, low):
@@ -510,7 +512,7 @@
 
     one_hot = (iota((128, rows), 0) == line(T_AT)).astype(f32).astype(bf16)
     rank = line(R_AT)
-    mine = arrived[pl.ds(0, TILES, stride=4), :]
+    mine = arrived[:, 0, :]
     turned = jnp.transpose(jnp.concatenate([mine, jnp.zeros((128 - TILES, 128), f32)], axis=0))
     spread = [dot(part, one_hot, NN) for part in split3(turned)]
     spread = spread[0] + (spread[1] + spread[2])
@@ -545,10 +547,25 @@
     return parts[0:n] + (parts[n : 2 * n] + parts[2 * n : 3 * n])
 
 
-def final_kernel(parts, inverse, panel_high, panel_low, hessian, filtered, coefficients):
-    solved = dot_f32(jnp.sum(parts[...], axis=0), inverse[...])
-    coefficients[...] = solved
-    removed = dot3(split2(solved), (panel_high[...], panel_low[...]), NN)
+def copies_kernel(own, other, copies):
+    copies[...] = jnp.broadcast_to((own[...] + other[...])[None], copies.shape)
+
+
+def last_kernel(number, before, panel_high, panel_low, high, middle, low, spread_high, spread_low, matrix):
+    matrix[...] = before[...]
+    eliminate(matrix, number)
+    inverse = matrix[...]
+    high[...], middle[...], low[...] = split3(inverse)
+    spread = dot3(split2(inverse), (panel_high[...], panel_low[...]), NN)
+    spread_high[...], spread_low[...] = split2(spread)
+
+
+def final_kernel(parts, high, middle, low, spread_high, spread_low, hessian, filtered, coefficients):
+    a1, a2, a3 = split3(jnp.sum(parts[...], axis=0))
+    removed = dot3((a1, a2), (spread_high[...], spread_low[...]), NN)
+    b1, b2, b3 = high[...], middle[...], low[...]
+    small = dot(a1, b3, NN) + dot(a3, b1, NN) + dot(a2, b2, NN)
+    coefficients[...] = dot(a1, b1, NN) + ((dot(a1, b2, NN) + dot(a2, b1, NN)) + small)
     for x in range(CX):
         filtered[x] = hessian[x] - removed[:, x * NY : (x + 1) * NY]
 
@@ -602,23 +619,20 @@
     swap_b = swap(packed, "tile", 1, 1)
     far_c = swap(edge_c, "tile", 2)
     far_d = swap(edge_d, "tile", 2, 2)
-    asked, swap_a, swap_b, far_c, far_d = lax.optimization_barrier(
-        (asked, swap_a, swap_b, far_c, far_d)
-    )
+    asked, swap_b, far_d = lax.optimization_barrier((asked, swap_b, far_d))
     n_basis = 4 * basis.shape[0]
     panel_high, panel_low, request = call(
         gram_kernel,
-        [sds((n_basis, cells), bf16), sds((n_basis, cells), bf16), sds((TILES * 4, 128))],
+        [sds((n_basis, cells), bf16), sds((n_basis, cells), bf16), sds((TILES, 8, 128))],
         [me, own_basis, *others, asked],
+        scratch=[pltpu.VMEM((HALF, HALF), f32)] * 3,
         scalars=1,
         flops=20 * 10**9,
         moved=1500000,
     )
 
     def exchange(value):
-        return lax.all_to_all(
-            value.reshape(TILES, 4, 128), "tile", split_axis=0, concat_axis=0, tiled=True
-        ).reshape(TILES * 4, 128)
+        return lax.all_to_all(value, "tile", split_axis=0, concat_axis=0, tiled=True)
 
     meta = exchange(request)
     precision_parts = call(
@@ -650,13 +664,12 @@
     )
     payload = call(
         gather_kernel,
-        sds((TILES * 4, 128)),
+        sds((TILES, 8, 128)),
         [meta, surface],
         flops=2 * 48 * 512 * 1024,
         moved=300000,
     )
     arrived = exchange(payload)
-    quarters = [swap(arrived, "probe", d) for d in (1, 2, 3)]
     outgoing = call(
         precision_kernel,
         sds((TILES * 4, 128)),
@@ -664,13 +677,12 @@
         flops=20 * 10**9,
         moved=1500000,
     )
-    outgoing, *quarters = lax.optimization_barrier((outgoing, *quarters))
-    returned = exchange(outgoing)
+    returned = exchange(outgoing.reshape(TILES, 4, 128)).reshape(TILES * 4, 128)
     matrix = call(
         first_kernel,
         sds((n_basis, n_basis)),
-        [me, arrived, *quarters],
-        scalars=1,
+        [arrived],
+        scratch=[pltpu.VMEM((HALF, HALF), f32)] * 3,
         flops=12 * 64 * 256 * 256,
         moved=500000,
     )
@@ -700,10 +712,16 @@
         moved=2000000,
     )
     moments, matrix = lax.optimization_barrier((moments, matrix))
-    moments = moments + swap(moments, "tile", 1)
     half = TILES // 2
+    copies = call(
+        copies_kernel,
+        sds((half, KD, n_basis)),
+        [moments, swap(moments, "tile", 1)],
+        flops=half * KD * n_basis,
+        moved=4 * half * KD * n_basis,
+    )
     parts = lax.all_to_all(
-        jnp.broadcast_to(moments[None], (half, KD, n_basis)),
+        copies,
         "tile",
         split_axis=0,
         concat_axis=0,
@@ -711,10 +729,18 @@
         axis_index_groups=[list(range(core, TILES, 2)) for core in range(2)],
     )
     matrix = invert(matrix, PIECES[1])
+    inverse = call(
+        functools.partial(last_kernel, number),
+        [sds((n_basis, n_basis), bf16)] * 3 + [sds((n_basis, cells), bf16)] * 2,
+        [matrix, panel_high, panel_low],
+        scratch=[pltpu.VMEM((n_basis, n_basis), f32)],
+        flops=12 * 64 * 256 * 256 + 6 * 256 * 256 * 512,
+        moved=1500000,
+    )
     filtered, coefficients = call(
         final_kernel,
         [sds((CX, KD, NY)), sds((KD, n_basis))],
-        [parts, matrix, panel_high, panel_low, hessian],
+        [parts, *inverse, hessian],
         flops=12 * 8 * 256 * 512,
         moved=800000,
     )

time: 116 us -> 110 us (0.948)
  waiting for transfers between devices: 22 us -> 18.1 us
  starting transfers between devices: 39.7 us -> 36.4 us
  blocking collectives: 16.8 us -> 19.7 us
  local copies, waits for them, and re-layouts: 4.23 us -> 1.67 us
  Pallas kernels: 31.8 us -> 33.1 us
    ppermute x11 -> x8, starting transfers between devices: 15.1 us -> 7.72 us  [swap(): lax.ppermute(value, axis, [(i, j) for i, j in enumerate(partner) if 0 <=...]
    all_to_all x3, starting transfers between devices: 24.6 us -> 28.6 us  [the longest x2 22.9 us: exchange(): lax.all_to_all(value, 'tile', split_axis=0, concat_axis=0, tiled=True)]
    all_to_all x1, blocking collectives: 16.8 us -> 19.7 us  [exchange(): lax.all_to_all(value, 'tile', split_axis=0, concat_axis=0, tiled=True)]
    ppermute x11 -> x8, waiting for transfers between devices: 7.45 us -> 5.25 us  [swap(): lax.ppermute(value, axis, [(i, j) for i, j in enumerate(partner) if 0 <=...]
    unnamed x12 -> x10, local copies, waits for them, and re-layouts: 3.51 us -> 1.67 us
    all_to_all x3, waiting for transfers between devices: 14.5 us -> 12.8 us  [the longest x2 7.23 us: exchange(): lax.all_to_all(value, 'tile', split_axis=0, concat_axis=0, tiled=True)]
    pallas_call x16 -> x17, Pallas kernels: 31.8 us -> 33.1 us  [call(): pl.pallas_call(kernel, out_shape=shapes, in_specs=places or [SM] * scalar...]
  transfers between devices with their start and end apart: 14 -> 11, of which waited for: 9 -> 7; matrix products, arithmetic and copies ran while one was open for 0% -> 0% of each run, Pallas kernels for 20% -> 21%
where the time goes in v3:
time: 110 us
  starting transfers between devices  36.4 us (33%)
  Pallas kernels  33.1 us (30%)
  blocking collectives  19.7 us (18%)
  waiting for transfers between devices  18.1 us (16%)
  local copies, waits for them, and re-layouts  1.67 us (2%)
    pallas_call x17, Pallas kernels, call(): pl.pallas_call(kernel, out_shape=shapes, in_specs=places or [SM] * scalar...  33.1 us
    all_to_all x2, starting transfers between devices, exchange(): lax.all_to_all(value, 'tile', split_axis=0, concat_axis=0, tiled=True)  22.9 us
    all_to_all x1, blocking collectives, exchange(): lax.all_to_all(value, 'tile', split_axis=0, concat_axis=0, tiled=True)  19.7 us
    ppermute x8, starting transfers between devices, swap(): lax.ppermute(value, axis, [(i, j) for i, j in enumerate(partner) if 0 <=...  7.72 us
    all_to_all x2, waiting for transfers between devices, exchange(): lax.all_to_all(value, 'tile', split_axis=0, concat_axis=0, tiled=True)  7.23 us
    all_to_all x1, starting transfers between devices, per_device(): lax.all_to_all(copies, 'tile', split_axis=0, concat_axis=0, tiled=True, a...  5.72 us
    all_to_all x1, waiting for transfers between devices, per_device(): lax.all_to_all(copies, 'tile', split_axis=0, concat_axis=0, tiled=True, a...  5.61 us
    ppermute x8, waiting for transfers between devices, swap(): lax.ppermute(value, axis, [(i, j) for i, j in enumerate(partner) if 0 <=...  5.25 us
  transfers between devices with their start and end apart: 11, of which 7 were waited for; matrix products, arithmetic and copies ran while one was open for 0% of the time, Pallas kernels for 21%

profile of v3, /device:TPU:2, one launch (start us, length us, event | category | flops | bytes accessed | tf_op | source)
XLA Modules:
  0.0 109.8 jit_solution(15428616004889211528)
XLA Ops:
  0.6 1.6 %collective-permute-start.2 = (f32[256,128]{1,0:T(8,128)}, f32[256,128]{1,0:T(8,128)S(1)}, u32[]{:S(2)}, u32[]{:S(2)}) collective-permute-start(f32[256,128]{1,0:T(8,128)} %bitcast.11), channel_id=1, source_target_pairs={{0,3},{1,2},{2,1},{3,0},{4,7},{5,6},{6,5},{7,4},{8,11},{9,10},{10,... | collective-permute-start | bytes 393224 | tf_op jit(solution)/shard_map/ppermute | solution.py:576
  2.2 2.8 %collective-permute-start.1 = (f32[256,128]{1,0:T(8,128)}, f32[256,128]{1,0:T(8,128)S(1)}, u32[]{:S(2)}, u32[]{:S(2)}) collective-permute-start(f32[256,128]{1,0:T(8,128)} %bitcast.12), channel_id=1, source_target_pairs={{0,2},{1,3},{2,0},{3,1},{4,6},{5,7},{6,4},{7,5},{8,10},{9,11},{10,... | collective-permute-start | bytes 393224 | tf_op jit(solution)/shard_map/ppermute | solution.py:576
  5.1 0.0 collective-permute-start
  5.1 2.1 %shard_map.105 = (f32[120,128]{1,0:T(8,128)}, f32[16,128]{1,0:T(8,128)}, f32[16,128]{1,0:T(8,128)}, f32[64,128]{1,0:T(8,128)}) custom-call(s32[1]{0:T(128)} %bitcast.2.at_ref, f32[64,128]{1,0:T(8,128)} %bitcast.15, f32[32,128]{1,0:T(8,128)} %bitcast.16, f32[8,128]{1,0:T(8,128)} %bitcast.17, f32[4,128]{1,0:T(4,128)} %fric.1, s32[1,512]{1,0:T(1,128)} %bitcast.18, ...), custom_call_target="tpu_custom_call" | custom-call | flops 65536000 | bytes 400000 | tf_op jit(solution)/shard_map/pallas_call | solution.py:40
  7.1 0.7 collective-permute-start.3
  7.8 0.7 collective-permute-start.4
  8.5 0.0 collective-permute-done.4.edge_d
  8.5 0.0 collective-permute-done.3.swap_b
  8.5 0.0 collective-permute-done.2.back
  8.5 1.8 %collective-permute-done.1.across = f32[256,128]{1,0:T(8,128)S(1)} collective-permute-done((f32[256,128]{1,0:T(8,128)}, f32[256,128]{1,0:T(8,128)S(1)}, u32[]{:S(2)}, u32[]{:S(2)}) %collective-permute-start.1) | collective-permute-done | bytes 131104 | tf_op jit(solution)/shard_map/ppermute | solution.py:576
  10.3 0.5 collective-permute-done.near
  10.8 0.0 copy-start.2
  10.8 0.9 copy-done.2
  11.7 0.0 copy-start.3
  11.7 0.8 copy-done.3
  12.5 0.0 copy-start
  12.5 1.3 %shard_map.106 = (bf16[256,512]{1,0:T(8,128)(2,1)S(1)}, bf16[256,512]{1,0:T(8,128)(2,1)S(1)}, f32[64,8,128]{2,1,0:T(8,128)}) custom-call(s32[1]{0:T(128)} %bitcast.me_ref, f32[256,128]{1,0:T(8,128)S(1)} %bitcast.14, f32[256,128]{1,0:T(8,128)S(1)} %collective-permute-done.near, f32[256,128]{1,0:T(8,128)S(1)} %collective-permute-done.1.across, ...), custom_call_target="tpu_custom_call" | custom-call | flops 20000000000 | bytes 1500000 | tf_op jit(solution)/shard_map/pallas_call | solution.py:40
  13.8 17.8 %all-to-all-start = ((f32[64,8,128]{2,1,0:T(8,128)}), f32[64,8,128]{2,1,0:T(8,128)S(1)}, u32[]{:S(2)}, u32[]{:S(2)}) async-start(f32[64,8,128]{2,1,0:T(8,128)} %get-tuple-element.37), calls=%async_computation | async-start | bytes 524288 | tf_op jit(solution)/shard_map/all_to_all | solution.py:635
  31.6 0.0 copy-done
  31.6 0.1 collective-permute-start.5
  31.8 0.0 copy-done.4
  31.8 1.7 %collective-permute-start.6 = (f32[16,128]{1,0:T(8,128)S(1)}, f32[16,128]{1,0:T(8,128)S(1)}, u32[]{:S(2)}, u32[]{:S(2)}) collective-permute-start(f32[16,128]{1,0:T(8,128)S(1)} %copy-done.4), channel_id=1, source_target_pairs={{0,8},{4,12},{8,0},{12,4},{16,24},{20,28},{24,16},{28,20},{32,40},... | collective-permute-start | bytes 24584 | tf_op jit(solution)/shard_map/ppermute | solution.py:576
  33.5 0.0 copy-done.1
  33.5 0.1 shard_map.104
  33.6 1.9 %collective-permute-done.6.edge_c = f32[16,128]{1,0:T(8,128)S(1)} collective-permute-done((f32[16,128]{1,0:T(8,128)S(1)}, f32[16,128]{1,0:T(8,128)S(1)}, u32[]{:S(2)}, u32[]{:S(2)}) %collective-permute-start.6) | collective-permute-done | bytes 8224 | tf_op jit(solution)/shard_map/ppermute | solution.py:576
  35.5 0.0 collective-permute-done.5.swap_a
  35.5 5.7 %shard_map.107 = (f32[2,4,8,128]{3,2,1,0:T(8,128)S(1)}, f32[13,12,16,128]{3,2,1,0:T(8,128)S(1)}, f32[2,4,128]{2,1,0:T(4,128)S(1)}) custom-call(s32[1]{0:T(128)} %bitcast.2.at_ref, f32[120,128]{1,0:T(8,128)S(1)} %copy-done, f32[120,128]{1,0:T(8,128)S(1)} %collective-permute-done.5.swap_a, f32[120,128]{1,0:T(8,128)S(1)} %collective-permute-done.3.swap_b, ...), custom_call_target="tpu_custom_call" | custom-call | flops 28835840 | bytes 2000000 | tf_op jit(solution)/shard_map/pallas_call | solution.py:40
  41.2 3.4 %all-to-all-done.meta = f32[64,8,128]{2,1,0:T(8,128)S(1)} async-done(((f32[64,8,128]{2,1,0:T(8,128)}), f32[64,8,128]{2,1,0:T(8,128)S(1)}, u32[]{:S(2)}, u32[]{:S(2)}) %all-to-all-start) | async-done | bytes 262176 | tf_op jit(solution)/shard_map/all_to_all | solution.py:635
  44.6 0.6 shard_map.108
  45.2 19.7 %all_to_all.20.arrived = f32[64,8,128]{2,1,0:T(8,128)S(1)} all-to-all(f32[64,8,128]{2,1,0:T(8,128)S(1)} %shard_map.108), channel_id=1, replica_groups=mesh['tile'=64,'probe'=4] {'tile'}, dimensions={0} | all-to-all | bytes 524288 | tf_op jit(solution)/shard_map/all_to_all | solution.py:635
  65.0 1.6 %shard_map.109 = f32[256,128]{1,0:T(8,128)} custom-call(f32[64,8,128]{2,1,0:T(8,128)S(1)} %all_to_all.20.arrived, f32[120,128]{1,0:T(8,128)S(1)} %copy-done, bf16[512,512]{1,0:T(8,128)(2,1)S(1)} %get-tuple-element.43.precision_high, bf16[512,512]{1,0:T(8,128)(2,1)S(1)} %get-tuple-element.44.precision_low), custom_call_target="tpu_custom_call" | custom-call | flops 20000000000 | bytes 1500000 | tf_op jit(solution)/shard_map/pallas_call | solution.py:40
  66.6 5.1 %all-to-all-start.2 = ((f32[64,4,128]{2,1,0:T(4,128)}), f32[64,4,128]{2,1,0:T(4,128)S(1)}, u32[]{:S(2)}, u32[]{:S(2)}) async-start(f32[64,4,128]{2,1,0:T(4,128)} %bitcast.8), calls=%async_computation.2 | async-start | bytes 262144 | tf_op jit(solution)/shard_map/all_to_all | solution.py:635
  71.7 1.8 %shard_map.110.before = f32[256,256]{1,0:T(8,128)S(1)} custom-call(f32[64,8,128]{2,1,0:T(8,128)S(1)} %all_to_all.20.arrived), custom_call_target="tpu_custom_call" | custom-call | flops 50331648 | bytes 500000 | tf_op jit(solution)/shard_map/pallas_call | solution.py:40
  73.5 1.8 %shard_map.111.before = f32[256,256]{1,0:T(8,128)S(1)} custom-call(f32[256,256]{1,0:T(8,128)S(1)} %shard_map.110.before), custom_call_target="tpu_custom_call" | custom-call | flops 50331648 | bytes 500000 | tf_op jit(solution)/shard_map/pallas_call | solution.py:40
  75.2 1.8 %shard_map.112.before = f32[256,256]{1,0:T(8,128)S(1)} custom-call(f32[256,256]{1,0:T(8,128)S(1)} %shard_map.111.before), custom_call_target="tpu_custom_call" | custom-call | flops 50331648 | bytes 500000 | tf_op jit(solution)/shard_map/pallas_call | solution.py:40
  77.0 1.8 %shard_map.113.before = f32[256,256]{1,0:T(8,128)S(1)} custom-call(f32[256,256]{1,0:T(8,128)S(1)} %shard_map.112.before), custom_call_target="tpu_custom_call" | custom-call | flops 50331648 | bytes 500000 | tf_op jit(solution)/shard_map/pallas_call | solution.py:40
  78.8 3.8 %all-to-all-done.2 = f32[64,4,128]{2,1,0:T(4,128)S(1)} async-done(((f32[64,4,128]{2,1,0:T(4,128)}), f32[64,4,128]{2,1,0:T(4,128)S(1)}, u32[]{:S(2)}, u32[]{:S(2)}) %all-to-all-start.2) | async-done | bytes 131104 | tf_op jit(solution)/shard_map/all_to_all | solution.py:635
  82.6 5.3 %shard_map.114 = (f32[4,8,128]{2,1,0:T(8,128)S(1)}, f32[8,256]{1,0:T(8,128)S(1)}) custom-call(f32[256,128]{1,0:T(8,128)S(1)} %bitcast.10, f32[64,8,128]{2,1,0:T(8,128)S(1)} %all-to-all-done.meta, f32[13,12,16,128]{3,2,1,0:T(8,128)S(1)} %get-tuple-element.46.coef, f32[2,4,128]{2,1,0:T(4,128)S(1)} %get-tuple-element.47.gain, ...), custom_call_target="tpu_custom_call" | custom-call | flops 28835840 | bytes 2000000 | tf_op jit(solution)/shard_map/pallas_call | solution.py:40
  87.9 0.1 collective-permute-start.7
  88.0 1.1 collective-permute-done.7.other
  89.1 0.7 shard_map.115
  89.8 5.7 %all-to-all-start.3 = ((f32[32,8,256]{2,1,0:T(8,128)}), f32[32,8,256]{2,1,0:T(8,128)S(1)}, u32[]{:S(2)}, u32[]{:S(2)}) async-start(f32[32,8,256]{2,1,0:T(8,128)} %shard_map.115), calls=%async_computation.3 | async-start | bytes 524288 | tf_op jit(solution)/shard_map/all_to_all | solution.py:723
  95.6 1.8 %shard_map.116.before = f32[256,256]{1,0:T(8,128)S(1)} custom-call(f32[256,256]{1,0:T(8,128)S(1)} %shard_map.113.before), custom_call_target="tpu_custom_call" | custom-call | flops 50331648 | bytes 500000 | tf_op jit(solution)/shard_map/pallas_call | solution.py:40
  97.3 1.8 %shard_map.117.before = f32[256,256]{1,0:T(8,128)S(1)} custom-call(f32[256,256]{1,0:T(8,128)S(1)} %shard_map.116.before), custom_call_target="tpu_custom_call" | custom-call | flops 50331648 | bytes 500000 | tf_op jit(solution)/shard_map/pallas_call | solution.py:40
  99.1 1.8 %shard_map.118.before = f32[256,256]{1,0:T(8,128)S(1)} custom-call(f32[256,256]{1,0:T(8,128)S(1)} %shard_map.117.before), custom_call_target="tpu_custom_call" | custom-call | flops 50331648 | bytes 500000 | tf_op jit(solution)/shard_map/pallas_call | solution.py:40
  100.8 2.4 %shard_map.119 = (bf16[256,256]{1,0:T(8,128)(2,1)S(1)}, bf16[256,256]{1,0:T(8,128)(2,1)S(1)}, bf16[256,256]{1,0:T(8,128)(2,1)S(1)}, bf16[256,512]{1,0:T(8,128)(2,1)S(1)}, bf16[256,512]{1,0:T(8,128)(2,1)S(1)}) custom-call(f32[256,256]{1,0:T(8,128)S(1)} %shard_map.118.before, bf16[256,512]{1,0:T(8,128)(2,1)S(1)} %get-tuple-element.48.panel_high, ...), custom_call_target="tpu_custom_call" | custom-call | flops 251658240 | bytes 1500000 | tf_op jit(solution)/shard_map/pallas_call | solution.py:40
  103.2 5.6 %all-to-all-done.3.parts = f32[32,8,256]{2,1,0:T(8,128)S(1)} async-done(((f32[32,8,256]{2,1,0:T(8,128)}), f32[32,8,256]{2,1,0:T(8,128)S(1)}, u32[]{:S(2)}, u32[]{:S(2)}) %all-to-all-start.3) | async-done | bytes 262176 | tf_op jit(solution)/shard_map/all_to_all | solution.py:723
  108.8 0.9 shard_map.120
  (2 shorter events, 0.0 us)
Async XLA Ops:
  0.6 7.9 %collective-permute-start.2 = (f32[256,128]{1,0:T(8,128)}, f32[256,128]{1,0:T(8,128)S(1)}, u32[]{:S(2)}, u32[]{:S(2)}) collective-permute-start(f32[256,128]{1,0:T(8,128)} %bitcast.11), channel_id=1, source_target_pairs={{0,3},{1,2},{2,1},{3,0},{4,7},{5,6},{6,5},{7,4},{8,11},{9,10},{10,... | collective-permute-start | bytes 393224 | tf_op jit(solution)/shard_map/ppermute | solution.py:576
  2.2 8.1 %collective-permute-start.1 = (f32[256,128]{1,0:T(8,128)}, f32[256,128]{1,0:T(8,128)S(1)}, u32[]{:S(2)}, u32[]{:S(2)}) collective-permute-start(f32[256,128]{1,0:T(8,128)} %bitcast.12), channel_id=1, source_target_pairs={{0,2},{1,3},{2,0},{3,1},{4,6},{5,7},{6,4},{7,5},{8,10},{9,11},{10,... | collective-permute-start | bytes 393224 | tf_op jit(solution)/shard_map/ppermute | solution.py:576
  5.1 5.7 %collective-permute-start = (f32[256,128]{1,0:T(8,128)}, f32[256,128]{1,0:T(8,128)S(1)}, u32[]{:S(2)}, u32[]{:S(2)}) collective-permute-start(f32[256,128]{1,0:T(8,128)} %bitcast.13), channel_id=1, source_target_pairs={{0,1},{1,0},{2,3},{3,2},{4,5},{5,4},{6,7},{7,6},{8,9},{9,8},{10,11... | collective-permute-start | bytes 393224 | tf_op jit(solution)/shard_map/ppermute | solution.py:576
  7.1 1.4 %collective-permute-start.3 = (f32[120,128]{1,0:T(8,128)}, f32[120,128]{1,0:T(8,128)S(1)}, u32[]{:S(2)}, u32[]{:S(2)}) collective-permute-start(f32[120,128]{1,0:T(8,128)} %get-tuple-element.34.own.packed), channel_id=1, source_target_pairs={{4,8},{8,4},{12,16},{16,12},{20,24},{24,20},{28,32},{32,28},{36,40... | collective-permute-start | bytes 184328 | tf_op jit(solution)/shard_map/ppermute | solution.py:576
  7.8 0.7 collective-permute-start.4
  10.8 0.9 copy-start.2
  11.7 0.8 copy-start.3
  12.5 19.2 %copy-start = (f32[120,128]{1,0:T(8,128)S(1)}, f32[120,128]{1,0:T(8,128)}, u32[]{:S(2)}) copy-start(f32[120,128]{1,0:T(8,128)} %get-tuple-element.34.own.packed) | copy-start | bytes 184324
  12.5 19.3 %copy-start.4 = (f32[16,128]{1,0:T(8,128)S(1)}, f32[16,128]{1,0:T(8,128)}, u32[]{:S(2)}) copy-start(f32[16,128]{1,0:T(8,128)} %get-tuple-element.40) | copy-start | bytes 24580
  12.5 21.0 %copy-start.1 = (f32[512,512]{1,0:T(8,128)S(1)}, f32[512,512]{1,0:T(8,128)}, u32[]{:S(2)}) copy-start(f32[512,512]{1,0:T(8,128)} %precision.1) | copy-start | bytes 3145732
  13.8 30.8 %all-to-all-start = ((f32[64,8,128]{2,1,0:T(8,128)}), f32[64,8,128]{2,1,0:T(8,128)S(1)}, u32[]{:S(2)}, u32[]{:S(2)}) async-start(f32[64,8,128]{2,1,0:T(8,128)} %get-tuple-element.37), calls=%async_computation | async-start | bytes 524288 | tf_op jit(solution)/shard_map/all_to_all | solution.py:635
  31.6 3.9 %collective-permute-start.5 = (f32[120,128]{1,0:T(8,128)S(1)}, f32[120,128]{1,0:T(8,128)S(1)}, u32[]{:S(2)}, u32[]{:S(2)}) collective-permute-start(f32[120,128]{1,0:T(8,128)S(1)} %copy-done), channel_id=1, source_target_pairs={{0,4},{4,0},{8,12},{12,8},{16,20},{20,16},{24,28},{28,24},{32,36},... | collective-permute-start | bytes 184328 | tf_op jit(solution)/shard_map/ppermute | solution.py:576
  31.8 3.7 %collective-permute-start.6 = (f32[16,128]{1,0:T(8,128)S(1)}, f32[16,128]{1,0:T(8,128)S(1)}, u32[]{:S(2)}, u32[]{:S(2)}) collective-permute-start(f32[16,128]{1,0:T(8,128)S(1)} %copy-done.4), channel_id=1, source_target_pairs={{0,8},{4,12},{8,0},{12,4},{16,24},{20,28},{24,16},{28,20},{32,40},... | collective-permute-start | bytes 24584 | tf_op jit(solution)/shard_map/ppermute | solution.py:576
  66.6 16.0 %all-to-all-start.2 = ((f32[64,4,128]{2,1,0:T(4,128)}), f32[64,4,128]{2,1,0:T(4,128)S(1)}, u32[]{:S(2)}, u32[]{:S(2)}) async-start(f32[64,4,128]{2,1,0:T(4,128)} %bitcast.8), calls=%async_computation.2 | async-start | bytes 262144 | tf_op jit(solution)/shard_map/all_to_all | solution.py:635
  87.9 1.2 %collective-permute-start.7 = (f32[8,256]{1,0:T(8,128)S(1)}, f32[8,256]{1,0:T(8,128)S(1)}, u32[]{:S(2)}, u32[]{:S(2)}) collective-permute-start(f32[8,256]{1,0:T(8,128)S(1)} %get-tuple-element.52.own), channel_id=1, source_target_pairs={{0,4},{4,0},{8,12},{12,8},{16,20},{20,16},{24,28},{28,24},{32,36},... | collective-permute-start | bytes 24584 | tf_op jit(solution)/shard_map/ppermute | solution.py:576
  89.8 19.0 %all-to-all-start.3 = ((f32[32,8,256]{2,1,0:T(8,128)}), f32[32,8,256]{2,1,0:T(8,128)S(1)}, u32[]{:S(2)}, u32[]{:S(2)}) async-start(f32[32,8,256]{2,1,0:T(8,128)} %shard_map.115), calls=%async_computation.3 | async-start | bytes 524288 | tf_op jit(solution)/shard_map/all_to_all | solution.py:723

commit v4 on v3

--- a/solution.py
+++ b/solution.py
@@ -24,7 +24,7 @@
 PIVOTS = 4
 PIECES = (3, 3)
 V_AT, P_AT, B_AT, F_AT = 0, CX * NZ, CX * (NZ + KD), CX * (NZ + KD + 2)
-T_AT, R_AT, PACK = F_AT + CX, F_AT + 8, F_AT + 16
+PACK = F_AT + 8
 f32 = jnp.float32
 bf16 = jnp.bfloat16
 VM = pl.BlockSpec(memory_space=pltpu.VMEM)
@@ -80,18 +80,12 @@
 
 
 def prepare_kernel(
-    at_ref, visc, probes, base, fric, tile_row, cell_row, sight,
-    packed, edge_c, edge_d, asked,
-    fric_in, tile_in, cell_in, sight_in, sems,
+    at_ref, visc, probes, base, fric, packed, edge_c, edge_d, fric_in, sems
 ):
-    rows = tile_in.shape[1]
     upper_pair = lax.rem(at_ref[0], 4) // 2
     high_row = pl.multiple_of((CX - 1) * NZ * (1 - upper_pair), NZ)
     low_row = pl.multiple_of((CX - 1) * NZ * upper_pair, NZ)
     moves = [
-        (tile_row, tile_in),
-        (cell_row, cell_in),
-        (sight, sight_in),
         (fric, fric_in),
         (visc, packed.at[pl.ds(V_AT, CX * NZ), :]),
         (probes, packed.at[pl.ds(P_AT, CX * KD), :]),
@@ -107,16 +101,21 @@
         copy.start()
     for copy in copies:
         copy.wait()
+    packed[F_AT:PACK, :] = jnp.concatenate(
+        [fric_in[...], jnp.zeros((PACK - F_AT - CX, NY), f32)], axis=0
+    )
+
+
+def meta_kernel(tile_in, cell_in, sight_in, basis, asked, slots, own_basis):
+    own_basis[...] = basis[...]
+    rows = tile_in.shape[1]
     one_hot = (iota((TILES, rows), 0) == tile_in[...]).astype(f32)
     before = (iota((rows, rows), 0) < iota((rows, rows), 1)).astype(f32).astype(bf16)
     one_hot_b = one_hot.astype(bf16)
     earlier = dot(one_hot_b, before, NN)
     rank = jnp.sum(one_hot * earlier, axis=0, keepdims=True).astype(jnp.int32)
-    tail = [fric_in[...]]
-    for values in (tile_in[...], rank):
-        tail += [values[:, n * 128 : (n + 1) * 128].astype(f32) for n in range(rows // 128)]
-    tail.append(jnp.zeros((PACK - F_AT - CX - 2 * rows // 128, NY), f32))
-    packed[F_AT:PACK, :] = jnp.concatenate(tail, axis=0)
+    slots[0:1, :] = tile_in[...]
+    slots[1:2, :] = rank
     chosen = (iota((CAP, rows), 0) == rank).astype(f32)
     values = jnp.concatenate(
         [
@@ -502,16 +501,11 @@
     high[...], low[...] = split2(precision[...])
 
 
-def precision_kernel(arrived, packed, precision_high, precision_low, payload):
+def precision_kernel(arrived, slots, precision_high, precision_low, payload):
     rows = precision_high.shape[0]
 
-    def line(at):
-        return jnp.concatenate(
-            [packed[at + n : at + n + 1, :] for n in range(rows // 128)], axis=1
-        ).astype(jnp.int32)
-
-    one_hot = (iota((128, rows), 0) == line(T_AT)).astype(f32).astype(bf16)
-    rank = line(R_AT)
+    one_hot = (iota((128, rows), 0) == slots[0:1, :]).astype(f32).astype(bf16)
+    rank = slots[1:2, :]
     mine = arrived[:, 0, :]
     turned = jnp.transpose(jnp.concatenate([mine, jnp.zeros((128 - TILES, 128), f32)], axis=0))
     spread = [dot(part, one_hot, NN) for part in split3(turned)]
@@ -588,38 +582,29 @@
         probes.reshape(CX * KD, NY),
         base_velocity.reshape(CX * 2, NY),
         friction,
-        obs_tile.reshape(1, -1),
-        obs_cell.reshape(1, -1),
-        sight_lines,
     ]
-    own_basis = basis.reshape(-1, NY)
-    others = [swap(own_basis, "probe", d) for d in (1, 2, 3)]
-    packed, edge_c, edge_d, asked = call(
+    others = [swap(basis.reshape(-1, NY), "probe", d) for d in (1, 2, 3)]
+    packed, edge_c, edge_d = call(
         prepare_kernel,
-        [
-            sds((PACK, NY)),
-            sds((NZ, NY)),
-            sds((NZ, NY)),
-            sds((TILES, 128)),
-        ],
+        [sds((PACK, NY)), sds((NZ, NY)), sds((NZ, NY))],
         [at, *arguments],
         places=[SM] + [pl.BlockSpec(memory_space=pltpu.HBM)] * len(arguments),
-        scratch=[
-            pltpu.VMEM((CX, NY), f32),
-            pltpu.VMEM((1, rows), jnp.int32),
-            pltpu.VMEM((1, rows), jnp.int32),
-            pltpu.VMEM((2, rows), f32),
-            pltpu.SemaphoreType.DMA((9,)),
-        ],
-        flops=2 * 64 * 512 * 1000,
+        scratch=[pltpu.VMEM((CX, NY), f32), pltpu.SemaphoreType.DMA((6,))],
         moved=400000,
         vmem=VMEM_PREP,
+    )
+    asked, slots, own_basis = call(
+        meta_kernel,
+        [sds((TILES, 128)), sds((2, rows), jnp.int32), sds((basis.shape[0] * CX, NY))],
+        [obs_tile.reshape(1, -1), obs_cell.reshape(1, -1), sight_lines, basis.reshape(-1, NY)],
+        flops=10**10,
+        moved=400000,
     )
     swap_a = swap(packed, "tile", 1)
     swap_b = swap(packed, "tile", 1, 1)
     far_c = swap(edge_c, "tile", 2)
     far_d = swap(edge_d, "tile", 2, 2)
-    asked, swap_b, far_d = lax.optimization_barrier((asked, swap_b, far_d))
+    asked, swap_b, far_c, far_d = lax.optimization_barrier((asked, swap_b, far_c, far_d))
     n_basis = 4 * basis.shape[0]
     panel_high, panel_low, request = call(
         gram_kernel,
@@ -673,7 +658,7 @@
     outgoing = call(
         precision_kernel,
         sds((TILES * 4, 128)),
-        [arrived, packed, *precision_parts],
+        [arrived, slots, *precision_parts],
         flops=20 * 10**9,
         moved=1500000,
     )

time: 110 us -> 108 us (0.982)
  blocking collectives: 19.7 us -> 17.7 us
  starting transfers between devices: 36.4 us -> 34.8 us
  local copies, waits for them, and re-layouts: 1.67 us -> 2.96 us
    all_to_all x2, waiting for transfers between devices: 7.23 us -> 9.76 us  [exchange(): lax.all_to_all(value, 'tile', split_axis=0, concat_axis=0, tiled=True)]
    ppermute x8, waiting for transfers between devices: 5.25 us -> 2.95 us  [swap(): lax.ppermute(value, axis, [(i, j) for i, j in enumerate(partner) if 0 <=...]
    all_to_all x1, blocking collectives: 19.7 us -> 17.7 us  [exchange(): lax.all_to_all(value, 'tile', split_axis=0, concat_axis=0, tiled=True)]
    unnamed x10 -> x12, local copies, waits for them, and re-layouts: 1.67 us -> 2.96 us
    all_to_all x2, starting transfers between devices: 22.9 us -> 21.7 us  [exchange(): lax.all_to_all(value, 'tile', split_axis=0, concat_axis=0, tiled=True)]
    pallas_call x17 -> x18, Pallas kernels: 33.1 us -> 33 us  [call(): pl.pallas_call(kernel, out_shape=shapes, in_specs=places or [SM] * scalar...]
  transfers between devices with their start and end apart: 11 -> 11, of which waited for: 7 -> 7; matrix products, arithmetic and copies ran while one was open for 0% -> 0% of each run, Pallas kernels for 21% -> 20%
where the time goes in v4:
time: 108 us
  starting transfers between devices  34.8 us (32%)
  Pallas kernels  33 us (31%)
  waiting for transfers between devices  18.3 us (17%)
  blocking collectives  17.7 us (16%)
  local copies, waits for them, and re-layouts  2.96 us (3%)
    pallas_call x18, Pallas kernels, call(): pl.pallas_call(kernel, out_shape=shapes, in_specs=places or [SM] * scalar...  33 us
    all_to_all x2, starting transfers between devices, exchange(): lax.all_to_all(value, 'tile', split_axis=0, concat_axis=0, tiled=True)  21.7 us
    all_to_all x1, blocking collectives, exchange(): lax.all_to_all(value, 'tile', split_axis=0, concat_axis=0, tiled=True)  17.7 us
    all_to_all x2, waiting for transfers between devices, exchange(): lax.all_to_all(value, 'tile', split_axis=0, concat_axis=0, tiled=True)  9.76 us
    ppermute x8, starting transfers between devices, swap(): lax.ppermute(value, axis, [(i, j) for i, j in enumerate(partner) if 0 <=...  7.36 us
    all_to_all x1, starting transfers between devices, per_device(): lax.all_to_all(copies, 'tile', split_axis=0, concat_axis=0, tiled=True, a...  5.71 us
    all_to_all x1, waiting for transfers between devices, per_device(): lax.all_to_all(copies, 'tile', split_axis=0, concat_axis=0, tiled=True, a...  5.62 us
    unnamed x12, local copies, waits for them, and re-layouts  2.96 us
  transfers between devices with their start and end apart: 11, of which 7 were waited for; matrix products, arithmetic and copies ran while one was open for 0% of the time, Pallas kernels for 20%

profile of v4, /device:TPU:2, one launch (start us, length us, event | category | flops | bytes accessed | tf_op | source)
XLA Modules:
  0.0 107.6 jit_solution(11459648526284691858)
XLA Ops:
  0.6 1.5 %shard_map.106 = (f32[112,128]{1,0:T(8,128)}, f32[16,128]{1,0:T(8,128)}, f32[16,128]{1,0:T(8,128)}) custom-call(s32[1]{0:T(128)} %bitcast.4.at_ref, f32[64,128]{1,0:T(8,128)} %bitcast.17, f32[32,128]{1,0:T(8,128)} %bitcast.18, f32[8,128]{1,0:T(8,128)} %bitcast.19, f32[4,128]{1,0:T(4,128)} %fric.1), custom_call_target="tpu_custom_call" | custom-call | bytes 400000 | tf_op jit(solution)/shard_map/pallas_call | solution.py:40
  2.1 1.7 %collective-permute-start.4 = (f32[16,128]{1,0:T(8,128)}, f32[16,128]{1,0:T(8,128)S(1)}, u32[]{:S(2)}, u32[]{:S(2)}) collective-permute-start(f32[16,128]{1,0:T(8,128)} %get-tuple-element.39), channel_id=1, source_target_pairs={{0,8},{4,12},{8,0},{12,4},{16,24},{20,28},{24,16},{28,20},{32,40},... | collective-permute-start | bytes 24584 | tf_op jit(solution)/shard_map/ppermute | solution.py:570
  3.8 1.5 %collective-permute-start.2 = (f32[256,128]{1,0:T(8,128)}, f32[256,128]{1,0:T(8,128)S(1)}, u32[]{:S(2)}, u32[]{:S(2)}) collective-permute-start(f32[256,128]{1,0:T(8,128)} %bitcast.11), channel_id=1, source_target_pairs={{0,3},{1,2},{2,1},{3,0},{4,7},{5,6},{6,5},{7,4},{8,11},{9,10},{10,... | collective-permute-start | bytes 393224 | tf_op jit(solution)/shard_map/ppermute | solution.py:570
  5.3 1.4 %collective-permute-start.1 = (f32[256,128]{1,0:T(8,128)}, f32[256,128]{1,0:T(8,128)S(1)}, u32[]{:S(2)}, u32[]{:S(2)}) collective-permute-start(f32[256,128]{1,0:T(8,128)} %bitcast.12), channel_id=1, source_target_pairs={{0,2},{1,3},{2,0},{3,1},{4,6},{5,7},{6,4},{7,5},{8,10},{9,11},{10,... | collective-permute-start | bytes 393224 | tf_op jit(solution)/shard_map/ppermute | solution.py:570
  6.6 1.2 %collective-permute-start = (f32[256,128]{1,0:T(8,128)}, f32[256,128]{1,0:T(8,128)S(1)}, u32[]{:S(2)}, u32[]{:S(2)}) collective-permute-start(f32[256,128]{1,0:T(8,128)} %bitcast.13), channel_id=1, source_target_pairs={{0,1},{1,0},{2,3},{3,2},{4,5},{5,4},{6,7},{7,6},{8,9},{9,8},{10,11... | collective-permute-start | bytes 393224 | tf_op jit(solution)/shard_map/ppermute | solution.py:570
  7.9 0.6 collective-permute-start.5
  8.5 0.0 collective-permute-done.4.edge_c
  8.5 0.7 collective-permute-start.3
  9.2 0.0 copy-start.2
  9.2 0.9 copy-done.2
  10.1 0.7 copy-done.3
  10.8 0.7 copy-done.4
  11.5 0.7 copy-done.5
  12.2 0.5 shard_map.105
  12.7 0.0 collective-permute-done.5.edge_d
  12.7 0.0 collective-permute-done.3.swap_b
  12.7 0.0 collective-permute-done.2.back
  12.7 0.4 collective-permute-done.1.across
  13.1 0.5 collective-permute-done.near
  13.6 1.3 %shard_map.107 = (bf16[256,512]{1,0:T(8,128)(2,1)S(1)}, bf16[256,512]{1,0:T(8,128)(2,1)S(1)}, f32[64,8,128]{2,1,0:T(8,128)}) custom-call(s32[1]{0:T(128)} %bitcast.me_ref, f32[256,128]{1,0:T(8,128)S(1)} %get-tuple-element.36.own, f32[256,128]{1,0:T(8,128)S(1)} %collective-permute-done.near, f32[256,128]{1,0:T(8,128)S(1)} %collective-permute-done.1.across, ...), custom_call_target="tpu_custom_call" | custom-call | flops 20000000000 | bytes 1500000 | tf_op jit(solution)/shard_map/pallas_call | solution.py:40
  14.9 16.6 %all-to-all-start = ((f32[64,8,128]{2,1,0:T(8,128)}), f32[64,8,128]{2,1,0:T(8,128)S(1)}, u32[]{:S(2)}, u32[]{:S(2)}) async-start(f32[64,8,128]{2,1,0:T(8,128)} %get-tuple-element.42), calls=%async_computation | async-start | bytes 524288 | tf_op jit(solution)/shard_map/all_to_all | solution.py:620
  31.6 0.0 copy-done
  31.6 0.1 collective-permute-start.6
  31.7 0.0 copy-done.1
  31.7 0.1 shard_map.104
  31.9 1.0 collective-permute-done.6.swap_a
  32.9 5.7 %shard_map.108 = (f32[2,4,8,128]{3,2,1,0:T(8,128)S(1)}, f32[13,12,16,128]{3,2,1,0:T(8,128)S(1)}, f32[2,4,128]{2,1,0:T(4,128)S(1)}) custom-call(s32[1]{0:T(128)} %bitcast.4.at_ref, f32[112,128]{1,0:T(8,128)S(1)} %copy-done, f32[112,128]{1,0:T(8,128)S(1)} %collective-permute-done.6.swap_a, f32[112,128]{1,0:T(8,128)S(1)} %collective-permute-done.3.swap_b, ...), custom_call_target="tpu_custom_call" | custom-call | flops 28835840 | bytes 2000000 | tf_op jit(solution)/shard_map/pallas_call | solution.py:40
  38.6 6.0 %all-to-all-done.meta = f32[64,8,128]{2,1,0:T(8,128)S(1)} async-done(((f32[64,8,128]{2,1,0:T(8,128)}), f32[64,8,128]{2,1,0:T(8,128)S(1)}, u32[]{:S(2)}, u32[]{:S(2)}) %all-to-all-start) | async-done | bytes 262176 | tf_op jit(solution)/shard_map/all_to_all | solution.py:620
  44.5 0.6 shard_map.109
  45.1 17.7 %all_to_all.20.arrived = f32[64,8,128]{2,1,0:T(8,128)S(1)} all-to-all(f32[64,8,128]{2,1,0:T(8,128)S(1)} %shard_map.109), channel_id=1, replica_groups=mesh['tile'=64,'probe'=4] {'tile'}, dimensions={0} | all-to-all | bytes 524288 | tf_op jit(solution)/shard_map/all_to_all | solution.py:620
  62.8 1.6 %shard_map.110 = f32[256,128]{1,0:T(8,128)} custom-call(f32[64,8,128]{2,1,0:T(8,128)S(1)} %all_to_all.20.arrived, s32[2,512]{1,0:T(2,128)S(1)} %get-tuple-element.48.slots, bf16[512,512]{1,0:T(8,128)(2,1)S(1)} %get-tuple-element.49.precision_high, bf16[512,512]{1,0:T(8,128)(2,1)S(1)} %get-tuple-element.50.precision_low), custom_call_target="tpu_custom_call" | custom-call | flops 20000000000 | bytes 1500000 | tf_op jit(solution)/shard_map/pallas_call | solution.py:40
  64.4 5.1 %all-to-all-start.2 = ((f32[64,4,128]{2,1,0:T(4,128)}), f32[64,4,128]{2,1,0:T(4,128)S(1)}, u32[]{:S(2)}, u32[]{:S(2)}) async-start(f32[64,4,128]{2,1,0:T(4,128)} %bitcast.8), calls=%async_computation.2 | async-start | bytes 262144 | tf_op jit(solution)/shard_map/all_to_all | solution.py:620
  69.5 1.8 %shard_map.111.before = f32[256,256]{1,0:T(8,128)S(1)} custom-call(f32[64,8,128]{2,1,0:T(8,128)S(1)} %all_to_all.20.arrived), custom_call_target="tpu_custom_call" | custom-call | flops 50331648 | bytes 500000 | tf_op jit(solution)/shard_map/pallas_call | solution.py:40
  71.3 1.8 %shard_map.112.before = f32[256,256]{1,0:T(8,128)S(1)} custom-call(f32[256,256]{1,0:T(8,128)S(1)} %shard_map.111.before), custom_call_target="tpu_custom_call" | custom-call | flops 50331648 | bytes 500000 | tf_op jit(solution)/shard_map/pallas_call | solution.py:40
  73.1 1.8 %shard_map.113.before = f32[256,256]{1,0:T(8,128)S(1)} custom-call(f32[256,256]{1,0:T(8,128)S(1)} %shard_map.112.before), custom_call_target="tpu_custom_call" | custom-call | flops 50331648 | bytes 500000 | tf_op jit(solution)/shard_map/pallas_call | solution.py:40
  74.9 1.8 %shard_map.114.before = f32[256,256]{1,0:T(8,128)S(1)} custom-call(f32[256,256]{1,0:T(8,128)S(1)} %shard_map.113.before), custom_call_target="tpu_custom_call" | custom-call | flops 50331648 | bytes 500000 | tf_op jit(solution)/shard_map/pallas_call | solution.py:40
  76.6 3.8 %all-to-all-done.2 = f32[64,4,128]{2,1,0:T(4,128)S(1)} async-done(((f32[64,4,128]{2,1,0:T(4,128)}), f32[64,4,128]{2,1,0:T(4,128)S(1)}, u32[]{:S(2)}, u32[]{:S(2)}) %all-to-all-start.2) | async-done | bytes 131104 | tf_op jit(solution)/shard_map/all_to_all | solution.py:620
  80.4 5.3 %shard_map.115 = (f32[4,8,128]{2,1,0:T(8,128)S(1)}, f32[8,256]{1,0:T(8,128)S(1)}) custom-call(f32[256,128]{1,0:T(8,128)S(1)} %bitcast.10, f32[64,8,128]{2,1,0:T(8,128)S(1)} %all-to-all-done.meta, f32[13,12,16,128]{3,2,1,0:T(8,128)S(1)} %get-tuple-element.52.coef, f32[2,4,128]{2,1,0:T(4,128)S(1)} %get-tuple-element.53.gain, ...), custom_call_target="tpu_custom_call" | custom-call | flops 28835840 | bytes 2000000 | tf_op jit(solution)/shard_map/pallas_call | solution.py:40
  85.8 0.1 collective-permute-start.7
  85.9 1.1 collective-permute-done.7.other
  87.0 0.7 shard_map.116
  87.7 5.7 %all-to-all-start.3 = ((f32[32,8,256]{2,1,0:T(8,128)}), f32[32,8,256]{2,1,0:T(8,128)S(1)}, u32[]{:S(2)}, u32[]{:S(2)}) async-start(f32[32,8,256]{2,1,0:T(8,128)} %shard_map.116), calls=%async_computation.3 | async-start | bytes 524288 | tf_op jit(solution)/shard_map/all_to_all | solution.py:708
  93.4 1.8 %shard_map.117.before = f32[256,256]{1,0:T(8,128)S(1)} custom-call(f32[256,256]{1,0:T(8,128)S(1)} %shard_map.114.before), custom_call_target="tpu_custom_call" | custom-call | flops 50331648 | bytes 500000 | tf_op jit(solution)/shard_map/pallas_call | solution.py:40
  95.2 1.7 %shard_map.118.before = f32[256,256]{1,0:T(8,128)S(1)} custom-call(f32[256,256]{1,0:T(8,128)S(1)} %shard_map.117.before), custom_call_target="tpu_custom_call" | custom-call | flops 50331648 | bytes 500000 | tf_op jit(solution)/shard_map/pallas_call | solution.py:40
  96.9 1.8 %shard_map.119.before = f32[256,256]{1,0:T(8,128)S(1)} custom-call(f32[256,256]{1,0:T(8,128)S(1)} %shard_map.118.before), custom_call_target="tpu_custom_call" | custom-call | flops 50331648 | bytes 500000 | tf_op jit(solution)/shard_map/pallas_call | solution.py:40
  98.7 2.4 %shard_map.120 = (bf16[256,256]{1,0:T(8,128)(2,1)S(1)}, bf16[256,256]{1,0:T(8,128)(2,1)S(1)}, bf16[256,256]{1,0:T(8,128)(2,1)S(1)}, bf16[256,512]{1,0:T(8,128)(2,1)S(1)}, bf16[256,512]{1,0:T(8,128)(2,1)S(1)}) custom-call(f32[256,256]{1,0:T(8,128)S(1)} %shard_map.119.before, bf16[256,512]{1,0:T(8,128)(2,1)S(1)} %get-tuple-element.54.panel_high, ...), custom_call_target="tpu_custom_call" | custom-call | flops 251658240 | bytes 1500000 | tf_op jit(solution)/shard_map/pallas_call | solution.py:40
  101.0 5.6 %all-to-all-done.3.parts = f32[32,8,256]{2,1,0:T(8,128)S(1)} async-done(((f32[32,8,256]{2,1,0:T(8,128)}), f32[32,8,256]{2,1,0:T(8,128)S(1)}, u32[]{:S(2)}, u32[]{:S(2)}) %all-to-all-start.3) | async-done | bytes 262176 | tf_op jit(solution)/shard_map/all_to_all | solution.py:708
  106.7 0.9 shard_map.121
  (5 shorter events, 0.0 us)
Async XLA Ops:
  2.1 6.4 %collective-permute-start.4 = (f32[16,128]{1,0:T(8,128)}, f32[16,128]{1,0:T(8,128)S(1)}, u32[]{:S(2)}, u32[]{:S(2)}) collective-permute-start(f32[16,128]{1,0:T(8,128)} %get-tuple-element.39), channel_id=1, source_target_pairs={{0,8},{4,12},{8,0},{12,4},{16,24},{20,28},{24,16},{28,20},{32,40},... | collective-permute-start | bytes 24584 | tf_op jit(solution)/shard_map/ppermute | solution.py:570
  3.8 9.0 %collective-permute-start.2 = (f32[256,128]{1,0:T(8,128)}, f32[256,128]{1,0:T(8,128)S(1)}, u32[]{:S(2)}, u32[]{:S(2)}) collective-permute-start(f32[256,128]{1,0:T(8,128)} %bitcast.11), channel_id=1, source_target_pairs={{0,3},{1,2},{2,1},{3,0},{4,7},{5,6},{6,5},{7,4},{8,11},{9,10},{10,... | collective-permute-start | bytes 393224 | tf_op jit(solution)/shard_map/ppermute | solution.py:570
  5.3 7.8 %collective-permute-start.1 = (f32[256,128]{1,0:T(8,128)}, f32[256,128]{1,0:T(8,128)S(1)}, u32[]{:S(2)}, u32[]{:S(2)}) collective-permute-start(f32[256,128]{1,0:T(8,128)} %bitcast.12), channel_id=1, source_target_pairs={{0,2},{1,3},{2,0},{3,1},{4,6},{5,7},{6,4},{7,5},{8,10},{9,11},{10,... | collective-permute-start | bytes 393224 | tf_op jit(solution)/shard_map/ppermute | solution.py:570
  6.6 6.9 %collective-permute-start = (f32[256,128]{1,0:T(8,128)}, f32[256,128]{1,0:T(8,128)S(1)}, u32[]{:S(2)}, u32[]{:S(2)}) collective-permute-start(f32[256,128]{1,0:T(8,128)} %bitcast.13), channel_id=1, source_target_pairs={{0,1},{1,0},{2,3},{3,2},{4,5},{5,4},{6,7},{7,6},{8,9},{9,8},{10,11... | collective-permute-start | bytes 393224 | tf_op jit(solution)/shard_map/ppermute | solution.py:570
  7.9 4.8 %collective-permute-start.5 = (f32[16,128]{1,0:T(8,128)}, f32[16,128]{1,0:T(8,128)S(1)}, u32[]{:S(2)}, u32[]{:S(2)}) collective-permute-start(f32[16,128]{1,0:T(8,128)} %get-tuple-element.40), channel_id=1, source_target_pairs={{8,16},{12,20},{16,8},{20,12},{24,32},{28,36},{32,24},{36,28},{40,... | collective-permute-start | bytes 24584 | tf_op jit(solution)/shard_map/ppermute | solution.py:570
  8.5 4.2 %collective-permute-start.3 = (f32[112,128]{1,0:T(8,128)}, f32[112,128]{1,0:T(8,128)S(1)}, u32[]{:S(2)}, u32[]{:S(2)}) collective-permute-start(f32[112,128]{1,0:T(8,128)} %get-tuple-element.38.own), channel_id=1, source_target_pairs={{4,8},{8,4},{12,16},{16,12},{20,24},{24,20},{28,32},{32,28},{36,40... | collective-permute-start | bytes 172040 | tf_op jit(solution)/shard_map/ppermute | solution.py:570
  9.2 0.9 copy-start.2
  10.1 0.7 copy-start.3
  10.8 0.7 copy-start.4
  11.5 0.7 copy-start.5
  13.6 18.0 %copy-start = (f32[112,128]{1,0:T(8,128)S(1)}, f32[112,128]{1,0:T(8,128)}, u32[]{:S(2)}) copy-start(f32[112,128]{1,0:T(8,128)} %get-tuple-element.38.own) | copy-start | bytes 172036
  13.6 18.1 %copy-start.1 = (f32[512,512]{1,0:T(8,128)S(1)}, f32[512,512]{1,0:T(8,128)}, u32[]{:S(2)}) copy-start(f32[512,512]{1,0:T(8,128)} %precision.1) | copy-start | bytes 3145732
  14.9 29.6 %all-to-all-start = ((f32[64,8,128]{2,1,0:T(8,128)}), f32[64,8,128]{2,1,0:T(8,128)S(1)}, u32[]{:S(2)}, u32[]{:S(2)}) async-start(f32[64,8,128]{2,1,0:T(8,128)} %get-tuple-element.42), calls=%async_computation | async-start | bytes 524288 | tf_op jit(solution)/shard_map/all_to_all | solution.py:620
  31.6 1.3 %collective-permute-start.6 = (f32[112,128]{1,0:T(8,128)S(1)}, f32[112,128]{1,0:T(8,128)S(1)}, u32[]{:S(2)}, u32[]{:S(2)}) collective-permute-start(f32[112,128]{1,0:T(8,128)S(1)} %copy-done), channel_id=1, source_target_pairs={{0,4},{4,0},{8,12},{12,8},{16,20},{20,16},{24,28},{28,24},{32,36},... | collective-permute-start | bytes 172040 | tf_op jit(solution)/shard_map/ppermute | solution.py:570
  64.4 16.0 %all-to-all-start.2 = ((f32[64,4,128]{2,1,0:T(4,128)}), f32[64,4,128]{2,1,0:T(4,128)S(1)}, u32[]{:S(2)}, u32[]{:S(2)}) async-start(f32[64,4,128]{2,1,0:T(4,128)} %bitcast.8), calls=%async_computation.2 | async-start | bytes 262144 | tf_op jit(solution)/shard_map/all_to_all | solution.py:620
  85.8 1.2 %collective-permute-start.7 = (f32[8,256]{1,0:T(8,128)S(1)}, f32[8,256]{1,0:T(8,128)S(1)}, u32[]{:S(2)}, u32[]{:S(2)}) collective-permute-start(f32[8,256]{1,0:T(8,128)S(1)} %get-tuple-element.58.own), channel_id=1, source_target_pairs={{0,4},{4,0},{8,12},{12,8},{16,20},{20,16},{24,28},{28,24},{32,36},... | collective-permute-start | bytes 24584 | tf_op jit(solution)/shard_map/ppermute | solution.py:570
  87.7 19.0 %all-to-all-start.3 = ((f32[32,8,256]{2,1,0:T(8,128)}), f32[32,8,256]{2,1,0:T(8,128)S(1)}, u32[]{:S(2)}, u32[]{:S(2)}) async-start(f32[32,8,256]{2,1,0:T(8,128)} %shard_map.116), calls=%async_computation.3 | async-start | bytes 524288 | tf_op jit(solution)/shard_map/all_to_all | solution.py:708

commit v5 on v4

--- a/solution.py
+++ b/solution.py
@@ -24,7 +24,7 @@
 PIVOTS = 4
 PIECES = (3, 3)
 V_AT, P_AT, B_AT, F_AT = 0, CX * NZ, CX * (NZ + KD), CX * (NZ + KD + 2)
-PACK = F_AT + 8
+O_AT, PACK = F_AT + 4, F_AT + 24
 f32 = jnp.float32
 bf16 = jnp.bfloat16
 VM = pl.BlockSpec(memory_space=pltpu.VMEM)
@@ -80,13 +80,17 @@
 
 
 def prepare_kernel(
-    at_ref, visc, probes, base, fric, packed, edge_c, edge_d, fric_in, sems
+    at_ref, visc, probes, base, fric, tile_row, cell_row, sight,
+    packed, edge_c, edge_d, fric_in, tile_in, cell_in, sight_in, sems,
 ):
     upper_pair = lax.rem(at_ref[0], 4) // 2
     high_row = pl.multiple_of((CX - 1) * NZ * (1 - upper_pair), NZ)
     low_row = pl.multiple_of((CX - 1) * NZ * upper_pair, NZ)
     moves = [
         (fric, fric_in),
+        (tile_row, tile_in),
+        (cell_row, cell_in),
+        (sight, sight_in),
         (visc, packed.at[pl.ds(V_AT, CX * NZ), :]),
         (probes, packed.at[pl.ds(P_AT, CX * KD), :]),
         (base, packed.at[pl.ds(B_AT, CX * 2), :]),
@@ -101,27 +105,37 @@
         copy.start()
     for copy in copies:
         copy.wait()
-    packed[F_AT:PACK, :] = jnp.concatenate(
-        [fric_in[...], jnp.zeros((PACK - F_AT - CX, NY), f32)], axis=0
-    )
-
-
-def meta_kernel(tile_in, cell_in, sight_in, basis, asked, slots, own_basis):
+    tail = [fric_in[...]]
+    for line in (tile_in[...], cell_in[...], sight_in[0:1, :], sight_in[1:2, :]):
+        tail += [line[:, n : n + 128].astype(f32) for n in range(0, line.shape[1], 128)]
+    tail.append(jnp.zeros((4, NY), f32))
+    packed[F_AT:PACK, :] = jnp.concatenate(tail, axis=0)
+
+
+def meta_kernel(packed, basis, asked, slots, own_basis):
     own_basis[...] = basis[...]
-    rows = tile_in.shape[1]
-    one_hot = (iota((TILES, rows), 0) == tile_in[...]).astype(f32)
+    rows = slots.shape[1]
+
+    def line(at):
+        start = O_AT + at * (rows // 128)
+        return jnp.concatenate(
+            [packed[n : n + 1, :] for n in range(start, start + rows // 128)], axis=1
+        )
+
+    tiles = line(0).astype(jnp.int32)
+    one_hot = (iota((TILES, rows), 0) == tiles).astype(f32)
     before = (iota((rows, rows), 0) < iota((rows, rows), 1)).astype(f32).astype(bf16)
     one_hot_b = one_hot.astype(bf16)
     earlier = dot(one_hot_b, before, NN)
     rank = jnp.sum(one_hot * earlier, axis=0, keepdims=True).astype(jnp.int32)
-    slots[0:1, :] = tile_in[...]
+    slots[0:1, :] = tiles
     slots[1:2, :] = rank
     chosen = (iota((CAP, rows), 0) == rank).astype(f32)
     values = jnp.concatenate(
         [
-            chosen * cell_in[...].astype(f32),
-            chosen * sight_in[0:1, :],
-            chosen * sight_in[1:2, :],
+            chosen * line(1),
+            chosen * line(2),
+            chosen * line(3),
             jnp.zeros((128 - 3 * CAP, rows), f32),
         ],
         axis=0,
@@ -582,6 +596,9 @@
         probes.reshape(CX * KD, NY),
         base_velocity.reshape(CX * 2, NY),
         friction,
+        obs_tile.reshape(1, -1),
+        obs_cell.reshape(1, -1),
+        sight_lines,
     ]
     others = [swap(basis.reshape(-1, NY), "probe", d) for d in (1, 2, 3)]
     packed, edge_c, edge_d = call(
@@ -589,14 +606,20 @@
         [sds((PACK, NY)), sds((NZ, NY)), sds((NZ, NY))],
         [at, *arguments],
         places=[SM] + [pl.BlockSpec(memory_space=pltpu.HBM)] * len(arguments),
-        scratch=[pltpu.VMEM((CX, NY), f32), pltpu.SemaphoreType.DMA((6,))],
+        scratch=[
+            pltpu.VMEM((CX, NY), f32),
+            pltpu.VMEM((1, rows), jnp.int32),
+            pltpu.VMEM((1, rows), jnp.int32),
+            pltpu.VMEM((2, rows), f32),
+            pltpu.SemaphoreType.DMA((9,)),
+        ],
         moved=400000,
         vmem=VMEM_PREP,
     )
     asked, slots, own_basis = call(
         meta_kernel,
         [sds((TILES, 128)), sds((2, rows), jnp.int32), sds((basis.shape[0] * CX, NY))],
-        [obs_tile.reshape(1, -1), obs_cell.reshape(1, -1), sight_lines, basis.reshape(-1, NY)],
+        [packed, basis.reshape(-1, NY)],
         flops=10**10,
         moved=400000,
     )

time: 108 us -> 108 us (level)
  local copies, waits for them, and re-layouts: 2.96 us -> 1.74 us
  waiting for transfers between devices: 18.3 us -> 19.5 us
    ppermute x8, waiting for transfers between devices: 2.95 us -> 4.18 us  [swap(): lax.ppermute(value, axis, [(i, j) for i, j in enumerate(partner) if 0 <=...]
    unnamed x12 -> x8, local copies, waits for them, and re-layouts: 2.96 us -> 1.74 us
where the time goes in v5:
time: 108 us
  starting transfers between devices  34.7 us (32%)
  Pallas kernels  33.1 us (31%)
  waiting for transfers between devices  19.5 us (18%)
  blocking collectives  17.7 us (16%)
  local copies, waits for them, and re-layouts  1.74 us (2%)
    pallas_call x18, Pallas kernels, call(): pl.pallas_call(kernel, out_shape=shapes, in_specs=places or [SM] * scalar...  33.1 us
    all_to_all x2, starting transfers between devices, exchange(): lax.all_to_all(value, 'tile', split_axis=0, concat_axis=0, tiled=True)  21.6 us
    all_to_all x1, blocking collectives, exchange(): lax.all_to_all(value, 'tile', split_axis=0, concat_axis=0, tiled=True)  17.7 us
    all_to_all x2, waiting for transfers between devices, exchange(): lax.all_to_all(value, 'tile', split_axis=0, concat_axis=0, tiled=True)  9.75 us
    ppermute x8, starting transfers between devices, swap(): lax.ppermute(value, axis, [(i, j) for i, j in enumerate(partner) if 0 <=...  7.36 us
    all_to_all x1, starting transfers between devices, per_device(): lax.all_to_all(copies, 'tile', split_axis=0, concat_axis=0, tiled=True, a...  5.71 us
    all_to_all x1, waiting for transfers between devices, per_device(): lax.all_to_all(copies, 'tile', split_axis=0, concat_axis=0, tiled=True, a...  5.62 us
    ppermute x8, waiting for transfers between devices, swap(): lax.ppermute(value, axis, [(i, j) for i, j in enumerate(partner) if 0 <=...  4.18 us
  transfers between devices with their start and end apart: 11, of which 7 were waited for; matrix products, arithmetic and copies ran while one was open for 0% of the time, Pallas kernels for 20%

profile of v5, /device:TPU:2, one launch (start us, length us, event | category | flops | bytes accessed | tf_op | source)
XLA Modules:
  0.0 107.6 jit_solution(8949333971065254946)
XLA Ops:
  0.6 1.5 %shard_map.105 = (f32[128,128]{1,0:T(8,128)}, f32[16,128]{1,0:T(8,128)}, f32[16,128]{1,0:T(8,128)}) custom-call(s32[1]{0:T(128)} %bitcast.1.at_ref, f32[64,128]{1,0:T(8,128)} %bitcast.15, f32[32,128]{1,0:T(8,128)} %bitcast.16, f32[8,128]{1,0:T(8,128)} %bitcast.17, f32[4,128]{1,0:T(4,128)} %fric.1, s32[1,512]{1,0:T(1,128)} %bitcast.18, s32[1,512]{1,0:T(1,128)} %bitcast.19, ...), custom_call_target="tpu_custom_call" | custom-call | bytes 400000 | tf_op jit(solution)/shard_map/pallas_call | solution.py:40
  2.2 1.7 %collective-permute-start.4 = (f32[16,128]{1,0:T(8,128)}, f32[16,128]{1,0:T(8,128)S(1)}, u32[]{:S(2)}, u32[]{:S(2)}) collective-permute-start(f32[16,128]{1,0:T(8,128)} %get-tuple-element.39), channel_id=1, source_target_pairs={{0,8},{4,12},{8,0},{12,4},{16,24},{20,28},{24,16},{28,20},{32,40},... | collective-permute-start | bytes 24584 | tf_op jit(solution)/shard_map/ppermute | solution.py:584
  3.8 1.5 %collective-permute-start.2 = (f32[256,128]{1,0:T(8,128)}, f32[256,128]{1,0:T(8,128)S(1)}, u32[]{:S(2)}, u32[]{:S(2)}) collective-permute-start(f32[256,128]{1,0:T(8,128)} %bitcast.11), channel_id=1, source_target_pairs={{0,3},{1,2},{2,1},{3,0},{4,7},{5,6},{6,5},{7,4},{8,11},{9,10},{10,... | collective-permute-start | bytes 393224 | tf_op jit(solution)/shard_map/ppermute | solution.py:584
  5.3 1.4 %collective-permute-start.1 = (f32[256,128]{1,0:T(8,128)}, f32[256,128]{1,0:T(8,128)S(1)}, u32[]{:S(2)}, u32[]{:S(2)}) collective-permute-start(f32[256,128]{1,0:T(8,128)} %bitcast.12), channel_id=1, source_target_pairs={{0,2},{1,3},{2,0},{3,1},{4,6},{5,7},{6,4},{7,5},{8,10},{9,11},{10,... | collective-permute-start | bytes 393224 | tf_op jit(solution)/shard_map/ppermute | solution.py:584
  6.7 1.2 %collective-permute-start = (f32[256,128]{1,0:T(8,128)}, f32[256,128]{1,0:T(8,128)S(1)}, u32[]{:S(2)}, u32[]{:S(2)}) collective-permute-start(f32[256,128]{1,0:T(8,128)} %bitcast.13), channel_id=1, source_target_pairs={{0,1},{1,0},{2,3},{3,2},{4,5},{5,4},{6,7},{7,6},{8,9},{9,8},{10,11... | collective-permute-start | bytes 393224 | tf_op jit(solution)/shard_map/ppermute | solution.py:584
  7.9 0.6 collective-permute-start.5
  8.6 0.0 collective-permute-done.4.edge_c
  8.6 0.7 collective-permute-start.3
  9.3 0.0 copy-start
  9.3 0.8 copy-done
  10.1 0.0 copy-start.3
  10.1 0.9 copy-done.3
  11.0 0.5 shard_map.106
  11.6 0.0 collective-permute-done.5.edge_d
  11.6 0.0 collective-permute-done.3.swap_b
  11.6 0.0 collective-permute-done.2.back
  11.6 1.6 %collective-permute-done.1.across = f32[256,128]{1,0:T(8,128)S(1)} collective-permute-done((f32[256,128]{1,0:T(8,128)}, f32[256,128]{1,0:T(8,128)S(1)}, u32[]{:S(2)}, u32[]{:S(2)}) %collective-permute-start.1) | collective-permute-done | bytes 131104 | tf_op jit(solution)/shard_map/ppermute | solution.py:584
  13.2 0.5 collective-permute-done.near
  13.7 0.0 copy-start.1
  13.7 1.3 %shard_map.107 = (bf16[256,512]{1,0:T(8,128)(2,1)S(1)}, bf16[256,512]{1,0:T(8,128)(2,1)S(1)}, f32[64,8,128]{2,1,0:T(8,128)}) custom-call(s32[1]{0:T(128)} %bitcast.me_ref, f32[256,128]{1,0:T(8,128)S(1)} %get-tuple-element.37.own, f32[256,128]{1,0:T(8,128)S(1)} %collective-permute-done.near, f32[256,128]{1,0:T(8,128)S(1)} %collective-permute-done.1.across, ...), custom_call_target="tpu_custom_call" | custom-call | flops 20000000000 | bytes 1500000 | tf_op jit(solution)/shard_map/pallas_call | solution.py:40
  15.0 16.5 %all-to-all-start = ((f32[64,8,128]{2,1,0:T(8,128)}), f32[64,8,128]{2,1,0:T(8,128)S(1)}, u32[]{:S(2)}, u32[]{:S(2)}) async-start(f32[64,8,128]{2,1,0:T(8,128)} %get-tuple-element.42), calls=%async_computation | async-start | bytes 524288 | tf_op jit(solution)/shard_map/all_to_all | solution.py:643
  31.5 0.0 copy-done.1
  31.6 0.1 collective-permute-start.6
  31.7 0.0 copy-done.2
  31.7 0.1 shard_map.104
  31.8 1.1 collective-permute-done.6.swap_a
  32.9 5.7 %shard_map.108 = (f32[2,4,8,128]{3,2,1,0:T(8,128)S(1)}, f32[13,12,16,128]{3,2,1,0:T(8,128)S(1)}, f32[2,4,128]{2,1,0:T(4,128)S(1)}) custom-call(s32[1]{0:T(128)} %bitcast.1.at_ref, f32[128,128]{1,0:T(8,128)S(1)} %copy-done.1, f32[128,128]{1,0:T(8,128)S(1)} %collective-permute-done.6.swap_a, f32[128,128]{1,0:T(8,128)S(1)} %collective-permute-done.3.swap_b, ...), custom_call_target="tpu_custom_call" | custom-call | flops 28835840 | bytes 2000000 | tf_op jit(solution)/shard_map/pallas_call | solution.py:40
  38.6 5.9 %all-to-all-done.meta = f32[64,8,128]{2,1,0:T(8,128)S(1)} async-done(((f32[64,8,128]{2,1,0:T(8,128)}), f32[64,8,128]{2,1,0:T(8,128)S(1)}, u32[]{:S(2)}, u32[]{:S(2)}) %all-to-all-start) | async-done | bytes 262176 | tf_op jit(solution)/shard_map/all_to_all | solution.py:643
  44.5 0.6 shard_map.109
  45.1 17.7 %all_to_all.20.arrived = f32[64,8,128]{2,1,0:T(8,128)S(1)} all-to-all(f32[64,8,128]{2,1,0:T(8,128)S(1)} %shard_map.109), channel_id=1, replica_groups=mesh['tile'=64,'probe'=4] {'tile'}, dimensions={0} | all-to-all | bytes 524288 | tf_op jit(solution)/shard_map/all_to_all | solution.py:643
  62.8 1.6 %shard_map.110 = f32[256,128]{1,0:T(8,128)} custom-call(f32[64,8,128]{2,1,0:T(8,128)S(1)} %all_to_all.20.arrived, s32[2,512]{1,0:T(2,128)S(1)} %get-tuple-element.48.slots, bf16[512,512]{1,0:T(8,128)(2,1)S(1)} %get-tuple-element.49.precision_high, bf16[512,512]{1,0:T(8,128)(2,1)S(1)} %get-tuple-element.50.precision_low), custom_call_target="tpu_custom_call" | custom-call | flops 20000000000 | bytes 1500000 | tf_op jit(solution)/shard_map/pallas_call | solution.py:40
  64.4 5.1 %all-to-all-start.2 = ((f32[64,4,128]{2,1,0:T(4,128)}), f32[64,4,128]{2,1,0:T(4,128)S(1)}, u32[]{:S(2)}, u32[]{:S(2)}) async-start(f32[64,4,128]{2,1,0:T(4,128)} %bitcast.8), calls=%async_computation.2 | async-start | bytes 262144 | tf_op jit(solution)/shard_map/all_to_all | solution.py:643
  69.5 1.8 %shard_map.111.before = f32[256,256]{1,0:T(8,128)S(1)} custom-call(f32[64,8,128]{2,1,0:T(8,128)S(1)} %all_to_all.20.arrived), custom_call_target="tpu_custom_call" | custom-call | flops 50331648 | bytes 500000 | tf_op jit(solution)/shard_map/pallas_call | solution.py:40
  71.3 1.8 %shard_map.112.before = f32[256,256]{1,0:T(8,128)S(1)} custom-call(f32[256,256]{1,0:T(8,128)S(1)} %shard_map.111.before), custom_call_target="tpu_custom_call" | custom-call | flops 50331648 | bytes 500000 | tf_op jit(solution)/shard_map/pallas_call | solution.py:40
  73.1 1.8 %shard_map.113.before = f32[256,256]{1,0:T(8,128)S(1)} custom-call(f32[256,256]{1,0:T(8,128)S(1)} %shard_map.112.before), custom_call_target="tpu_custom_call" | custom-call | flops 50331648 | bytes 500000 | tf_op jit(solution)/shard_map/pallas_call | solution.py:40
  74.8 1.8 %shard_map.114.before = f32[256,256]{1,0:T(8,128)S(1)} custom-call(f32[256,256]{1,0:T(8,128)S(1)} %shard_map.113.before), custom_call_target="tpu_custom_call" | custom-call | flops 50331648 | bytes 500000 | tf_op jit(solution)/shard_map/pallas_call | solution.py:40
  76.6 3.8 %all-to-all-done.2 = f32[64,4,128]{2,1,0:T(4,128)S(1)} async-done(((f32[64,4,128]{2,1,0:T(4,128)}), f32[64,4,128]{2,1,0:T(4,128)S(1)}, u32[]{:S(2)}, u32[]{:S(2)}) %all-to-all-start.2) | async-done | bytes 131104 | tf_op jit(solution)/shard_map/all_to_all | solution.py:643
  80.4 5.3 %shard_map.115 = (f32[4,8,128]{2,1,0:T(8,128)S(1)}, f32[8,256]{1,0:T(8,128)S(1)}) custom-call(f32[256,128]{1,0:T(8,128)S(1)} %bitcast.10, f32[64,8,128]{2,1,0:T(8,128)S(1)} %all-to-all-done.meta, f32[13,12,16,128]{3,2,1,0:T(8,128)S(1)} %get-tuple-element.52.coef, f32[2,4,128]{2,1,0:T(4,128)S(1)} %get-tuple-element.53.gain, ...), custom_call_target="tpu_custom_call" | custom-call | flops 28835840 | bytes 2000000 | tf_op jit(solution)/shard_map/pallas_call | solution.py:40
  85.7 0.1 collective-permute-start.7
  85.9 1.1 collective-permute-done.7.other
  86.9 0.7 shard_map.116
  87.7 5.7 %all-to-all-start.3 = ((f32[32,8,256]{2,1,0:T(8,128)}), f32[32,8,256]{2,1,0:T(8,128)S(1)}, u32[]{:S(2)}, u32[]{:S(2)}) async-start(f32[32,8,256]{2,1,0:T(8,128)} %shard_map.116), calls=%async_computation.3 | async-start | bytes 524288 | tf_op jit(solution)/shard_map/all_to_all | solution.py:731
  93.4 1.8 %shard_map.117.before = f32[256,256]{1,0:T(8,128)S(1)} custom-call(f32[256,256]{1,0:T(8,128)S(1)} %shard_map.114.before), custom_call_target="tpu_custom_call" | custom-call | flops 50331648 | bytes 500000 | tf_op jit(solution)/shard_map/pallas_call | solution.py:40
  95.2 1.7 %shard_map.118.before = f32[256,256]{1,0:T(8,128)S(1)} custom-call(f32[256,256]{1,0:T(8,128)S(1)} %shard_map.117.before), custom_call_target="tpu_custom_call" | custom-call | flops 50331648 | bytes 500000 | tf_op jit(solution)/shard_map/pallas_call | solution.py:40
  96.9 1.8 %shard_map.119.before = f32[256,256]{1,0:T(8,128)S(1)} custom-call(f32[256,256]{1,0:T(8,128)S(1)} %shard_map.118.before), custom_call_target="tpu_custom_call" | custom-call | flops 50331648 | bytes 500000 | tf_op jit(solution)/shard_map/pallas_call | solution.py:40
  98.7 2.4 %shard_map.120 = (bf16[256,256]{1,0:T(8,128)(2,1)S(1)}, bf16[256,256]{1,0:T(8,128)(2,1)S(1)}, bf16[256,256]{1,0:T(8,128)(2,1)S(1)}, bf16[256,512]{1,0:T(8,128)(2,1)S(1)}, bf16[256,512]{1,0:T(8,128)(2,1)S(1)}) custom-call(f32[256,256]{1,0:T(8,128)S(1)} %shard_map.119.before, bf16[256,512]{1,0:T(8,128)(2,1)S(1)} %get-tuple-element.54.panel_high, ...), custom_call_target="tpu_custom_call" | custom-call | flops 251658240 | bytes 1500000 | tf_op jit(solution)/shard_map/pallas_call | solution.py:40
  101.0 5.6 %all-to-all-done.3.parts = f32[32,8,256]{2,1,0:T(8,128)S(1)} async-done(((f32[32,8,256]{2,1,0:T(8,128)}), f32[32,8,256]{2,1,0:T(8,128)S(1)}, u32[]{:S(2)}, u32[]{:S(2)}) %all-to-all-start.3) | async-done | bytes 262176 | tf_op jit(solution)/shard_map/all_to_all | solution.py:731
  106.7 0.9 shard_map.121
  (1 shorter events, 0.0 us)
Async XLA Ops:
  2.2 6.4 %collective-permute-start.4 = (f32[16,128]{1,0:T(8,128)}, f32[16,128]{1,0:T(8,128)S(1)}, u32[]{:S(2)}, u32[]{:S(2)}) collective-permute-start(f32[16,128]{1,0:T(8,128)} %get-tuple-element.39), channel_id=1, source_target_pairs={{0,8},{4,12},{8,0},{12,4},{16,24},{20,28},{24,16},{28,20},{32,40},... | collective-permute-start | bytes 24584 | tf_op jit(solution)/shard_map/ppermute | solution.py:584
  3.8 7.7 %collective-permute-start.2 = (f32[256,128]{1,0:T(8,128)}, f32[256,128]{1,0:T(8,128)S(1)}, u32[]{:S(2)}, u32[]{:S(2)}) collective-permute-start(f32[256,128]{1,0:T(8,128)} %bitcast.11), channel_id=1, source_target_pairs={{0,3},{1,2},{2,1},{3,0},{4,7},{5,6},{6,5},{7,4},{8,11},{9,10},{10,... | collective-permute-start | bytes 393224 | tf_op jit(solution)/shard_map/ppermute | solution.py:584
  5.3 7.8 %collective-permute-start.1 = (f32[256,128]{1,0:T(8,128)}, f32[256,128]{1,0:T(8,128)S(1)}, u32[]{:S(2)}, u32[]{:S(2)}) collective-permute-start(f32[256,128]{1,0:T(8,128)} %bitcast.12), channel_id=1, source_target_pairs={{0,2},{1,3},{2,0},{3,1},{4,6},{5,7},{6,4},{7,5},{8,10},{9,11},{10,... | collective-permute-start | bytes 393224 | tf_op jit(solution)/shard_map/ppermute | solution.py:584
  6.7 6.9 %collective-permute-start = (f32[256,128]{1,0:T(8,128)}, f32[256,128]{1,0:T(8,128)S(1)}, u32[]{:S(2)}, u32[]{:S(2)}) collective-permute-start(f32[256,128]{1,0:T(8,128)} %bitcast.13), channel_id=1, source_target_pairs={{0,1},{1,0},{2,3},{3,2},{4,5},{5,4},{6,7},{7,6},{8,9},{9,8},{10,11... | collective-permute-start | bytes 393224 | tf_op jit(solution)/shard_map/ppermute | solution.py:584
  7.9 3.6 %collective-permute-start.5 = (f32[16,128]{1,0:T(8,128)}, f32[16,128]{1,0:T(8,128)S(1)}, u32[]{:S(2)}, u32[]{:S(2)}) collective-permute-start(f32[16,128]{1,0:T(8,128)} %get-tuple-element.40), channel_id=1, source_target_pairs={{8,16},{12,20},{16,8},{20,12},{24,32},{28,36},{32,24},{36,28},{40,... | collective-permute-start | bytes 24584 | tf_op jit(solution)/shard_map/ppermute | solution.py:584
  8.6 3.0 %collective-permute-start.3 = (f32[128,128]{1,0:T(8,128)}, f32[128,128]{1,0:T(8,128)S(1)}, u32[]{:S(2)}, u32[]{:S(2)}) collective-permute-start(f32[128,128]{1,0:T(8,128)} %get-tuple-element.36.packed.own), channel_id=1, source_target_pairs={{4,8},{8,4},{12,16},{16,12},{20,24},{24,20},{28,32},{32,28},{36,40... | collective-permute-start | bytes 196616 | tf_op jit(solution)/shard_map/ppermute | solution.py:584
  9.3 0.8 copy-start
  10.1 0.9 copy-start.3
  13.7 17.9 %copy-start.1 = (f32[128,128]{1,0:T(8,128)S(1)}, f32[128,128]{1,0:T(8,128)}, u32[]{:S(2)}) copy-start(f32[128,128]{1,0:T(8,128)} %get-tuple-element.36.packed.own) | copy-start | bytes 196612
  13.7 18.0 %copy-start.2 = (f32[512,512]{1,0:T(8,128)S(1)}, f32[512,512]{1,0:T(8,128)}, u32[]{:S(2)}) copy-start(f32[512,512]{1,0:T(8,128)} %precision.1) | copy-start | bytes 3145732
  15.0 29.5 %all-to-all-start = ((f32[64,8,128]{2,1,0:T(8,128)}), f32[64,8,128]{2,1,0:T(8,128)S(1)}, u32[]{:S(2)}, u32[]{:S(2)}) async-start(f32[64,8,128]{2,1,0:T(8,128)} %get-tuple-element.42), calls=%async_computation | async-start | bytes 524288 | tf_op jit(solution)/shard_map/all_to_all | solution.py:643
  31.6 1.3 %collective-permute-start.6 = (f32[128,128]{1,0:T(8,128)S(1)}, f32[128,128]{1,0:T(8,128)S(1)}, u32[]{:S(2)}, u32[]{:S(2)}) collective-permute-start(f32[128,128]{1,0:T(8,128)S(1)} %copy-done.1), channel_id=1, source_target_pairs={{0,4},{4,0},{8,12},{12,8},{16,20},{20,16},{24,28},{28,24},{32,36},... | collective-permute-start | bytes 196616 | tf_op jit(solution)/shard_map/ppermute | solution.py:584
  64.4 16.0 %all-to-all-start.2 = ((f32[64,4,128]{2,1,0:T(4,128)}), f32[64,4,128]{2,1,0:T(4,128)S(1)}, u32[]{:S(2)}, u32[]{:S(2)}) async-start(f32[64,4,128]{2,1,0:T(4,128)} %bitcast.8), calls=%async_computation.2 | async-start | bytes 262144 | tf_op jit(solution)/shard_map/all_to_all | solution.py:643
  85.7 1.2 %collective-permute-start.7 = (f32[8,256]{1,0:T(8,128)S(1)}, f32[8,256]{1,0:T(8,128)S(1)}, u32[]{:S(2)}, u32[]{:S(2)}) collective-permute-start(f32[8,256]{1,0:T(8,128)S(1)} %get-tuple-element.58.own), channel_id=1, source_target_pairs={{0,4},{4,0},{8,12},{12,8},{16,20},{20,16},{24,28},{28,24},{32,36},... | collective-permute-start | bytes 24584 | tf_op jit(solution)/shard_map/ppermute | solution.py:584
  87.7 19.0 %all-to-all-start.3 = ((f32[32,8,256]{2,1,0:T(8,128)}), f32[32,8,256]{2,1,0:T(8,128)S(1)}, u32[]{:S(2)}, u32[]{:S(2)}) async-start(f32[32,8,256]{2,1,0:T(8,128)} %shard_map.116), calls=%async_computation.3 | async-start | bytes 524288 | tf_op jit(solution)/shard_map/all_to_all | solution.py:731

commit v6 on v5

--- a/solution.py
+++ b/solution.py
@@ -627,7 +627,7 @@
     swap_b = swap(packed, "tile", 1, 1)
     far_c = swap(edge_c, "tile", 2)
     far_d = swap(edge_d, "tile", 2, 2)
-    asked, swap_b, far_c, far_d = lax.optimization_barrier((asked, swap_b, far_c, far_d))
+    asked, swap_b, far_d = lax.optimization_barrier((asked, swap_b, far_d))
     n_basis = 4 * basis.shape[0]
     panel_high, panel_low, request = call(
         gram_kernel,

time: 108 us -> 109 us (level)
  waiting for transfers between devices: 19.5 us -> 16.3 us
  starting transfers between devices: 34.7 us -> 37.2 us
  blocking collectives: 17.7 us -> 19.7 us
    all_to_all x2, waiting for transfers between devices: 9.75 us -> 7.24 us  [exchange(): lax.all_to_all(value, 'tile', split_axis=0, concat_axis=0, tiled=True)]
    all_to_all x2, starting transfers between devices: 21.6 us -> 23.8 us  [exchange(): lax.all_to_all(value, 'tile', split_axis=0, concat_axis=0, tiled=True)]
    all_to_all x1, blocking collectives: 17.7 us -> 19.7 us  [exchange(): lax.all_to_all(value, 'tile', split_axis=0, concat_axis=0, tiled=True)]
  transfers between devices with their start and end apart: 11 -> 11, of which waited for: 7 -> 6; matrix products, arithmetic and copies ran while one was open for 0% -> 0% of each run, Pallas kernels for 20% -> 21%
where the time goes in v6:
time: 109 us
  starting transfers between devices  37.2 us (34%)
  Pallas kernels  33.1 us (30%)
  blocking collectives  19.7 us (18%)
  waiting for transfers between devices  16.3 us (15%)
  local copies, waits for them, and re-layouts  1.75 us (2%)
    pallas_call x18, Pallas kernels, call(): pl.pallas_call(kernel, out_shape=shapes, in_specs=places or [SM] * scalar...  33.1 us
    all_to_all x2, starting transfers between devices, exchange(): lax.all_to_all(value, 'tile', split_axis=0, concat_axis=0, tiled=True)  23.8 us
    all_to_all x1, blocking collectives, exchange(): lax.all_to_all(value, 'tile', split_axis=0, concat_axis=0, tiled=True)  19.7 us
    ppermute x8, starting transfers between devices, swap(): lax.ppermute(value, axis, [(i, j) for i, j in enumerate(partner) if 0 <=...  7.72 us
    all_to_all x2, waiting for transfers between devices, exchange(): lax.all_to_all(value, 'tile', split_axis=0, concat_axis=0, tiled=True)  7.24 us
    all_to_all x1, starting transfers between devices, per_device(): lax.all_to_all(copies, 'tile', split_axis=0, concat_axis=0, tiled=True, a...  5.71 us
    all_to_all x1, waiting for transfers between devices, per_device(): lax.all_to_all(copies, 'tile', split_axis=0, concat_axis=0, tiled=True, a...  5.62 us
    ppermute x8, waiting for transfers between devices, swap(): lax.ppermute(value, axis, [(i, j) for i, j in enumerate(partner) if 0 <=...  3.48 us
  transfers between devices with their start and end apart: 11, of which 6 were waited for; matrix products, arithmetic and copies ran while one was open for 0% of the time, Pallas kernels for 21%

profile of v6, /device:TPU:2, one launch (start us, length us, event | category | flops | bytes accessed | tf_op | source)
XLA Modules:
  0.0 108.9 jit_solution(16421595621862162948)
XLA Ops:
  0.6 1.6 %collective-permute-start.2 = (f32[256,128]{1,0:T(8,128)}, f32[256,128]{1,0:T(8,128)S(1)}, u32[]{:S(2)}, u32[]{:S(2)}) collective-permute-start(f32[256,128]{1,0:T(8,128)} %bitcast.11), channel_id=1, source_target_pairs={{0,3},{1,2},{2,1},{3,0},{4,7},{5,6},{6,5},{7,4},{8,11},{9,10},{10,... | collective-permute-start | bytes 393224 | tf_op jit(solution)/shard_map/ppermute | solution.py:584
  2.2 2.8 %collective-permute-start.1 = (f32[256,128]{1,0:T(8,128)}, f32[256,128]{1,0:T(8,128)S(1)}, u32[]{:S(2)}, u32[]{:S(2)}) collective-permute-start(f32[256,128]{1,0:T(8,128)} %bitcast.12), channel_id=1, source_target_pairs={{0,2},{1,3},{2,0},{3,1},{4,6},{5,7},{6,4},{7,5},{8,10},{9,11},{10,... | collective-permute-start | bytes 393224 | tf_op jit(solution)/shard_map/ppermute | solution.py:584
  5.1 0.0 collective-permute-start
  5.1 1.5 %shard_map.105 = (f32[128,128]{1,0:T(8,128)}, f32[16,128]{1,0:T(8,128)}, f32[16,128]{1,0:T(8,128)}) custom-call(s32[1]{0:T(128)} %bitcast.1.at_ref, f32[64,128]{1,0:T(8,128)} %bitcast.15, f32[32,128]{1,0:T(8,128)} %bitcast.16, f32[8,128]{1,0:T(8,128)} %bitcast.17, f32[4,128]{1,0:T(4,128)} %fric.1, s32[1,512]{1,0:T(1,128)} %bitcast.18, s32[1,512]{1,0:T(1,128)} %bitcast.19, ...), custom_call_target="tpu_custom_call" | custom-call | bytes 400000 | tf_op jit(solution)/shard_map/pallas_call | solution.py:40
  6.6 0.7 collective-permute-start.4
  7.3 0.7 collective-permute-start.3
  8.0 0.0 copy-start
  8.0 0.8 copy-done
  8.8 0.0 copy-start.3
  8.8 0.9 copy-done.3
  9.7 0.5 shard_map.106
  10.2 0.0 collective-permute-done.4.edge_d
  10.3 0.0 collective-permute-done.3.swap_b
  10.3 0.0 collective-permute-done.2.back
  10.3 0.0 collective-permute-done.1.across
  10.3 0.5 collective-permute-done.near
  10.8 1.3 %shard_map.107 = (bf16[256,512]{1,0:T(8,128)(2,1)S(1)}, bf16[256,512]{1,0:T(8,128)(2,1)S(1)}, f32[64,8,128]{2,1,0:T(8,128)}) custom-call(s32[1]{0:T(128)} %bitcast.me_ref, f32[256,128]{1,0:T(8,128)S(1)} %get-tuple-element.36.own, f32[256,128]{1,0:T(8,128)S(1)} %collective-permute-done.near, f32[256,128]{1,0:T(8,128)S(1)} %collective-permute-done.1.across, ...), custom_call_target="tpu_custom_call" | custom-call | flops 20000000000 | bytes 1500000 | tf_op jit(solution)/shard_map/pallas_call | solution.py:40
  12.1 18.7 %all-to-all-start = ((f32[64,8,128]{2,1,0:T(8,128)}), f32[64,8,128]{2,1,0:T(8,128)S(1)}, u32[]{:S(2)}, u32[]{:S(2)}) async-start(f32[64,8,128]{2,1,0:T(8,128)} %get-tuple-element.40), calls=%async_computation | async-start | bytes 524288 | tf_op jit(solution)/shard_map/all_to_all | solution.py:643
  30.8 0.0 copy-done.1
  30.8 0.1 collective-permute-start.5
  31.0 0.0 copy-done.4
  31.0 1.7 %collective-permute-start.6 = (f32[16,128]{1,0:T(8,128)S(1)}, f32[16,128]{1,0:T(8,128)S(1)}, u32[]{:S(2)}, u32[]{:S(2)}) collective-permute-start(f32[16,128]{1,0:T(8,128)S(1)} %copy-done.4), channel_id=1, source_target_pairs={{0,8},{4,12},{8,0},{12,4},{16,24},{20,28},{24,16},{28,20},{32,40},... | collective-permute-start | bytes 24584 | tf_op jit(solution)/shard_map/ppermute | solution.py:584
  32.6 0.0 copy-done.2
  32.6 0.1 shard_map.104
  32.8 1.9 %collective-permute-done.6.edge_c = f32[16,128]{1,0:T(8,128)S(1)} collective-permute-done((f32[16,128]{1,0:T(8,128)S(1)}, f32[16,128]{1,0:T(8,128)S(1)}, u32[]{:S(2)}, u32[]{:S(2)}) %collective-permute-start.6) | collective-permute-done | bytes 8224 | tf_op jit(solution)/shard_map/ppermute | solution.py:584
  34.7 0.0 collective-permute-done.5.swap_a
  34.7 5.7 %shard_map.108 = (f32[2,4,8,128]{3,2,1,0:T(8,128)S(1)}, f32[13,12,16,128]{3,2,1,0:T(8,128)S(1)}, f32[2,4,128]{2,1,0:T(4,128)S(1)}) custom-call(s32[1]{0:T(128)} %bitcast.1.at_ref, f32[128,128]{1,0:T(8,128)S(1)} %copy-done.1, f32[128,128]{1,0:T(8,128)S(1)} %collective-permute-done.5.swap_a, f32[128,128]{1,0:T(8,128)S(1)} %collective-permute-done.3.swap_b, ...), custom_call_target="tpu_custom_call" | custom-call | flops 28835840 | bytes 2000000 | tf_op jit(solution)/shard_map/pallas_call | solution.py:40
  40.3 3.4 %all-to-all-done.meta = f32[64,8,128]{2,1,0:T(8,128)S(1)} async-done(((f32[64,8,128]{2,1,0:T(8,128)}), f32[64,8,128]{2,1,0:T(8,128)S(1)}, u32[]{:S(2)}, u32[]{:S(2)}) %all-to-all-start) | async-done | bytes 262176 | tf_op jit(solution)/shard_map/all_to_all | solution.py:643
  43.8 0.6 shard_map.109
  44.4 19.7 %all_to_all.20.arrived = f32[64,8,128]{2,1,0:T(8,128)S(1)} all-to-all(f32[64,8,128]{2,1,0:T(8,128)S(1)} %shard_map.109), channel_id=1, replica_groups=mesh['tile'=64,'probe'=4] {'tile'}, dimensions={0} | all-to-all | bytes 524288 | tf_op jit(solution)/shard_map/all_to_all | solution.py:643
  64.1 1.6 %shard_map.110 = f32[256,128]{1,0:T(8,128)} custom-call(f32[64,8,128]{2,1,0:T(8,128)S(1)} %all_to_all.20.arrived, s32[2,512]{1,0:T(2,128)S(1)} %get-tuple-element.46.slots, bf16[512,512]{1,0:T(8,128)(2,1)S(1)} %get-tuple-element.47.precision_high, bf16[512,512]{1,0:T(8,128)(2,1)S(1)} %get-tuple-element.48.precision_low), custom_call_target="tpu_custom_call" | custom-call | flops 20000000000 | bytes 1500000 | tf_op jit(solution)/shard_map/pallas_call | solution.py:40
  65.7 5.1 %all-to-all-start.2 = ((f32[64,4,128]{2,1,0:T(4,128)}), f32[64,4,128]{2,1,0:T(4,128)S(1)}, u32[]{:S(2)}, u32[]{:S(2)}) async-start(f32[64,4,128]{2,1,0:T(4,128)} %bitcast.8), calls=%async_computation.2 | async-start | bytes 262144 | tf_op jit(solution)/shard_map/all_to_all | solution.py:643
  70.8 1.8 %shard_map.111.before = f32[256,256]{1,0:T(8,128)S(1)} custom-call(f32[64,8,128]{2,1,0:T(8,128)S(1)} %all_to_all.20.arrived), custom_call_target="tpu_custom_call" | custom-call | flops 50331648 | bytes 500000 | tf_op jit(solution)/shard_map/pallas_call | solution.py:40
  72.6 1.8 %shard_map.112.before = f32[256,256]{1,0:T(8,128)S(1)} custom-call(f32[256,256]{1,0:T(8,128)S(1)} %shard_map.111.before), custom_call_target="tpu_custom_call" | custom-call | flops 50331648 | bytes 500000 | tf_op jit(solution)/shard_map/pallas_call | solution.py:40
  74.4 1.8 %shard_map.113.before = f32[256,256]{1,0:T(8,128)S(1)} custom-call(f32[256,256]{1,0:T(8,128)S(1)} %shard_map.112.before), custom_call_target="tpu_custom_call" | custom-call | flops 50331648 | bytes 500000 | tf_op jit(solution)/shard_map/pallas_call | solution.py:40
  76.2 1.8 %shard_map.114.before = f32[256,256]{1,0:T(8,128)S(1)} custom-call(f32[256,256]{1,0:T(8,128)S(1)} %shard_map.113.before), custom_call_target="tpu_custom_call" | custom-call | flops 50331648 | bytes 500000 | tf_op jit(solution)/shard_map/pallas_call | solution.py:40
  77.9 3.8 %all-to-all-done.2 = f32[64,4,128]{2,1,0:T(4,128)S(1)} async-done(((f32[64,4,128]{2,1,0:T(4,128)}), f32[64,4,128]{2,1,0:T(4,128)S(1)}, u32[]{:S(2)}, u32[]{:S(2)}) %all-to-all-start.2) | async-done | bytes 131104 | tf_op jit(solution)/shard_map/all_to_all | solution.py:643
  81.7 5.3 %shard_map.115 = (f32[4,8,128]{2,1,0:T(8,128)S(1)}, f32[8,256]{1,0:T(8,128)S(1)}) custom-call(f32[256,128]{1,0:T(8,128)S(1)} %bitcast.10, f32[64,8,128]{2,1,0:T(8,128)S(1)} %all-to-all-done.meta, f32[13,12,16,128]{3,2,1,0:T(8,128)S(1)} %get-tuple-element.50.coef, f32[2,4,128]{2,1,0:T(4,128)S(1)} %get-tuple-element.51.gain, ...), custom_call_target="tpu_custom_call" | custom-call | flops 28835840 | bytes 2000000 | tf_op jit(solution)/shard_map/pallas_call | solution.py:40
  87.1 0.1 collective-permute-start.7
  87.2 1.1 collective-permute-done.7.other
  88.3 0.7 shard_map.116
  89.0 5.7 %all-to-all-start.3 = ((f32[32,8,256]{2,1,0:T(8,128)}), f32[32,8,256]{2,1,0:T(8,128)S(1)}, u32[]{:S(2)}, u32[]{:S(2)}) async-start(f32[32,8,256]{2,1,0:T(8,128)} %shard_map.116), calls=%async_computation.3 | async-start | bytes 524288 | tf_op jit(solution)/shard_map/all_to_all | solution.py:731
  94.7 1.8 %shard_map.117.before = f32[256,256]{1,0:T(8,128)S(1)} custom-call(f32[256,256]{1,0:T(8,128)S(1)} %shard_map.114.before), custom_call_target="tpu_custom_call" | custom-call | flops 50331648 | bytes 500000 | tf_op jit(solution)/shard_map/pallas_call | solution.py:40
  96.5 1.8 %shard_map.118.before = f32[256,256]{1,0:T(8,128)S(1)} custom-call(f32[256,256]{1,0:T(8,128)S(1)} %shard_map.117.before), custom_call_target="tpu_custom_call" | custom-call | flops 50331648 | bytes 500000 | tf_op jit(solution)/shard_map/pallas_call | solution.py:40
  98.2 1.7 %shard_map.119.before = f32[256,256]{1,0:T(8,128)S(1)} custom-call(f32[256,256]{1,0:T(8,128)S(1)} %shard_map.118.before), custom_call_target="tpu_custom_call" | custom-call | flops 50331648 | bytes 500000 | tf_op jit(solution)/shard_map/pallas_call | solution.py:40
  100.0 2.4 %shard_map.120 = (bf16[256,256]{1,0:T(8,128)(2,1)S(1)}, bf16[256,256]{1,0:T(8,128)(2,1)S(1)}, bf16[256,256]{1,0:T(8,128)(2,1)S(1)}, bf16[256,512]{1,0:T(8,128)(2,1)S(1)}, bf16[256,512]{1,0:T(8,128)(2,1)S(1)}) custom-call(f32[256,256]{1,0:T(8,128)S(1)} %shard_map.119.before, bf16[256,512]{1,0:T(8,128)(2,1)S(1)} %get-tuple-element.52.panel_high, ...), custom_call_target="tpu_custom_call" | custom-call | flops 251658240 | bytes 1500000 | tf_op jit(solution)/shard_map/pallas_call | solution.py:40
  102.3 5.6 %all-to-all-done.3.parts = f32[32,8,256]{2,1,0:T(8,128)S(1)} async-done(((f32[32,8,256]{2,1,0:T(8,128)}), f32[32,8,256]{2,1,0:T(8,128)S(1)}, u32[]{:S(2)}, u32[]{:S(2)}) %all-to-all-start.3) | async-done | bytes 262176 | tf_op jit(solution)/shard_map/all_to_all | solution.py:731
  108.0 0.9 shard_map.121
  (3 shorter events, 0.0 us)
Async XLA Ops:
  0.6 9.6 %collective-permute-start.2 = (f32[256,128]{1,0:T(8,128)}, f32[256,128]{1,0:T(8,128)S(1)}, u32[]{:S(2)}, u32[]{:S(2)}) collective-permute-start(f32[256,128]{1,0:T(8,128)} %bitcast.11), channel_id=1, source_target_pairs={{0,3},{1,2},{2,1},{3,0},{4,7},{5,6},{6,5},{7,4},{8,11},{9,10},{10,... | collective-permute-start | bytes 393224 | tf_op jit(solution)/shard_map/ppermute | solution.py:584
  2.2 8.1 %collective-permute-start.1 = (f32[256,128]{1,0:T(8,128)}, f32[256,128]{1,0:T(8,128)S(1)}, u32[]{:S(2)}, u32[]{:S(2)}) collective-permute-start(f32[256,128]{1,0:T(8,128)} %bitcast.12), channel_id=1, source_target_pairs={{0,2},{1,3},{2,0},{3,1},{4,6},{5,7},{6,4},{7,5},{8,10},{9,11},{10,... | collective-permute-start | bytes 393224 | tf_op jit(solution)/shard_map/ppermute | solution.py:584
  5.1 5.7 %collective-permute-start = (f32[256,128]{1,0:T(8,128)}, f32[256,128]{1,0:T(8,128)S(1)}, u32[]{:S(2)}, u32[]{:S(2)}) collective-permute-start(f32[256,128]{1,0:T(8,128)} %bitcast.13), channel_id=1, source_target_pairs={{0,1},{1,0},{2,3},{3,2},{4,5},{5,4},{6,7},{7,6},{8,9},{9,8},{10,11... | collective-permute-start | bytes 393224 | tf_op jit(solution)/shard_map/ppermute | solution.py:584
  6.6 3.6 %collective-permute-start.4 = (f32[16,128]{1,0:T(8,128)}, f32[16,128]{1,0:T(8,128)S(1)}, u32[]{:S(2)}, u32[]{:S(2)}) collective-permute-start(f32[16,128]{1,0:T(8,128)} %get-tuple-element.38), channel_id=1, source_target_pairs={{8,16},{12,20},{16,8},{20,12},{24,32},{28,36},{32,24},{36,28},{40,... | collective-permute-start | bytes 24584 | tf_op jit(solution)/shard_map/ppermute | solution.py:584
  7.3 3.0 %collective-permute-start.3 = (f32[128,128]{1,0:T(8,128)}, f32[128,128]{1,0:T(8,128)S(1)}, u32[]{:S(2)}, u32[]{:S(2)}) collective-permute-start(f32[128,128]{1,0:T(8,128)} %get-tuple-element.35.packed.own), channel_id=1, source_target_pairs={{4,8},{8,4},{12,16},{16,12},{20,24},{24,20},{28,32},{32,28},{36,40... | collective-permute-start | bytes 196616 | tf_op jit(solution)/shard_map/ppermute | solution.py:584
  8.0 0.8 copy-start
  8.8 0.9 copy-start.3
  10.8 20.0 %copy-start.1 = (f32[128,128]{1,0:T(8,128)S(1)}, f32[128,128]{1,0:T(8,128)}, u32[]{:S(2)}) copy-start(f32[128,128]{1,0:T(8,128)} %get-tuple-element.35.packed.own) | copy-start | bytes 196612
  10.8 20.2 %copy-start.4 = (f32[16,128]{1,0:T(8,128)S(1)}, f32[16,128]{1,0:T(8,128)}, u32[]{:S(2)}) copy-start(f32[16,128]{1,0:T(8,128)} %get-tuple-element.43) | copy-start | bytes 24580
  10.8 21.8 %copy-start.2 = (f32[512,512]{1,0:T(8,128)S(1)}, f32[512,512]{1,0:T(8,128)}, u32[]{:S(2)}) copy-start(f32[512,512]{1,0:T(8,128)} %precision.1) | copy-start | bytes 3145732
  12.1 31.6 %all-to-all-start = ((f32[64,8,128]{2,1,0:T(8,128)}), f32[64,8,128]{2,1,0:T(8,128)S(1)}, u32[]{:S(2)}, u32[]{:S(2)}) async-start(f32[64,8,128]{2,1,0:T(8,128)} %get-tuple-element.40), calls=%async_computation | async-start | bytes 524288 | tf_op jit(solution)/shard_map/all_to_all | solution.py:643
  30.8 3.9 %collective-permute-start.5 = (f32[128,128]{1,0:T(8,128)S(1)}, f32[128,128]{1,0:T(8,128)S(1)}, u32[]{:S(2)}, u32[]{:S(2)}) collective-permute-start(f32[128,128]{1,0:T(8,128)S(1)} %copy-done.1), channel_id=1, source_target_pairs={{0,4},{4,0},{8,12},{12,8},{16,20},{20,16},{24,28},{28,24},{32,36},... | collective-permute-start | bytes 196616 | tf_op jit(solution)/shard_map/ppermute | solution.py:584
  31.0 3.7 %collective-permute-start.6 = (f32[16,128]{1,0:T(8,128)S(1)}, f32[16,128]{1,0:T(8,128)S(1)}, u32[]{:S(2)}, u32[]{:S(2)}) collective-permute-start(f32[16,128]{1,0:T(8,128)S(1)} %copy-done.4), channel_id=1, source_target_pairs={{0,8},{4,12},{8,0},{12,4},{16,24},{20,28},{24,16},{28,20},{32,40},... | collective-permute-start | bytes 24584 | tf_op jit(solution)/shard_map/ppermute | solution.py:584
  65.7 16.0 %all-to-all-start.2 = ((f32[64,4,128]{2,1,0:T(4,128)}), f32[64,4,128]{2,1,0:T(4,128)S(1)}, u32[]{:S(2)}, u32[]{:S(2)}) async-start(f32[64,4,128]{2,1,0:T(4,128)} %bitcast.8), calls=%async_computation.2 | async-start | bytes 262144 | tf_op jit(solution)/shard_map/all_to_all | solution.py:643
  87.1 1.2 %collective-permute-start.7 = (f32[8,256]{1,0:T(8,128)S(1)}, f32[8,256]{1,0:T(8,128)S(1)}, u32[]{:S(2)}, u32[]{:S(2)}) collective-permute-start(f32[8,256]{1,0:T(8,128)S(1)} %get-tuple-element.56.own), channel_id=1, source_target_pairs={{0,4},{4,0},{8,12},{12,8},{16,20},{20,16},{24,28},{28,24},{32,36},... | collective-permute-start | bytes 24584 | tf_op jit(solution)/shard_map/ppermute | solution.py:584
  89.0 19.0 %all-to-all-start.3 = ((f32[32,8,256]{2,1,0:T(8,128)}), f32[32,8,256]{2,1,0:T(8,128)S(1)}, u32[]{:S(2)}, u32[]{:S(2)}) async-start(f32[32,8,256]{2,1,0:T(8,128)} %shard_map.116), calls=%async_computation.3 | async-start | bytes 524288 | tf_op jit(solution)/shard_map/all_to_all | solution.py:731
